TPU v7x, 256 devices: a whole 4x4x8 slice. The times are simulated.
256 devices in a mesh: band: 16 (over y_hi, z), space: 16 (over y_lo, x, core).
Axes of the slice: x: 4, y: 4 (y_hi: 2, y_lo: 2; y = y_hi * 2 + y_lo), z: 8, core: 2. Of those that a mesh axis runs over, the one named last changes fastest.
Arguments:
- psi_start: float32 [2, 32, 16, 9216], P(None, 'band', 'space'), may hold values from -6 to 6
- adjoint_end: float32 [2, 32, 16, 9216], P(None, 'band', 'space'), may hold values from -6 to 6
- potential_now: float32 [16, 9216], P('space'), may hold values from -12 to 12
- potential_next: float32 [16, 9216], P('space'), may hold values from -12 to 12
- projector_tiles: float32 [16, 16, 9216], P('band', 'space'), may hold values from -0.015625 to 0.015625
- tile_map: int32 [4, 16, 72], P(None, 'space'), may hold values 0 or 1
- strengths: float32 [16], replicated, may hold values from 30 to 90
- positions: int32 [3, 4], replicated, may hold values from 0 to 95, as said below
Outputs:
- psi_end: float32 [2, 32, 16, 9216], P(None, 'band', 'space')
- adjoint_start: float32 [2, 32, 16, 9216], P(None, 'band', 'space')
- adjoint_density: float32 [16, 9216], P('space', 'band')
- forces: float32 [3, 4], replicated
Inputs may be any that keep to these rules, and one draw needn't show every extreme that they name: positions[0], positions[1], positions[2] hold an atom's plane, row and column, within 0 to 15, 95 and 95.
All inputs are finite; a program needn't handle non-finite values. No bound on the sum of `tile_map` on one device may be relied on, other than what follows from the above.
Results may differ from a plain program's by a relative error of at most 0.00016.
Values sent between devices are 32-bit elements; how exact they have to be, the bound alone decides.
No kernel may reach another device: no remote copies, remote signals or barrier semaphores. Data moves between devices by JAX's collectives and lax.ppermute only.
A program may use at most 128 MiB of HBM per device.

v0:
```python
import math

import jax
import jax.numpy as jnp
from jax import lax
from jax.sharding import PartitionSpec as P

NB = 32
NY = 96
NZ = 96


half_step = 0.025
kinetic_scale = 3.125
highest = lax.Precision.HIGHEST


def padded_2(array, sides, width):
    for axis, dim in sides:
        size, length = (lax.axis_size(axis), array.shape[dim])
        up = [(i, (i + 1) % size) for i in range(size)]
        down = [(j, i) for i, j in up]
        last = lax.slice_in_dim(array, length - width, length, axis=dim)
        first = lax.slice_in_dim(array, 0, width, axis=dim)
        before = lax.ppermute(last, axis, up)
        after = lax.ppermute(first, axis, down)
        array = jnp.concatenate([before, array, after], axis=dim)
    return array


def neighbours(fields, points):
    padded = padded_2(fields, (("space", 3),), 1)
    column = lax.broadcasted_iota(jnp.int32, (points,), 0) % NZ
    along_x = padded[:, :, :, 2:, :] + padded[:, :, :, :-2, :]
    rows_up = jnp.roll(fields, -NZ, axis=4)
    rows_down = jnp.roll(fields, NZ, axis=4)
    cols_up = jnp.where(
        column == NZ - 1, jnp.roll(fields, NZ - 1, axis=4), jnp.roll(fields, -1, axis=4)
    )
    cols_down = jnp.where(
        column == 0, jnp.roll(fields, 1 - NZ, axis=4), jnp.roll(fields, 1, axis=4)
    )
    return along_x + rows_up + rows_down + cols_up + cols_down


def hamiltonian(fields, potentials, basis_rows, strengths):
    members, components, orbitals, planes, points = fields.shape
    beside_all = neighbours(fields, points)
    flat_rows = fields.reshape(members * components * orbitals, planes * points)
    partial_value = jnp.dot(
        flat_rows, basis_rows.T, precision=highest, preferred_element_type=jnp.float32
    )
    summed = lax.psum(partial_value, "space")
    projected = jnp.dot(
        summed * strengths, basis_rows, precision=highest, preferred_element_type=jnp.float32
    ).reshape(fields.shape)
    applied = (
        kinetic_scale * (6.0 * fields - beside_all) + potentials[:, None, None] * fields + projected
    )
    return (applied, summed)


def taylor(fields, potentials, sign_set, basis_rows, leading_rows, strengths):
    accumulated = fields
    current = fields
    leading = None
    for degree in range(1, 5):
        applied, summed = hamiltonian(
            current, potentials, leading_rows if degree == 1 else basis_rows, strengths
        )
        if degree == 1:
            leading = summed
        factor = sign_set * (half_step / degree)
        current = jnp.stack([-(factor * applied[:, 1]), factor * applied[:, 0]], axis=1)
        accumulated = accumulated + current
    return (accumulated, leading)


def body(
    psi_start,
    adjoint_end,
    potential_now,
    potential_next,
    projector_tiles,
    tile_map,
    strengths,
    positions,
):
    components, orbitals, planes, points = psi_start.shape
    proj_count = strengths.shape[0]
    atom_count = positions.shape[1]
    gathered = lax.all_gather(projector_tiles, "band", axis=0, tiled=True)
    masked = gathered.reshape(atom_count, proj_count // atom_count, planes, points // 128, 128)
    masked = masked * tile_map.astype(jnp.float32).reshape(atom_count, 1, planes, points // 128, 1)
    shaped = masked.reshape(atom_count, proj_count // atom_count, planes, points)
    total_planes = planes * lax.axis_size("space")
    plane_index = lax.axis_index("space") * planes + lax.broadcasted_iota(jnp.int32, (planes,), 0)
    flat_index = lax.broadcasted_iota(jnp.int32, (points,), 0)
    wave_x = jnp.sin(
        2.0
        * math.pi
        / total_planes
        * (plane_index[None, :] - positions[0][:, None]).astype(jnp.float32)
    )
    wave_y = jnp.sin(
        2.0 * math.pi / NY * (flat_index[None, :] // NZ - positions[1][:, None]).astype(jnp.float32)
    )
    wave_z = jnp.sin(
        2.0 * math.pi / NZ * (flat_index[None, :] % NZ - positions[2][:, None]).astype(jnp.float32)
    )
    slab_points = planes * points
    basis_rows = shaped.reshape(proj_count, slab_points)
    extended = jnp.concatenate(
        [
            basis_rows,
            (shaped * wave_x[:, None, :, None]).reshape(proj_count, slab_points),
            (shaped * wave_y[:, None, None, :]).reshape(proj_count, slab_points),
            (shaped * wave_z[:, None, None, :]).reshape(proj_count, slab_points),
        ],
        0,
    )
    forward = jnp.asarray([-1.0], jnp.float32).reshape(1, 1, 1, 1)
    backward = jnp.asarray([1.0], jnp.float32).reshape(1, 1, 1, 1)
    psi_mid, _ = taylor(
        psi_start[None], potential_now[None], forward, basis_rows, basis_rows, strengths
    )
    adjoint_mid, _ = taylor(
        adjoint_end[None], potential_next[None], backward, basis_rows, basis_rows, strengths
    )
    psi_final, coeffs_psi = taylor(
        psi_mid, potential_next[None], forward, basis_rows, basis_rows, strengths
    )
    adjoint_final, coeffs_adjoint = taylor(
        adjoint_mid, potential_now[None], backward, basis_rows, basis_rows, strengths
    )
    psi_half = psi_mid[0]
    adjoint_half = adjoint_mid[0]
    psi_end = psi_final[0]
    adjoint_start = adjoint_final[0]
    mid_coeffs = jnp.concatenate([coeffs_psi, coeffs_adjoint], 0)
    stacked_rows = jnp.stack([psi_half, adjoint_half]).reshape(
        2 * components * orbitals, slab_points
    )
    mid_coeffs = lax.psum(
        jnp.dot(stacked_rows, extended.T, precision=highest, preferred_element_type=jnp.float32),
        "space",
    )
    coeffs = mid_coeffs.reshape(2, components, orbitals, 4, proj_count)
    orbital_part = coeffs[0]
    adjoint_part = coeffs[1]
    products = (
        orbital_part[:, :, :1] * adjoint_part[:, :, 1:]
        + adjoint_part[:, :, :1] * orbital_part[:, :, 1:]
    )
    weighted = jnp.sum(products, axis=(0, 1)) * strengths
    local_force = jnp.sum(weighted.reshape(3, atom_count, proj_count // atom_count), axis=2)
    local_density = (
        2.0
        * half_step
        * jnp.sum(psi_half[0] * adjoint_half[1] - psi_half[1] * adjoint_half[0], axis=0)
    )
    density = lax.psum_scatter(local_density, "band", scatter_dimension=1, tiled=True)
    forces = lax.psum(local_force, "band") / NB
    return (psi_end, adjoint_start, density, forces)


def solution(mesh):
    return jax.shard_map(
        body,
        mesh=mesh,
        in_specs=(
            P(None, "band", "space", None),
            P(None, "band", "space", None),
            P("space", None),
            P("space", None),
            P("band", "space", None),
            P(None, "space", None),
            P(),
            P(),
        ),
        out_specs=(
            P(None, "band", "space", None),
            P(None, "band", "space", None),
            P("space", "band"),
            P(),
        ),
        check_vma=False,
    )
```

profile of v0, /device:TPU:1, one launch (start us, length us, event | category | flops | bytes accessed | tf_op | source)
XLA Modules:
  0.0 697.6 jit_solution(5259860496915839688)
XLA Ops:
  8.2 3.3 collective-permute-start.16
  12.5 1.6 collective-permute-start
  15.7 1.3 reduce.2
  26.2 39.8 %all_gather.3 = f32[16,1,9216]{2,1,0:T(1,128)S(1)} all-gather(f32[1,1,9216]{2,1,0:T(1,128)S(1)} %copy-done.48), channel_id=1, replica_groups=mesh['band'=16,'space'=16] {'band'}, dimensions={0}, use_global_device_ids=true | all-gather | bytes 626688 | tf_op jit(solution)/shard_map/all_gather | solution.py:92
  67.1 1.4 convolution_bitcast_fusion.16
  68.5 1.4 convolution_bitcast_fusion.17
  69.9 2.1 multiply_sine_fusion
  76.3 37.7 %all-reduce.7 = (f32[4,16]{1,0:T(4,128)S(1)}, f32[4,16]{1,0:T(4,128)S(1)}) all-reduce(f32[4,16]{1,0:T(4,128)} %convolution_bitcast_fusion.17, f32[4,16]{1,0:T(4,128)} %convolution_bitcast_fusion.16), channel_id=1, replica_groups=mesh['band'=16,'space'=16] {'space'}, use_global_device_ids=true, to_apply=%region_0.1 | all-reduce | flops 128 | bytes 1024 | tf_op jit(solution)/shard_map/psum | solution.py:53
  114.7 2.9 broadcast_multiply_fusion
  118.4 2.1 fusion.8
  124.8 2.3 fusion
  131.3 1.7 collective-permute-start.3
  136.6 27.6 %all-reduce.6 = (f32[4,16]{1,0:T(4,128)S(1)}, f32[4,16]{1,0:T(4,128)S(1)}) all-reduce(f32[4,16]{1,0:T(4,128)S(1)} %fusion.66, f32[4,16]{1,0:T(4,128)S(1)} %fusion.56), channel_id=1, replica_groups=mesh['band'=16,'space'=16] {'space'}, use_global_device_ids=true, to_apply=%region_1.2 | all-reduce | flops 128 | bytes 1024 | tf_op jit(solution)/shard_map/psum | solution.py:53
  165.0 2.1 fusion.9
  169.4 4.5 collective-permute-start.20
  174.8 2.4 fusion.1
  184.1 1.4 fusion.40
  186.2 28.9 %all-reduce.5 = (f32[4,16]{1,0:T(4,128)S(1)}, f32[4,16]{1,0:T(4,128)S(1)}) all-reduce(f32[4,16]{1,0:T(4,128)S(1)} %fusion.62, f32[4,16]{1,0:T(4,128)} %fusion.40), channel_id=1, replica_groups=mesh['band'=16,'space'=16] {'space'}, use_global_device_ids=true, to_apply=%region_2.3 | all-reduce | flops 128 | bytes 1024 | tf_op jit(solution)/shard_map/psum | solution.py:53
  216.4 2.1 fusion.10
  222.9 4.6 collective-permute-start.22
  228.2 2.1 fusion.2
  234.5 1.4 collective-permute-start.7
  236.0 1.4 fusion.48
  238.1 28.9 %all-reduce.4 = (f32[4,16]{1,0:T(4,128)S(1)}, f32[4,16]{1,0:T(4,128)S(1)}) all-reduce(f32[4,16]{1,0:T(4,128)S(1)} %fusion.58, f32[4,16]{1,0:T(4,128)} %fusion.48), channel_id=1, replica_groups=mesh['band'=16,'space'=16] {'space'}, use_global_device_ids=true, to_apply=%region_3.4 | all-reduce | flops 128 | bytes 1024 | tf_op jit(solution)/shard_map/psum | solution.py:53
  267.1 2.4 fusion.11
  273.5 4.5 collective-permute-start.24
  280.1 2.1 fusion.3
  292.1 2.9 copy.268
  295.0 29.3 %all-reduce.3 = (f32[4,16]{1,0:T(4,128)S(1)}, f32[4,16]{1,0:T(4,128)S(1)}) all-reduce(f32[4,16]{1,0:T(4,128)S(1)} %fusion.54, f32[4,16]{1,0:T(4,128)S(1)} %fusion.64), channel_id=1, replica_groups=mesh['band'=16,'space'=16] {'space'}, use_global_device_ids=true, to_apply=%region_4.5 | all-reduce | flops 128 | bytes 1024 | tf_op jit(solution)/shard_map/psum | solution.py:53
  324.9 3.7 fusion.16
  328.6 172.6 %reduce-scatter.4.cloned.1.call-done = f32[576,1]{1,0:T(8,128)} async-done(((f32[9216,1]{1,0:T(8,128)}), f32[576,1]{1,0:T(8,128)}) %reduce-scatter.4.cloned.1.call-update) | async-done | bytes 2320
  501.2 1.7 copy.269
  502.9 2.4 fusion.12
  507.7 5.1 collective-permute-start.26
  515.9 2.1 fusion.4
  520.3 1.7 collective-permute-start.11
  523.8 27.7 %all-reduce.2 = (f32[4,16]{1,0:T(4,128)S(1)}, f32[4,16]{1,0:T(4,128)S(1)}) all-reduce(f32[4,16]{1,0:T(4,128)S(1)} %fusion.50, f32[4,16]{1,0:T(4,128)S(1)} %fusion.44), channel_id=1, replica_groups=mesh['band'=16,'space'=16] {'space'}, use_global_device_ids=true, to_apply=%region_5.6 | all-reduce | flops 128 | bytes 1024 | tf_op jit(solution)/shard_map/psum | solution.py:53
  551.6 2.3 fusion.13
  556.9 4.5 collective-permute-start.28
  563.4 2.1 fusion.5
  571.3 28.6 %all-reduce.1 = (f32[4,16]{1,0:T(4,128)S(1)}, f32[4,16]{1,0:T(4,128)S(1)}) all-reduce(f32[4,16]{1,0:T(4,128)S(1)} %fusion.46, f32[4,16]{1,0:T(4,128)S(1)} %fusion.52), channel_id=1, replica_groups=mesh['band'=16,'space'=16] {'space'}, use_global_device_ids=true, to_apply=%region_6.7 | all-reduce | flops 128 | bytes 1024 | tf_op jit(solution)/shard_map/psum | solution.py:53
  600.0 2.4 fusion.14
  605.4 4.5 collective-permute-start.30
  612.1 2.1 fusion.6
  618.7 30.3 %all-reduce = (f32[4,16]{1,0:T(4,128)S(1)}, f32[4,16]{1,0:T(4,128)S(1)}, f32[8,64]{1,0:T(8,128)S(1)}) all-reduce(f32[4,16]{1,0:T(4,128)S(1)} %fusion.42, f32[4,16]{1,0:T(4,128)S(1)} %fusion.60, f32[8,64]{1,0:T(8,128)} %fusion.16), channel_id=1, replica_groups=mesh['band'=16,'space'=16] {'space'}, use_global_device_ids=true, to_apply=%region_7.8 | all-reduce | flops 640 | bytes 5120 | tf_op jit(solution)/shard_map/psum | solution.py:53
  650.1 31.9 %psum.143 = f32[3,4]{1,0:T(4,128)S(1)} all-reduce(f32[3,4]{1,0:T(4,128)S(1)} %multiply_reduce_fusion), channel_id=1, replica_groups=mesh['band'=16,'space'=16] {'band'}, use_global_device_ids=true, to_apply=%region_21.22 | all-reduce | flops 12 | bytes 96 | tf_op jit(solution)/shard_map/psum | solution.py:163
  682.8 2.6 fusion.15
  686.9 2.2 fusion.7
  (447 shorter events, 104.6 us)
Async XLA Ops:
  7.2 19.0 %copy-start.73 = (s32[4,1,72]{2,1,0:T(1,128)S(1)}, s32[4,1,72]{2,1,0:T(1,128)}, u32[]{:S(2)}) copy-start(s32[4,1,72]{2,1,0:T(1,128)} %param.15) | copy-start | bytes 3460
  7.2 19.0 %copy-start.48 = (f32[1,1,9216]{2,1,0:T(1,128)S(1)}, f32[1,1,9216]{2,1,0:T(1,128)}, u32[]{:S(2)}) copy-start(f32[1,1,9216]{2,1,0:T(1,128)} %param.14) | copy-start | bytes 110596
  7.2 494.0 %reduce-scatter.4.cloned.1.call-start = ((), (), s32[]{:S(2)}) async-start(), calls=%async_computation.1 | async-start | bytes 5013504
  8.2 110.1 %collective-permute-start.16 = (f32[1,2,2,1,9216]{4,2,3,1,0:T(2,128)S(1)}, f32[1,2,2,1,9216]{4,2,3,1,0:T(2,128)}, u32[]{:S(2)}, u32[]{:S(2)}) collective-permute-start(f32[1,2,2,1,9216]{4,2,3,1,0:T(2,128)S(1)} %bitcast.528), channel_id=1, source_target_pairs={{1,0},{2,1},{3,2},{4,3},{5,4},{6,5},{7,6},{8,7},{9,8},{10,9},{11,1... | collective-permute-start | bytes 442376 | tf_op jit(solution)/shard_map/ppermute | solution.py:26
  11.5 106.7 %collective-permute-start.17 = (f32[1,2,2,1,9216]{4,2,3,1,0:T(2,128)S(1)}, f32[1,2,2,1,9216]{4,2,3,1,0:T(2,128)}, u32[]{:S(2)}, u32[]{:S(2)}) collective-permute-start(f32[1,2,2,1,9216]{4,2,3,1,0:T(2,128)S(1)} %bitcast.529), channel_id=1, source_target_pairs={{0,1},{1,2},{2,3},{3,4},{4,5},{5,6},{6,7},{7,8},{8,9},{9,10},{10,1... | collective-permute-start | bytes 442376 | tf_op jit(solution)/shard_map/ppermute | solution.py:25
  12.5 112.2 %collective-permute-start = (f32[1,2,2,1,9216]{4,2,3,1,0:T(2,128)S(1)}, f32[1,2,2,1,9216]{4,2,3,1,0:T(2,128)}, u32[]{:S(2)}, u32[]{:S(2)}) collective-permute-start(f32[1,2,2,1,9216]{4,2,3,1,0:T(2,128)S(1)} %bitcast.520), channel_id=1, source_target_pairs={{1,0},{2,1},{3,2},{4,3},{5,4},{6,5},{7,6},{8,7},{9,8},{10,9},{11,1... | collective-permute-start | bytes 442376 | tf_op jit(solution)/shard_map/ppermute | solution.py:26
  14.1 110.7 %collective-permute-start.1 = (f32[1,2,2,1,9216]{4,2,3,1,0:T(2,128)S(1)}, f32[1,2,2,1,9216]{4,2,3,1,0:T(2,128)}, u32[]{:S(2)}, u32[]{:S(2)}) collective-permute-start(f32[1,2,2,1,9216]{4,2,3,1,0:T(2,128)S(1)} %bitcast.521), channel_id=1, source_target_pairs={{0,1},{1,2},{2,3},{3,4},{4,5},{5,6},{6,7},{7,8},{8,9},{9,10},{10,1... | collective-permute-start | bytes 442376 | tf_op jit(solution)/shard_map/ppermute | solution.py:25
  122.2 42.7 %collective-permute-start.18 = (f32[1,2,2,1,9216]{4,2,3,1,0:T(2,128)S(1)}, f32[1,2,2,1,9216]{4,2,3,1,0:T(2,128)}, u32[]{:S(2)}, u32[]{:S(2)}) collective-permute-start(f32[1,2,2,1,9216]{4,2,3,1,0:T(2,128)S(1)} %pad_maximum_fusion.6), channel_id=1, source_target_pairs={{1,0},{2,1},{3,2},{4,3},{5,4},{6,5},{7,6},{8,7},{9,8},{10,9},{11,1... | collective-permute-start | bytes 442376 | tf_op jit(solution)/shard_map/ppermute | solution.py:26
  123.0 42.0 %collective-permute-start.19 = (f32[1,2,2,1,9216]{4,2,3,1,0:T(2,128)S(1)}, f32[1,2,2,1,9216]{4,2,3,1,0:T(2,128)}, u32[]{:S(2)}, u32[]{:S(2)}) collective-permute-start(f32[1,2,2,1,9216]{4,2,3,1,0:T(2,128)S(1)} %pad_maximum_fusion.6), channel_id=1, source_target_pairs={{0,1},{1,2},{2,3},{3,4},{4,5},{5,6},{6,7},{7,8},{8,9},{9,10},{10,1... | collective-permute-start | bytes 442376 | tf_op jit(solution)/shard_map/ppermute | solution.py:25
  127.1 37.8 %copy-start.50 = (pred[9216]{0:T(1024)(128)(4,1)S(1)}, pred[9216]{0:T(1024)(128)(4,1)}, u32[]{:S(2)}) copy-start(pred[9216]{0:T(1024)(128)(4,1)} %get-tuple-element.312) | copy-start | bytes 27652
  127.1 37.8 %copy-start.70 = (f32[1,2,2,1,96]{4,2,3,1,0:T(2,128)S(1)}, f32[1,2,2,1,96]{4,2,3,1,0:T(2,128)}, u32[]{:S(2)}) copy-start(f32[1,2,2,1,96]{4,2,3,1,0:T(2,128)} %get-tuple-element.243) | copy-start | bytes 4612
  127.1 37.8 %copy-start.71 = (f32[1,2,2,1,96]{4,2,3,1,0:T(2,128)S(1)}, f32[1,2,2,1,96]{4,2,3,1,0:T(2,128)}, u32[]{:S(2)}) copy-start(f32[1,2,2,1,96]{4,2,3,1,0:T(2,128)} %get-tuple-element.244) | copy-start | bytes 4612
  127.1 37.8 %copy-start.87 = (f32[1,9216]{1,0:T(1,128)S(1)}, f32[1,9216]{1,0:T(1,128)}, u32[]{:S(2)}) copy-start(f32[1,9216]{1,0:T(1,128)} %param.13) | copy-start | bytes 110596
  131.2 43.5 %collective-permute-start.2 = (f32[1,2,2,1,9216]{4,2,3,1,0:T(2,128)S(1)}, f32[1,2,2,1,9216]{4,2,3,1,0:T(2,128)}, u32[]{:S(2)}, u32[]{:S(2)}) collective-permute-start(f32[1,2,2,1,9216]{4,2,3,1,0:T(2,128)S(1)} %get-tuple-element.265), channel_id=1, source_target_pairs={{1,0},{2,1},{3,2},{4,3},{5,4},{6,5},{7,6},{8,7},{9,8},{10,9},{11,1... | collective-permute-start | bytes 442376 | tf_op jit(solution)/shard_map/ppermute | solution.py:26
  131.3 43.5 %collective-permute-start.3 = (f32[1,2,2,1,9216]{4,2,3,1,0:T(2,128)S(1)}, f32[1,2,2,1,9216]{4,2,3,1,0:T(2,128)}, u32[]{:S(2)}, u32[]{:S(2)}) collective-permute-start(f32[1,2,2,1,9216]{4,2,3,1,0:T(2,128)S(1)} %get-tuple-element.265), channel_id=1, source_target_pairs={{0,1},{1,2},{2,3},{3,4},{4,5},{5,6},{6,7},{7,8},{8,9},{9,10},{10,1... | collective-permute-start | bytes 442376 | tf_op jit(solution)/shard_map/ppermute | solution.py:25
  169.4 47.0 %collective-permute-start.20 = (f32[1,2,2,1,9216]{4,2,3,1,0:T(2,128)S(1)}, f32[1,2,2,1,9216]{4,2,3,1,0:T(2,128)}, u32[]{:S(2)}, u32[]{:S(2)}) collective-permute-start(f32[1,2,2,1,9216]{4,2,3,1,0:T(2,128)S(1)} %pad_maximum_fusion.7), channel_id=1, source_target_pairs={{1,0},{2,1},{3,2},{4,3},{5,4},{6,5},{7,6},{8,7},{9,8},{10,9},{11,1... | collective-permute-start | bytes 442376 | tf_op jit(solution)/shard_map/ppermute | solution.py:26
  173.9 42.5 %collective-permute-start.21 = (f32[1,2,2,1,9216]{4,2,3,1,0:T(2,128)S(1)}, f32[1,2,2,1,9216]{4,2,3,1,0:T(2,128)}, u32[]{:S(2)}, u32[]{:S(2)}) collective-permute-start(f32[1,2,2,1,9216]{4,2,3,1,0:T(2,128)S(1)} %pad_maximum_fusion.7), channel_id=1, source_target_pairs={{0,1},{1,2},{2,3},{3,4},{4,5},{5,6},{6,7},{7,8},{8,9},{9,10},{10,1... | collective-permute-start | bytes 442376 | tf_op jit(solution)/shard_map/ppermute | solution.py:25
  182.2 45.8 %collective-permute-start.4 = (f32[1,2,2,1,9216]{4,2,3,1,0:T(2,128)S(1)}, f32[1,2,2,1,9216]{4,2,3,1,0:T(2,128)}, u32[]{:S(2)}, u32[]{:S(2)}) collective-permute-start(f32[1,2,2,1,9216]{4,2,3,1,0:T(2,128)S(1)} %pad_maximum_fusion.1), channel_id=1, source_target_pairs={{1,0},{2,1},{3,2},{4,3},{5,4},{6,5},{7,6},{8,7},{9,8},{10,9},{11,1... | collective-permute-start | bytes 442376 | tf_op jit(solution)/shard_map/ppermute | solution.py:26
  182.8 45.3 %collective-permute-start.5 = (f32[1,2,2,1,9216]{4,2,3,1,0:T(2,128)S(1)}, f32[1,2,2,1,9216]{4,2,3,1,0:T(2,128)}, u32[]{:S(2)}, u32[]{:S(2)}) collective-permute-start(f32[1,2,2,1,9216]{4,2,3,1,0:T(2,128)S(1)} %pad_maximum_fusion.1), channel_id=1, source_target_pairs={{0,1},{1,2},{2,3},{3,4},{4,5},{5,6},{6,7},{7,8},{8,9},{9,10},{10,1... | collective-permute-start | bytes 442376 | tf_op jit(solution)/shard_map/ppermute | solution.py:25
  222.9 44.2 %collective-permute-start.22 = (f32[1,2,2,1,9216]{4,2,3,1,0:T(2,128)S(1)}, f32[1,2,2,1,9216]{4,2,3,1,0:T(2,128)}, u32[]{:S(2)}, u32[]{:S(2)}) collective-permute-start(f32[1,2,2,1,9216]{4,2,3,1,0:T(2,128)S(1)} %pad_maximum_fusion.8), channel_id=1, source_target_pairs={{1,0},{2,1},{3,2},{4,3},{5,4},{6,5},{7,6},{8,7},{9,8},{10,9},{11,1... | collective-permute-start | bytes 442376 | tf_op jit(solution)/shard_map/ppermute | solution.py:26
  227.5 39.7 %collective-permute-start.23 = (f32[1,2,2,1,9216]{4,2,3,1,0:T(2,128)S(1)}, f32[1,2,2,1,9216]{4,2,3,1,0:T(2,128)}, u32[]{:S(2)}, u32[]{:S(2)}) collective-permute-start(f32[1,2,2,1,9216]{4,2,3,1,0:T(2,128)S(1)} %pad_maximum_fusion.8), channel_id=1, source_target_pairs={{0,1},{1,2},{2,3},{3,4},{4,5},{5,6},{6,7},{7,8},{8,9},{9,10},{10,1... | collective-permute-start | bytes 442376 | tf_op jit(solution)/shard_map/ppermute | solution.py:25
  233.9 46.0 %collective-permute-start.6 = (f32[1,2,2,1,9216]{4,2,3,1,0:T(2,128)S(1)}, f32[1,2,2,1,9216]{4,2,3,1,0:T(2,128)}, u32[]{:S(2)}, u32[]{:S(2)}) collective-permute-start(f32[1,2,2,1,9216]{4,2,3,1,0:T(2,128)S(1)} %pad_maximum_fusion.2), channel_id=1, source_target_pairs={{1,0},{2,1},{3,2},{4,3},{5,4},{6,5},{7,6},{8,7},{9,8},{10,9},{11,1... | collective-permute-start | bytes 442376 | tf_op jit(solution)/shard_map/ppermute | solution.py:26
  234.5 45.5 %collective-permute-start.7 = (f32[1,2,2,1,9216]{4,2,3,1,0:T(2,128)S(1)}, f32[1,2,2,1,9216]{4,2,3,1,0:T(2,128)}, u32[]{:S(2)}, u32[]{:S(2)}) collective-permute-start(f32[1,2,2,1,9216]{4,2,3,1,0:T(2,128)S(1)} %pad_maximum_fusion.2), channel_id=1, source_target_pairs={{0,1},{1,2},{2,3},{3,4},{4,5},{5,6},{6,7},{7,8},{8,9},{9,10},{10,1... | collective-permute-start | bytes 442376 | tf_op jit(solution)/shard_map/ppermute | solution.py:25
  273.5 229.4 %collective-permute-start.24 = (f32[1,2,2,1,9216]{4,2,3,1,0:T(2,128)S(1)}, f32[1,2,2,1,9216]{4,2,3,1,0:T(2,128)}, u32[]{:S(2)}, u32[]{:S(2)}) collective-permute-start(f32[1,2,2,1,9216]{4,2,3,1,0:T(2,128)S(1)} %fusion.432), channel_id=1, source_target_pairs={{1,0},{2,1},{3,2},{4,3},{5,4},{6,5},{7,6},{8,7},{9,8},{10,9},{11,1... | collective-permute-start | bytes 442376 | tf_op jit(solution)/shard_map/ppermute | solution.py:26
  278.0 224.9 %collective-permute-start.25 = (f32[1,2,2,1,9216]{4,2,3,1,0:T(2,128)S(1)}, f32[1,2,2,1,9216]{4,2,3,1,0:T(2,128)}, u32[]{:S(2)}, u32[]{:S(2)}) collective-permute-start(f32[1,2,2,1,9216]{4,2,3,1,0:T(2,128)S(1)} %fusion.432), channel_id=1, source_target_pairs={{0,1},{1,2},{2,3},{3,4},{4,5},{5,6},{6,7},{7,8},{8,9},{9,10},{10,1... | collective-permute-start | bytes 442376 | tf_op jit(solution)/shard_map/ppermute | solution.py:25
  286.4 229.4 %collective-permute-start.8 = (f32[1,2,2,1,9216]{4,2,3,1,0:T(2,128)S(1)}, f32[1,2,2,1,9216]{4,2,3,1,0:T(2,128)}, u32[]{:S(2)}, u32[]{:S(2)}) collective-permute-start(f32[1,2,2,1,9216]{4,2,3,1,0:T(2,128)S(1)} %fusion.433), channel_id=1, source_target_pairs={{1,0},{2,1},{3,2},{4,3},{5,4},{6,5},{7,6},{8,7},{9,8},{10,9},{11,1... | collective-permute-start | bytes 442376 | tf_op jit(solution)/shard_map/ppermute | solution.py:26
  286.9 228.9 %collective-permute-start.9 = (f32[1,2,2,1,9216]{4,2,3,1,0:T(2,128)S(1)}, f32[1,2,2,1,9216]{4,2,3,1,0:T(2,128)}, u32[]{:S(2)}, u32[]{:S(2)}) collective-permute-start(f32[1,2,2,1,9216]{4,2,3,1,0:T(2,128)S(1)} %fusion.433), channel_id=1, source_target_pairs={{0,1},{1,2},{2,3},{3,4},{4,5},{5,6},{6,7},{7,8},{8,9},{9,10},{10,1... | collective-permute-start | bytes 442376 | tf_op jit(solution)/shard_map/ppermute | solution.py:25
  295.0 29.9 %copy-start.2 = (f32[16,9216]{1,0:T(8,128)S(1)}, f32[16,9216]{1,0:T(8,128)}, u32[]{:S(2)}) copy-start(f32[16,9216]{1,0:T(8,128)} %get-tuple-element.30) | copy-start | bytes 1769476
  295.0 29.9 %copy-start.3 = (f32[16,9216]{1,0:T(8,128)S(1)}, f32[16,9216]{1,0:T(8,128)}, u32[]{:S(2)}) copy-start(f32[16,9216]{1,0:T(8,128)} %get-tuple-element.31) | copy-start | bytes 1769476
  295.0 207.9 %copy-start.32 = (f32[1,2,2,1,9120]{4,2,3,1,0:T(2,128)S(1)}, f32[1,2,2,1,9120]{4,2,3,1,0:T(2,128)}, u32[]{:S(2)}) copy-start(f32[1,2,2,1,9120]{4,2,3,1,0:T(2,128)} %get-tuple-element.169) | copy-start | bytes 437764
  505.3 10.5 %copy-start.33 = (f32[1,2,2,1,9120]{4,2,3,1,0:T(2,128)S(1)}, f32[1,2,2,1,9120]{4,2,3,1,0:T(2,128)}, u32[]{:S(2)}) copy-start(f32[1,2,2,1,9120]{4,2,3,1,0:T(2,128)} %get-tuple-element.181) | copy-start | bytes 437764
  505.3 10.4 %copy-start.34 = (f32[1,2,2,1,9120]{4,2,3,1,0:T(2,128)S(1)}, f32[1,2,2,1,9120]{4,2,3,1,0:T(2,128)}, u32[]{:S(2)}) copy-start(f32[1,2,2,1,9120]{4,2,3,1,0:T(2,128)} %get-tuple-element.182) | copy-start | bytes 437764
  505.4 10.4 %copy-start.35 = (f32[1,2,2,1,9121]{4,2,3,1,0:T(2,128)S(1)}, f32[1,2,2,1,9121]{4,2,3,1,0:T(2,128)}, u32[]{:S(2)}) copy-start(f32[1,2,2,1,9121]{4,2,3,1,0:T(2,128)} %get-tuple-element.187) | copy-start | bytes 437812
  505.4 10.4 %copy-start.36 = (f32[1,2,2,1,9121]{4,2,3,1,0:T(2,128)S(1)}, f32[1,2,2,1,9121]{4,2,3,1,0:T(2,128)}, u32[]{:S(2)}) copy-start(f32[1,2,2,1,9121]{4,2,3,1,0:T(2,128)} %get-tuple-element.188) | copy-start | bytes 437812
  505.4 10.4 %copy-start.37 = (f32[1,2,2,1,9215]{4,2,3,1,0:T(2,128)S(1)}, f32[1,2,2,1,9215]{4,2,3,1,0:T(2,128)}, u32[]{:S(2)}) copy-start(f32[1,2,2,1,9215]{4,2,3,1,0:T(2,128)} %get-tuple-element.189) | copy-start | bytes 442324
  507.7 43.9 %collective-permute-start.26 = (f32[1,2,2,1,9216]{4,2,3,1,0:T(2,128)S(1)}, f32[1,2,2,1,9216]{4,2,3,1,0:T(2,128)}, u32[]{:S(2)}, u32[]{:S(2)}) collective-permute-start(f32[1,2,2,1,9216]{4,2,3,1,0:T(2,128)S(1)} %get-tuple-element.155), channel_id=1, source_target_pairs={{1,0},{2,1},{3,2},{4,3},{5,4},{6,5},{7,6},{8,7},{9,8},{10,9},{11,1... | collective-permute-start | bytes 442376 | tf_op jit(solution)/shard_map/ppermute | solution.py:26
  512.7 38.9 %collective-permute-start.27 = (f32[1,2,2,1,9216]{4,2,3,1,0:T(2,128)S(1)}, f32[1,2,2,1,9216]{4,2,3,1,0:T(2,128)}, u32[]{:S(2)}, u32[]{:S(2)}) collective-permute-start(f32[1,2,2,1,9216]{4,2,3,1,0:T(2,128)S(1)} %get-tuple-element.155), channel_id=1, source_target_pairs={{0,1},{1,2},{2,3},{3,4},{4,5},{5,6},{6,7},{7,8},{8,9},{9,10},{10,1... | collective-permute-start | bytes 442376 | tf_op jit(solution)/shard_map/ppermute | solution.py:25
  520.3 43.1 %collective-permute-start.10 = (f32[1,2,2,1,9216]{4,2,3,1,0:T(2,128)S(1)}, f32[1,2,2,1,9216]{4,2,3,1,0:T(2,128)}, u32[]{:S(2)}, u32[]{:S(2)}) collective-permute-start(f32[1,2,2,1,9216]{4,2,3,1,0:T(2,128)S(1)} %pad_maximum_fusion.3), channel_id=1, source_target_pairs={{1,0},{2,1},{3,2},{4,3},{5,4},{6,5},{7,6},{8,7},{9,8},{10,9},{11,1... | collective-permute-start | bytes 442376 | tf_op jit(solution)/shard_map/ppermute | solution.py:26
  520.3 43.0 %collective-permute-start.11 = (f32[1,2,2,1,9216]{4,2,3,1,0:T(2,128)S(1)}, f32[1,2,2,1,9216]{4,2,3,1,0:T(2,128)}, u32[]{:S(2)}, u32[]{:S(2)}) collective-permute-start(f32[1,2,2,1,9216]{4,2,3,1,0:T(2,128)S(1)} %pad_maximum_fusion.3), channel_id=1, source_target_pairs={{0,1},{1,2},{2,3},{3,4},{4,5},{5,6},{6,7},{7,8},{8,9},{9,10},{10,1... | collective-permute-start | bytes 442376 | tf_op jit(solution)/shard_map/ppermute | solution.py:25
  556.9 43.1 %collective-permute-start.28 = (f32[1,2,2,1,9216]{4,2,3,1,0:T(2,128)S(1)}, f32[1,2,2,1,9216]{4,2,3,1,0:T(2,128)}, u32[]{:S(2)}, u32[]{:S(2)}) collective-permute-start(f32[1,2,2,1,9216]{4,2,3,1,0:T(2,128)S(1)} %get-tuple-element.125), channel_id=1, source_target_pairs={{1,0},{2,1},{3,2},{4,3},{5,4},{6,5},{7,6},{8,7},{9,8},{10,9},{11,1... | collective-permute-start | bytes 442376 | tf_op jit(solution)/shard_map/ppermute | solution.py:26
  561.3 38.6 %collective-permute-start.29 = (f32[1,2,2,1,9216]{4,2,3,1,0:T(2,128)S(1)}, f32[1,2,2,1,9216]{4,2,3,1,0:T(2,128)}, u32[]{:S(2)}, u32[]{:S(2)}) collective-permute-start(f32[1,2,2,1,9216]{4,2,3,1,0:T(2,128)S(1)} %get-tuple-element.125), channel_id=1, source_target_pairs={{0,1},{1,2},{2,3},{3,4},{4,5},{5,6},{6,7},{7,8},{8,9},{9,10},{10,1... | collective-permute-start | bytes 442376 | tf_op jit(solution)/shard_map/ppermute | solution.py:25
  565.5 34.5 %copy-start.45 = (f32[1,2,2,1,9120]{4,2,3,1,0:T(2,128)S(1)}, f32[1,2,2,1,9120]{4,2,3,1,0:T(2,128)}, u32[]{:S(2)}) copy-start(f32[1,2,2,1,9120]{4,2,3,1,0:T(2,128)} %get-tuple-element.113) | copy-start | bytes 437764
  567.7 44.3 %collective-permute-start.12 = (f32[1,2,2,1,9216]{4,2,3,1,0:T(2,128)S(1)}, f32[1,2,2,1,9216]{4,2,3,1,0:T(2,128)}, u32[]{:S(2)}, u32[]{:S(2)}) collective-permute-start(f32[1,2,2,1,9216]{4,2,3,1,0:T(2,128)S(1)} %pad_maximum_fusion.4), channel_id=1, source_target_pairs={{1,0},{2,1},{3,2},{4,3},{5,4},{6,5},{7,6},{8,7},{9,8},{10,9},{11,1... | collective-permute-start | bytes 442376 | tf_op jit(solution)/shard_map/ppermute | solution.py:26
  568.3 43.7 %collective-permute-start.13 = (f32[1,2,2,1,9216]{4,2,3,1,0:T(2,128)S(1)}, f32[1,2,2,1,9216]{4,2,3,1,0:T(2,128)}, u32[]{:S(2)}, u32[]{:S(2)}) collective-permute-start(f32[1,2,2,1,9216]{4,2,3,1,0:T(2,128)S(1)} %pad_maximum_fusion.4), channel_id=1, source_target_pairs={{0,1},{1,2},{2,3},{3,4},{4,5},{5,6},{6,7},{7,8},{8,9},{9,10},{10,1... | collective-permute-start | bytes 442376 | tf_op jit(solution)/shard_map/ppermute | solution.py:25
  605.4 77.3 %collective-permute-start.30 = (f32[1,2,2,1,9216]{4,2,3,1,0:T(2,128)S(1)}, f32[1,2,2,1,9216]{4,2,3,1,0:T(2,128)}, u32[]{:S(2)}, u32[]{:S(2)}) collective-permute-start(f32[1,2,2,1,9216]{4,2,3,1,0:T(2,128)S(1)} %get-tuple-element.69), channel_id=1, source_target_pairs={{1,0},{2,1},{3,2},{4,3},{5,4},{6,5},{7,6},{8,7},{9,8},{10,9},{11,1... | collective-permute-start | bytes 442376 | tf_op jit(solution)/shard_map/ppermute | solution.py:26
  609.8 72.8 %collective-permute-start.31 = (f32[1,2,2,1,9216]{4,2,3,1,0:T(2,128)S(1)}, f32[1,2,2,1,9216]{4,2,3,1,0:T(2,128)}, u32[]{:S(2)}, u32[]{:S(2)}) collective-permute-start(f32[1,2,2,1,9216]{4,2,3,1,0:T(2,128)S(1)} %get-tuple-element.69), channel_id=1, source_target_pairs={{0,1},{1,2},{2,3},{3,4},{4,5},{5,6},{6,7},{7,8},{8,9},{9,10},{10,1... | collective-permute-start | bytes 442376 | tf_op jit(solution)/shard_map/ppermute | solution.py:25
  616.4 70.4 %collective-permute-start.14 = (f32[1,2,2,1,9216]{4,2,3,1,0:T(2,128)S(1)}, f32[1,2,2,1,9216]{4,2,3,1,0:T(2,128)}, u32[]{:S(2)}, u32[]{:S(2)}) collective-permute-start(f32[1,2,2,1,9216]{4,2,3,1,0:T(2,128)S(1)} %pad_maximum_fusion.5), channel_id=1, source_target_pairs={{1,0},{2,1},{3,2},{4,3},{5,4},{6,5},{7,6},{8,7},{9,8},{10,9},{11,1... | collective-permute-start | bytes 442376 | tf_op jit(solution)/shard_map/ppermute | solution.py:26
  650.0 36.8 %collective-permute-start.15 = (f32[1,2,2,1,9216]{4,2,3,1,0:T(2,128)S(1)}, f32[1,2,2,1,9216]{4,2,3,1,0:T(2,128)}, u32[]{:S(2)}, u32[]{:S(2)}) collective-permute-start(f32[1,2,2,1,9216]{4,2,3,1,0:T(2,128)S(1)} %pad_maximum_fusion.5), channel_id=1, source_target_pairs={{0,1},{1,2},{2,3},{3,4},{4,5},{5,6},{6,7},{7,8},{8,9},{9,10},{10,1... | collective-permute-start | bytes 442376 | tf_op jit(solution)/shard_map/ppermute | solution.py:25
  (77 other events, 488.3 us)
Sparse Core Ops, SparseCore 0:
  295.1 206.0 reduce-scatter.3
where the time goes:
time: 711 us; the launch traced here: 698 us
  blocking collectives  311 us (44%)
  waiting for transfers between devices  173 us (24%)
  matrix products  54.6 us (8%)
  local copies, waits for them, and re-layouts  50.8 us (7%)
  starting transfers between devices  47.6 us (7%)
  other arithmetic  45 us (6%)
  between operations  16.3 us (2%)
    psum x8, blocking collectives, hamiltonian(): summed = lax.psum(partial_value, 'space')  239 us
    unnamed x2, waiting for transfers between devices  173 us
    all_gather x1, blocking collectives, body(): gathered = lax.all_gather(projector_tiles, 'band', axis=0, tiled=True)  39.8 us
    ppermute x16, starting transfers between devices, padded_2(): after = lax.ppermute(first, axis, down)  36.1 us
    dot_general x16, matrix products, hamiltonian(): jnp.dot(summed * strengths, basis_rows, precision=highest, preferred_elem...  35.9 us
    psum x1, blocking collectives, body(): forces = lax.psum(local_force, 'band') / NB  31.9 us
    another operation x80, other arithmetic, taylor(): jnp.stack([-(factor * applied[:, 1]), factor * applied[:, 0]], axis=1)  29.5 us
    dot_general x16, matrix products, hamiltonian(): jnp.dot(flat_rows, basis_rows.T, precision=highest, preferred_element_typ...  15 us
  transfers between devices with their start and end apart: 33, of which 1 were waited for; matrix products, arithmetic and copies ran while one was open for 21% of the time, Pallas kernels for 0%

commit v1 on v0

v1 whole, which is shorter than its diff:
```python
import functools
import math

import jax
import jax.numpy as jnp
import numpy as np
from jax import lax
from jax.experimental import pallas as pl
from jax.experimental.pallas import tpu as pltpu
from jax.sharding import PartitionSpec as P

NB = 32
NY = 96
NZ = 96
ROWS = 72
LANES = 128
PRJ = 16
PRJ_ATOM = 4

half_step = 0.025
kinetic_scale = 3.125
highest = lax.Precision.HIGHEST
f32 = jnp.float32

A2 = -(half_step**2) / 2.0
A3 = -(half_step**3) / 6.0
A4 = half_step**4 / 24.0


def neighbour_masks():
    flat = np.arange(ROWS * LANES)
    lane, column = flat % LANES, flat % NZ
    masks = [
        (column == 95) & (lane >= 95),
        (column != 95) & (lane < 127),
        (column == 0) & (lane < 33),
        (column != 0) & (lane >= 1),
        (column == 32) & (lane >= 33),
        (column != 31) & (lane == 127),
        (column == 63) & (lane < 95),
        (column != 64) & (lane == 0),
    ]
    return np.stack(masks).astype(np.float32).reshape(8, ROWS, LANES)


def in_plane(x, masks):
    lane = lax.broadcasted_iota(jnp.int32, (ROWS, LANES), 1)
    up_z = pltpu.roll(x, 127, 1)
    up_z_end = pltpu.roll(x, 95, 1)
    down_z = pltpu.roll(x, 1, 1)
    down_z_end = pltpu.roll(x, 33, 1)
    up_y = pltpu.roll(x, 32, 1)
    down_y = pltpu.roll(x, 96, 1)
    same = (
        masks[0] * up_z_end
        + masks[1] * up_z
        + masks[2] * down_z_end
        + masks[3] * down_z
        + jnp.where(lane < 32, up_y, 0.0)
        + jnp.where(lane >= 96, down_y, 0.0)
    )
    after = masks[4] * down_z_end + masks[5] * up_z + jnp.where(lane >= 32, up_y, 0.0)
    before = masks[6] * up_z_end + masks[7] * down_z + jnp.where(lane < 96, down_y, 0.0)
    return same + pltpu.roll(after, ROWS - 1, 0) + pltpu.roll(before, 1, 0)


def local(x, beside, potential, masks):
    return kinetic_scale * (6.0 * x - in_plane(x, masks) - beside) + potential * x


def fold(x):
    return jnp.sum(x.reshape(ROWS // 8, 8, LANES), axis=0)


def rows8(parts):
    sub = lax.broadcasted_iota(jnp.int32, (8, LANES), 0)
    low = sub < 4
    parts = [
        jnp.where(low, a, b) + pltpu.roll(jnp.where(low, b, a), 4, 0)
        for a, b in zip(parts[:4], parts[4:])
    ]
    for step in (2, 1):
        first = (sub & step) == 0
        parts = [
            jnp.where(first, a + pltpu.roll(a, 8 - step, 0), b + pltpu.roll(b, step, 0))
            for a, b in zip(parts[:step], parts[step:])
        ]
    return parts[0]


def params(mib):
    return pltpu.CompilerParams(vmem_limit_bytes=mib * 2**20)


VMEM = pl.BlockSpec(memory_space=pltpu.VMEM)
SMEM = pl.BlockSpec(memory_space=pltpu.SMEM)


def call(kernel, outs, args, scratch=(), scalars=0, mib=24, cost=None):
    specs = [SMEM] * scalars + [VMEM] * (len(args) - scalars)
    single = not isinstance(outs, list)
    shapes = [jax.ShapeDtypeStruct(o, f32) for o in ([outs] if single else outs)]
    result = pl.pallas_call(
        kernel,
        out_shape=shapes,
        in_specs=specs,
        out_specs=[VMEM] * len(shapes),
        scratch_shapes=list(scratch),
        compiler_params=params(mib),
        cost_estimate=cost,
    )(*args)
    return result[0] if single else result


def projector_kernel(beta, beside_a, beside_b, masks, out):
    x = beta[...]
    out[0] = x
    out[1] = kinetic_scale * (6.0 * x - in_plane(x, masks) - (beside_a[...] + beside_b[...]))


def two_steps(near, far, center, edge_potential, potential, masks, first, edge, second):
    def row(q, carry):
        own, other = center[0, q], center[1, q]
        edge_near, edge_far = near[4 + q], far[q]
        first[0, q] = local(own, edge_near + other, potential[0], masks)
        first[1, q] = local(other, own + edge_far, potential[1], masks)
        edge[0, q] = local(edge_near, near[q] + own, edge_potential[0], masks)
        edge[1, q] = local(edge_far, other + far[4 + q], edge_potential[1], masks)
        second[0, q] = local(first[0, q], edge[0, q] + first[1, q], potential[0], masks)
        second[1, q] = local(first[1, q], first[0, q] + edge[1, q], potential[1], masks)
        return carry

    lax.fori_loop(0, 4, row, 0)


def spread(parts, lanes):
    total = jnp.concatenate([rows8(parts[k : k + 8]) for k in range(0, len(parts), 8)], 0)
    summed = jnp.sum(total, axis=1, keepdims=True)
    lane = lax.broadcasted_iota(jnp.int32, total.shape, 1)
    return jnp.where(lane == lanes, summed, 0.0)


def moments_kernel(slopes, *refs):
    near, far, center, edge_potential, potential, masks, basis_own, basis_other = refs[:8]
    refs = refs[8:]
    if slopes:
        wave_x, wave_y, wave_z = refs[:3]
        refs = refs[3:]
    first, second, out, edge = refs
    two_steps(near, far, center, edge_potential, potential, masks, first, edge, second)
    count = 32 if slopes else 16

    def projector(j, total):
        atom = j // PRJ_ATOM
        parts = [[None] * 4 for _ in range(7)]
        for plane, basis in ((0, basis_own), (1, basis_other)):
            beta = basis[j, 0]
            wide = basis[j, 1] + potential[plane] * beta
            if slopes:
                beta_y, beta_z = beta * wave_y[atom], beta * wave_z[atom]
            for q in range(4):
                x = center[plane, q]
                found = [fold(x * beta), fold(x * wide)]
                found += [fold(first[plane, q] * wide), fold(second[plane, q] * wide)]
                if slopes:
                    found += [found[0] * wave_x[plane, atom]]
                    found += [fold(x * beta_y), fold(x * beta_z)]
                for k, value in enumerate(found):
                    parts[k][q] = value if plane == 0 else parts[k][q] + value
        flat = [parts[k][q] for k in range(7 if slopes else 4) for q in range(4)]
        flat += [jnp.zeros((8, LANES), f32)] * (count - len(flat))
        return total + spread(flat, j)

    out[...] = lax.fori_loop(0, PRJ, projector, jnp.zeros((count, LANES), f32))


def gram_kernel(basis, potentials, out, wide):
    for k in range(2):
        for j in range(PRJ):
            wide[k, j] = basis[j, 1] + potentials[k] * basis[j, 0]

    def projector(j, total):
        beta, wide_a, wide_b = basis[j, 0], wide[0, j], wide[1, j]
        for group in range(2):
            members = range(8 * group, 8 * group + 8)
            found = [
                [fold(beta * basis[i, 0]) for i in members],
                [fold(wide_a * basis[i, 0]) for i in members],
                [fold(wide_a * wide[0, i]) for i in members],
                [fold(wide_b * basis[i, 0]) for i in members],
                [fold(wide_b * wide[1, i]) for i in members],
            ]
            for k, parts in enumerate(found):
                total[group] = total[group] + spread(parts, PRJ * (k + 1) + j)
        return total

    start = [jnp.zeros((8, LANES), f32)] * 2
    total = lax.fori_loop(0, PRJ, projector, start)
    out[...] = jnp.concatenate(total, 0)


def times_i(x):
    row = lax.broadcasted_iota(jnp.int32, (8, LANES), 0)
    return jnp.where(row < 2, -pltpu.roll(x, 6, 0), pltpu.roll(x, 2, 0))


def coefficients_kernel(later, flags, received, strengths, *refs):
    if later:
        gram, table = refs
    else:
        table, gram = refs
    upper, sign = flags[0], flags[1]
    sums = []
    for core in range(2):
        acc = received[core]
        for k in range(core + 2, 16, 2):
            acc = acc + received[k]
        sums.append(acc)
    if later:
        grams = gram[...]
    else:
        grams = (sums[0] + sums[1])[:PRJ]
        gram[...] = grams
    mine = jnp.where(upper > 0.5, sums[1], sums[0])[:PRJ]
    lane = lax.broadcasted_iota(jnp.int32, (PRJ, LANES), 1)
    valid = lane < PRJ

    def block(k):
        return jnp.where(valid, pltpu.roll(grams, LANES - PRJ * (k + 1), 1), 0.0)

    use_second = (upper < 0.5) if later else (upper > 0.5)
    g0 = block(0)
    g1 = jnp.where(use_second, block(3), block(1))
    g2 = jnp.where(use_second, block(4), block(2))
    weight = strengths[...]

    def moment(k):
        rolled = mine if k == 0 else pltpu.roll(mine, PRJ - 4 * k, 0)
        return jnp.where(valid, rolled, 0.0)[:8]

    def apply(c, g):
        return jnp.dot(c[:, :PRJ], g, precision=highest, preferred_element_type=f32)

    c0 = weight * moment(0)
    c1 = weight * (moment(1) + apply(c0, g0))
    c2 = weight * (moment(2) + apply(c0, g1) + apply(c1, g0))
    c3 = weight * (moment(3) + apply(c0, g2) + apply(c1, g1) + apply(c2, g0))
    e0 = times_i((sign * half_step) * c0 + (sign * A3) * c2) + A2 * c1 + A4 * c3
    e1 = A2 * c0 + A4 * c2
    row = lax.broadcasted_iota(jnp.int32, (PRJ, LANES), 0)
    for k, c in enumerate((c0, c1, e0, e1)):
        for q in range(4):
            wide = jnp.broadcast_to(c[q : q + 1], (PRJ, LANES))
            column = jnp.sum(jnp.where(row == lane, wide, 0.0), axis=1, keepdims=True)
            for j in range(PRJ):
                table[j, k, q] = jnp.broadcast_to(column[j : j + 1], (8, LANES))


def middle_kernel(flags, center, first, second, basis_own, basis_other, potential, table, u2, partial):
    sign = flags[1]

    def tile(i, carry):
        rows = pl.ds(pl.multiple_of(i * 8, 8), 8)
        for plane, basis in ((0, basis_own), (1, basis_other)):
            v = potential[plane, rows]
            ahead = [second[plane, q, rows] for q in range(4)]
            moved = [first[plane, q, rows] for q in range(4)]
            mixed = [-moved[2], -moved[3], moved[0], moved[1]]
            result = [
                center[plane, q, rows] + (sign * half_step) * mixed[q] + A2 * ahead[q]
                for q in range(4)
            ]
            for j in range(PRJ):
                beta = basis[j, 0, rows]
                wide = basis[j, 1, rows] + v * beta
                for q in range(4):
                    ahead[q] = ahead[q] + table[j, 0, q] * wide + table[j, 1, q] * beta
                    result[q] = result[q] + table[j, 3, q] * wide + table[j, 2, q] * beta
            for q in range(4):
                u2[plane, q, rows] = ahead[q]
                partial[plane, q, rows] = result[q]
        return carry

    lax.fori_loop(0, ROWS // 8, tile, 0)


def last_kernel(flags, near, far, center, edge_potential, potential, masks, partial, out, first, edge, second):
    two_steps(near, far, center, edge_potential, potential, masks, first, edge, second)
    sign = flags[1]
    for plane in range(2):
        for q in range(4):
            mixed = -first[plane, q + 2] if q < 2 else first[plane, q - 2]
            out[plane, q] = partial[plane, q] + (sign * A3) * mixed + A4 * second[plane, q]


def swap_core(x):
    return lax.ppermute(x, "space", [(i, i ^ 1) for i in range(16)])


def body(
    psi_start,
    adjoint_end,
    potential_now,
    potential_next,
    projector_tiles,
    tile_map,
    strengths,
    positions,
):
    space, band = lax.axis_index("space"), lax.axis_index("band")
    lower = (space % 2) == 0
    masks = jnp.asarray(neighbour_masks())
    plane_shape = (ROWS, LANES)
    psi = psi_start.reshape((4,) + plane_shape)
    adjoint = adjoint_end.reshape((4,) + plane_shape)
    potentials = jnp.stack([potential_now, potential_next]).reshape((2,) + plane_shape)
    reach = lax.dynamic_index_in_dim(tile_map.reshape(-1, ROWS), band // PRJ_ATOM, 0, False)
    beta = projector_tiles.reshape(plane_shape) * reach.astype(f32)[:, None]
    flags = jnp.stack([jnp.where(lower, 0.0, 1.0), jnp.where(lower, -1.0, 1.0)]).astype(f32)

    kept = jnp.where(lower, psi, adjoint)
    given = jnp.where(lower, adjoint, psi)
    beta_near = lax.ppermute(
        beta, "space", [(i, (i + 1) % 16 if i % 2 else (i - 1) % 16) for i in range(16)]
    )
    other = swap_core(jnp.concatenate([given, potentials, beta[None]], 0))
    center = jnp.stack([kept, other[:4]])
    potentials_other = other[4:6]

    from_near = [(i, (i + 2) % 16 if i % 2 == 0 else (i - 2) % 16) for i in range(16)]
    from_far = [(j, i) for i, j in from_near]

    def exchange(fields, near_extra=None, far_extra=None):
        flat = fields.reshape((8,) + plane_shape)
        near = flat if near_extra is None else jnp.concatenate([flat, near_extra], 0)
        far = flat if far_extra is None else jnp.concatenate([flat, far_extra], 0)
        return (lax.ppermute(near, "space", from_near), lax.ppermute(far, "space", from_far))

    near, far = exchange(center, potentials_other, potentials)

    own_pair = call(projector_kernel, (2,) + plane_shape, [beta, other[6], beta_near, masks])
    basis_own = lax.all_to_all(
        jnp.broadcast_to(own_pair[None], (PRJ, 2) + plane_shape), "band", 0, 0, tiled=True
    )
    basis_other = swap_core(basis_own)

    now_own, next_own = (potentials[0], potentials[1])
    own_a, own_b = jnp.where(lower, now_own, next_own), jnp.where(lower, next_own, now_own)
    far_side, near_side = far[8:10], near[8:10]
    stacked = jnp.stack([potentials, potentials_other, near_side, far_side], 1)
    early = jnp.where(lower, stacked[0], stacked[1])
    late = jnp.where(lower, stacked[1], stacked[0])

    plane = space + jnp.stack([jnp.int32(0), 1 - 2 * (space % 2)])
    flat = jnp.arange(ROWS * LANES, dtype=jnp.int32)
    wave_x = jnp.sin(
        2.0 * math.pi / 16 * (plane[:, None] - positions[0][None, :]).astype(f32)
    )
    wave_x = jnp.broadcast_to(wave_x[:, :, None, None], (2, 4, 8, LANES))
    wave_y = jnp.sin(
        2.0 * math.pi / NY * (flat[None, :] // NZ - positions[1][:, None]).astype(f32)
    ).reshape((4,) + plane_shape)
    wave_z = jnp.sin(
        2.0 * math.pi / NZ * (flat[None, :] % NZ - positions[2][:, None]).astype(f32)
    ).reshape((4,) + plane_shape)

    gram_part = call(
        gram_kernel,
        (PRJ, LANES),
        [basis_own, potentials],
        scratch=[pltpu.VMEM((2, PRJ) + plane_shape, f32)],
    )
    weight = jnp.pad(strengths, (0, LANES - PRJ)).reshape(1, LANES)
    fields_shape = (2, 4) + plane_shape
    field_scratch = pltpu.VMEM(fields_shape, f32)

    def total(part):
        return lax.all_to_all(
            jnp.broadcast_to(part[None], (16,) + part.shape), "space", 0, 0, tiled=True
        )

    def half(center, near, far, around, gram, slopes):
        v, edge_v = around[:2], around[2:]
        first, second, part = call(
            functools.partial(moments_kernel, slopes is not None),
            [fields_shape, fields_shape, (16 if slopes is None else 32, LANES)],
            [near, far, center, edge_v, v, masks, basis_own, basis_other] + list(slopes or ()),
            scratch=[field_scratch],
        )
        table_shape = (PRJ, 4, 4, 8, LANES)
        if gram is None:
            received = total(part + gram_part)
            table, gram = call(
                functools.partial(coefficients_kernel, False),
                [table_shape, (PRJ, LANES)],
                [flags, received, weight],
                scalars=1,
            )
        else:
            received = total(part)
            table = call(
                functools.partial(coefficients_kernel, True),
                table_shape,
                [flags, received, weight, gram],
                scalars=1,
            )
        u2, partial = call(
            middle_kernel,
            [fields_shape, fields_shape],
            [flags, center, first, second, basis_own, basis_other, v, table],
            scalars=1,
        )
        near, far = exchange(u2)
        result = call(
            last_kernel,
            fields_shape,
            [flags, near, far, u2, edge_v, v, masks, partial],
            scratch=[field_scratch] * 3,
            scalars=1,
        )
        return result, received, gram

    mid, _, gram = half(center, near, far, early, None, None)
    near, far = exchange(mid)
    mine, yours = mid[0], swap_core(mid[1])
    turned = mine[:2] * yours[2:] - mine[2:] * yours[:2]
    density = (-2.0 * half_step * flags[1]) * jnp.sum(turned, axis=0)
    end, received, _ = half(mid, near, far, late, gram, (wave_x, wave_y, wave_z))

    sums = jnp.sum(received.reshape(8, 2, 32, LANES), axis=0)[:, :, :PRJ]
    value, slope = sums[:, :4], sums[:, 16:28].reshape(2, 3, 4, PRJ)
    products = value[:1] * slope[1:] + value[1:] * slope[:1]
    weighted = jnp.sum(products[0], axis=1) * strengths
    forces = jnp.sum(weighted.reshape(3, 4, PRJ_ATOM), axis=2).reshape(12)
    parts = jnp.concatenate(
        [density.reshape(16, 576), jnp.broadcast_to(forces[None], (16, 12))], axis=1
    )
    parts = jnp.pad(parts, ((0, 0), (0, 1024 - 588))).reshape(16, 8, LANES)
    shared = jnp.sum(lax.all_to_all(parts, "band", 0, 0, tiled=True), axis=0).reshape(1024)

    swapped = swap_core(end[1])
    psi_end = jnp.where(lower, end[0], swapped).reshape(psi_start.shape)
    adjoint_start = jnp.where(lower, swapped, end[0]).reshape(adjoint_end.shape)
    return (
        psi_end,
        adjoint_start,
        shared[:576].reshape(1, 576),
        shared[576:588].reshape(3, 4) / NB,
    )


def solution(mesh):
    return jax.shard_map(
        body,
        mesh=mesh,
        in_specs=(
            P(None, "band", "space", None),
            P(None, "band", "space", None),
            P("space", None),
            P("space", None),
            P("band", "space", None),
            P(None, "space", None),
            P(),
            P(),
        ),
        out_specs=(
            P(None, "band", "space", None),
            P(None, "band", "space", None),
            P("space", "band"),
            P(),
        ),
        check_vma=False,
    )
```

time: 711 us -> 161 us (0.23); the launches traced: 698 us -> 160 us
  blocking collectives: 311 us -> 13.6 us
  waiting for transfers between devices: 173 us -> 52.7 us
  matrix products: 54.6 us -> 0 us
  local copies, waits for them, and re-layouts: 50.8 us -> 11.8 us
  other arithmetic: 45 us -> 9.04 us
  Pallas kernels: 0 us -> 30.3 us
  between operations: 16.3 us -> 0.99 us
    psum x9 -> x0, blocking collectives: 271 us -> none  [the longest x8 239 us: hamiltonian(): summed = lax.psum(partial_value, 'space')]
    unnamed x2 -> x0, waiting for transfers between devices: 173 us -> none
    dot_general x33 -> x0, matrix products: 54.6 us -> none  [the longest x16 35.9 us: hamiltonian(): jnp.dot(summed * strengths, basis_rows, precision=highest, preferred_elem...]
    all_gather x1 -> x0, blocking collectives: 39.8 us -> none  [body(): gathered = lax.all_gather(projector_tiles, 'band', axis=0, tiled=True)]
    slice x51 -> x6, local copies, waits for them, and re-layouts: 35.3 us -> 0.17 us  [the longest x1 0.13 us: body(): shared[576:588].reshape(3, 4) / NB]
    all_to_all x0 -> x3, waiting for transfers between devices: none -> 34.2 us  [the longest x1 22.1 us: body(): lax.all_to_all(jnp.broadcast_to(own_pair[None], (PRJ, 2) + plane_shape),...]
    pallas_call x0 -> x10, Pallas kernels: none -> 30.3 us  [call(): pl.pallas_call(kernel, out_shape=shapes, in_specs=specs, out_specs=[VMEM]...]
    another operation x81 -> x4, other arithmetic: 29.6 us -> 0.12 us  [the longest x1 0.07 us: body(): jnp.stack([jnp.where(lower, 0.0, 1.0), jnp.where(lower, -1.0, 1.0)])]
  transfers between devices with their start and end apart: 33 -> 16, of which waited for: 1 -> 10; matrix products, arithmetic and copies ran while one was open for 21% -> 5% of each run, Pallas kernels for 0% -> 7%
where the time goes in v1:
time: 161 us; the launch traced here: 160 us
  waiting for transfers between devices  52.7 us (33%)
  starting transfers between devices  41.6 us (26%)
  Pallas kernels  30.3 us (19%)
  blocking collectives  13.6 us (8%)
  local copies, waits for them, and re-layouts  11.8 us (7%)
  other arithmetic  9.04 us (6%)
    pallas_call x10, Pallas kernels, call(): pl.pallas_call(kernel, out_shape=shapes, in_specs=specs, out_specs=[VMEM]...  30.3 us
    all_to_all x1, waiting for transfers between devices, body(): lax.all_to_all(jnp.broadcast_to(own_pair[None], (PRJ, 2) + plane_shape),...  22.1 us
    all_to_all x1, blocking collectives, body(): lax.all_to_all(parts, 'band', 0, 0, tiled=True)  13.6 us
    all_to_all x2, waiting for transfers between devices, total(): lax.all_to_all(jnp.broadcast_to(part[None], (16,) + part.shape), 'space',...  12.1 us
    ppermute x4, starting transfers between devices, swap_core(): return lax.ppermute(x, 'space', [(i, i ^ 1) for i in range(16)])  11.6 us
    all_to_all x1, starting transfers between devices, body(): lax.all_to_all(jnp.broadcast_to(own_pair[None], (PRJ, 2) + plane_shape),...  9.32 us
    all_to_all x2, starting transfers between devices, total(): lax.all_to_all(jnp.broadcast_to(part[None], (16,) + part.shape), 'space',...  9.15 us
    ppermute x4, starting transfers between devices, exchange(): lax.ppermute(near, 'space', from_near)  8.07 us
  transfers between devices with their start and end apart: 16, of which 10 were waited for; matrix products, arithmetic and copies ran while one was open for 5% of the time, Pallas kernels for 7%

profile of v1, /device:TPU:1, one launch (start us, length us, event | category | flops | bytes accessed | tf_op | source)
XLA Modules:
  0.0 160.0 jit_solution(11585303588823539518)
XLA Ops:
  1.4 0.8 broadcast_multiply_fusion.2
  2.2 1.2 broadcast_select_fusion.1
  3.4 0.8 pad_maximum_fusion.4
  4.2 3.3 %collective-permute-start = (f32[7,72,128]{2,1,0:T(8,128)S(1)}, f32[7,72,128]{2,1,0:T(8,128)S(1)}, u32[]{:S(2)}, u32[]{:S(2)}) collective-permute-start(f32[7,72,128]{2,1,0:T(8,128)S(1)} %pad_maximum_fusion.4), channel_id=1, source_target_pairs={{0,1},{1,0},{2,3},{3,2},{4,5},{5,4},{6,7},{7,6},{8,9},{9,8},{10,11... | collective-permute-start | bytes 774152 | tf_op jit(solution)/shard_map/ppermute | solution.py:297
  7.7 1.0 collective-permute-done
  8.7 2.3 %collective-permute-done.3.beside_b = f32[72,128]{1,0:T(8,128)S(1)} collective-permute-done((f32[72,128]{1,0:T(8,128)S(1)}, f32[72,128]{1,0:T(8,128)S(1)}, u32[]{:S(2)}, u32[]{:S(2)}) %collective-permute-start.3) | collective-permute-done | bytes 36896 | tf_op jit(solution)/shard_map/ppermute | solution.py:323
  11.2 1.1 broadcast_in_dim.12
  12.3 9.3 %all-to-all-start = ((f32[16,2,72,128]{3,2,1,0:T(8,128)}), f32[16,2,72,128]{3,2,1,0:T(8,128)S(1)}, u32[]{:S(2)}, u32[]{:S(2)}) async-start(f32[16,2,72,128]{3,2,1,0:T(8,128)} %broadcast_in_dim.12), calls=%async_computation | async-start | bytes 2359296 | tf_op jit(solution)/shard_map/all_to_all | solution.py:342
  21.8 0.9 fusion
  22.7 1.2 collective-permute-start.2
  24.1 3.6 %collective-permute-start.1 = (f32[10,72,128]{2,1,0:T(8,128)}, f32[10,72,128]{2,1,0:T(8,128)}, u32[]{:S(2)}, u32[]{:S(2)}) collective-permute-start(f32[10,72,128]{2,1,0:T(8,128)} %get-tuple-element.45), channel_id=1, source_target_pairs={{0,2},{1,15},{2,4},{3,1},{4,6},{5,3},{6,8},{7,5},{8,10},{9,7},{10,... | collective-permute-start | bytes 1105928 | tf_op jit(solution)/shard_map/ppermute | solution.py:337
  27.6 22.1 %all-to-all-done.refs_6_.basis.basis_own = f32[16,2,72,128]{3,2,1,0:T(8,128)S(1)} async-done(((f32[16,2,72,128]{3,2,1,0:T(8,128)}), f32[16,2,72,128]{3,2,1,0:T(8,128)S(1)}, u32[]{:S(2)}, u32[]{:S(2)}) %all-to-all-start) | async-done | bytes 1179680 | tf_op jit(solution)/shard_map/all_to_all | solution.py:342
  49.7 4.7 %collective-permute-start.4 = (f32[16,2,72,128]{3,2,1,0:T(8,128)S(1)}, f32[16,2,72,128]{3,2,1,0:T(8,128)S(1)}, u32[]{:S(2)}, u32[]{:S(2)}) collective-permute-start(f32[16,2,72,128]{3,2,1,0:T(8,128)S(1)} %all-to-all-done.refs_6_.basis.basis_own), channel_id=1, source_target_pairs={{0,1},{1,0},{2,3},{3,2},{4,5},{5,4},{6,7},{7,6},{8,9},{9,8},{10,11... | collective-permute-start | bytes 3538952 | tf_op jit(solution)/shard_map/ppermute | solution.py:297
  54.5 0.9 slice_bitcast_fusion.11
  56.2 5.2 %shard_map.122 = f32[16,128]{1,0:T(8,128)S(1)} custom-call(f32[16,2,72,128]{3,2,1,0:T(8,128)S(1)} %all-to-all-done.refs_6_.basis.basis_own, f32[2,72,128]{2,1,0:T(8,128)S(1)} %pad_maximum_fusion.5.potentials), custom_call_target="tpu_custom_call" | custom-call | tf_op jit(solution)/shard_map/pallas_call | solution.py:103
  61.4 5.8 %shard_map.121 = (f32[2,4,72,128]{3,2,1,0:T(8,128)S(1)}, f32[2,4,72,128]{3,2,1,0:T(8,128)S(1)}, f32[16,128]{1,0:T(8,128)S(1)}) custom-call(f32[10,72,128]{2,1,0:T(8,128)} %collective-permute-done.1.refs_0_, f32[10,72,128]{2,1,0:T(8,128)S(1)} %collective-permute-done.2.refs_1_, f32[2,4,72,128]{3,2,1,0:T(8,128)S(1)} %pad_maximum_fusion.2.refs_2_.center, ...), custom_call_target="tpu_custom_call" | custom-call | tf_op jit(solution)/shard_map/pallas_call | solution.py:103
  67.2 0.7 copy-done.5
  67.9 0.7 copy-done.7
  69.3 4.7 %all-to-all-start.1 = ((f32[16,16,128]{2,1,0:T(8,128)}), f32[16,16,128]{2,1,0:T(8,128)S(1)}, u32[]{:S(2)}, u32[]{:S(2)}) async-start(f32[16,16,128]{2,1,0:T(8,128)} %broadcast_in_dim.13), calls=%async_computation.1 | async-start | bytes 262144 | tf_op jit(solution)/shard_map/all_to_all | solution.py:378
  74.1 5.9 %all-to-all-done.1.received = f32[16,16,128]{2,1,0:T(8,128)S(1)} async-done(((f32[16,16,128]{2,1,0:T(8,128)}), f32[16,16,128]{2,1,0:T(8,128)S(1)}, u32[]{:S(2)}, u32[]{:S(2)}) %all-to-all-start.1) | async-done | bytes 131104 | tf_op jit(solution)/shard_map/all_to_all | solution.py:378
  80.0 1.2 shard_map.123
  81.2 1.0 copy-done.6
  82.2 1.0 copy-done.8
  83.1 2.7 %shard_map.124 = (f32[2,4,72,128]{3,2,1,0:T(8,128)S(1)}, f32[2,4,72,128]{3,2,1,0:T(8,128)S(1)}) custom-call(f32[2]{0:T(128)S(1)} %pad_maximum_fusion.7.flags, f32[2,4,72,128]{3,2,1,0:T(8,128)S(1)} %pad_maximum_fusion.2.refs_2_.center, f32[2,4,72,128]{3,2,1,0:T(8,128)S(1)} %copy-done.6, f32[2,4,72,128]{3,2,1,0:T(8,128)S(1)} %copy-done.8, ...), custom_call_target="tpu_custom_call" | custom-call | tf_op jit(solution)/shard_map/pallas_call | solution.py:103
  85.8 1.1 collective-permute-start.5
  87.4 1.0 multiply_sine_fusion
  88.5 5.2 %collective-permute-done.5.near = f32[8,72,128]{2,1,0:T(8,128)S(1)} collective-permute-done((f32[8,72,128]{2,1,0:T(8,128)S(1)}, f32[8,72,128]{2,1,0:T(8,128)S(1)}, u32[]{:S(2)}, u32[]{:S(2)}) %collective-permute-start.5) | collective-permute-done | bytes 294944 | tf_op jit(solution)/shard_map/ppermute | solution.py:337
  93.7 4.2 %collective-permute-done.6.far = f32[8,72,128]{2,1,0:T(8,128)S(1)} collective-permute-done((f32[8,72,128]{2,1,0:T(8,128)S(1)}, f32[8,72,128]{2,1,0:T(8,128)S(1)}, u32[]{:S(2)}, u32[]{:S(2)}) %collective-permute-start.6) | collective-permute-done | bytes 294944 | tf_op jit(solution)/shard_map/ppermute | solution.py:337
  97.9 2.4 %shard_map.125.refs_2_.center = f32[2,4,72,128]{3,2,1,0:T(8,128)S(1)} custom-call(f32[2]{0:T(128)S(1)} %pad_maximum_fusion.7.flags, f32[8,72,128]{2,1,0:T(8,128)S(1)} %collective-permute-done.5.near, f32[8,72,128]{2,1,0:T(8,128)S(1)} %collective-permute-done.6.far, f32[2,4,72,128]{3,2,1,0:T(8,128)S(1)} %get-tuple-element.20.center, ...), custom_call_target="tpu_custom_call" | custom-call | tf_op jit(solution)/shard_map/pallas_call | solution.py:103
  100.3 1.5 collective-permute-start.8
  102.4 3.1 %collective-permute-start.12 = (f32[4,72,128]{2,1,0:T(8,128)}, f32[4,72,128]{2,1,0:T(8,128)}, u32[]{:S(2)}, u32[]{:S(2)}) collective-permute-start(f32[4,72,128]{2,1,0:T(8,128)} %slice_bitcast_fusion), channel_id=1, source_target_pairs={{0,1},{1,0},{2,3},{3,2},{4,5},{5,4},{6,7},{7,6},{8,9},{9,8},{10,11... | collective-permute-start | bytes 442376 | tf_op jit(solution)/shard_map/ppermute | solution.py:297
  105.5 2.9 %collective-permute-done.7.refs_0_ = f32[8,72,128]{2,1,0:T(8,128)S(1)} collective-permute-done((f32[8,72,128]{2,1,0:T(8,128)S(1)}, f32[8,72,128]{2,1,0:T(8,128)S(1)}, u32[]{:S(2)}, u32[]{:S(2)}) %collective-permute-start.7) | collective-permute-done | bytes 294944 | tf_op jit(solution)/shard_map/ppermute | solution.py:337
  108.4 2.4 %collective-permute-done.8.refs_1_ = f32[8,72,128]{2,1,0:T(8,128)S(1)} collective-permute-done((f32[8,72,128]{2,1,0:T(8,128)S(1)}, f32[8,72,128]{2,1,0:T(8,128)S(1)}, u32[]{:S(2)}, u32[]{:S(2)}) %collective-permute-start.8) | collective-permute-done | bytes 294944 | tf_op jit(solution)/shard_map/ppermute | solution.py:337
  110.9 5.6 %shard_map.126 = (f32[2,4,72,128]{3,2,1,0:T(8,128)S(1)}, f32[2,4,72,128]{3,2,1,0:T(8,128)S(1)}, f32[32,128]{1,0:T(8,128)S(1)}) custom-call(f32[8,72,128]{2,1,0:T(8,128)S(1)} %collective-permute-done.7.refs_0_, f32[8,72,128]{2,1,0:T(8,128)S(1)} %collective-permute-done.8.refs_1_, f32[2,4,72,128]{3,2,1,0:T(8,128)S(1)} %shard_map.125.refs_2_.center, ...), custom_call_target="tpu_custom_call" | custom-call | tf_op jit(solution)/shard_map/pallas_call | solution.py:103
  116.4 0.7 copy-done.1
  117.1 0.7 copy-done.3
  117.8 0.7 broadcast_in_dim.15
  118.6 4.5 %all-to-all-start.2 = ((f32[16,32,128]{2,1,0:T(8,128)}), f32[16,32,128]{2,1,0:T(8,128)S(1)}, u32[]{:S(2)}, u32[]{:S(2)}) async-start(f32[16,32,128]{2,1,0:T(8,128)} %broadcast_in_dim.15), calls=%async_computation.2 | async-start | bytes 524288 | tf_op jit(solution)/shard_map/all_to_all | solution.py:378
  123.0 0.9 fusion.4
  124.1 6.2 %all-to-all-done.2.received = f32[16,32,128]{2,1,0:T(8,128)S(1)} async-done(((f32[16,32,128]{2,1,0:T(8,128)}), f32[16,32,128]{2,1,0:T(8,128)S(1)}, u32[]{:S(2)}, u32[]{:S(2)}) %all-to-all-start.2) | async-done | bytes 262176 | tf_op jit(solution)/shard_map/all_to_all | solution.py:378
  130.3 1.1 shard_map.127.table
  131.5 3.4 %shard_map.128 = (f32[2,4,72,128]{3,2,1,0:T(8,128)}, f32[2,4,72,128]{3,2,1,0:T(8,128)S(1)}) custom-call(f32[2]{0:T(128)S(1)} %pad_maximum_fusion.7.flags, f32[2,4,72,128]{3,2,1,0:T(8,128)S(1)} %shard_map.125.refs_2_.center, f32[2,4,72,128]{3,2,1,0:T(8,128)S(1)} %copy-done.2, f32[2,4,72,128]{3,2,1,0:T(8,128)S(1)} %copy-done.4, ...), custom_call_target="tpu_custom_call" | custom-call | tf_op jit(solution)/shard_map/pallas_call | solution.py:103
  134.9 0.7 copy-done.9
  135.9 3.3 %collective-permute-start.9 = (f32[8,72,128]{2,1,0:T(8,128)}, f32[8,72,128]{2,1,0:T(8,128)S(1)}, u32[]{:S(2)}, u32[]{:S(2)}) collective-permute-start(f32[8,72,128]{2,1,0:T(8,128)} %bitcast.30), channel_id=1, source_target_pairs={{0,2},{1,15},{2,4},{3,1},{4,6},{5,3},{6,8},{7,5},{8,10},{9,7},{10,... | collective-permute-start | bytes 884744 | tf_op jit(solution)/shard_map/ppermute | solution.py:337
  139.6 13.6 %all_to_all.20 = f32[16,8,128]{2,1,0:T(8,128)S(1)} all-to-all(f32[16,8,128]{2,1,0:T(8,128)S(1)} %bitcast.93), channel_id=1, replica_groups=mesh['band'=16,'space'=16] {'band'}, dimensions={0} | all-to-all | bytes 131072 | tf_op jit(solution)/shard_map/all_to_all | solution.py:439
  153.9 1.0 copy-done.10
  154.9 2.8 %shard_map.129 = f32[2,4,72,128]{3,2,1,0:T(8,128)S(1)} custom-call(f32[2]{0:T(128)S(1)} %pad_maximum_fusion.7.flags, f32[8,72,128]{2,1,0:T(8,128)S(1)} %collective-permute-done.9.near, f32[8,72,128]{2,1,0:T(8,128)S(1)} %collective-permute-done.10.far, f32[2,4,72,128]{3,2,1,0:T(8,128)} %get-tuple-element.26.center, ...), custom_call_target="tpu_custom_call" | custom-call | tf_op jit(solution)/shard_map/pallas_call | solution.py:103
  159.2 0.7 fusion.1
  (83 shorter events, 7.2 us)
Async XLA Ops:
  0.6 10.4 %copy-start = (f32[8,72,128]{2,1,0:T(8,128)S(1)}, f32[8,72,128]{2,1,0:T(8,128)}, u32[]{:S(2)}) copy-start(f32[8,72,128]{2,1,0:T(8,128)} %constant.87.clone.masks.refs_5_) | copy-start | bytes 884740
  0.6 6.9 %copy-start.14 = (f32[1,1,9216]{2,1,0:T(1,128)S(1)}, f32[1,1,9216]{2,1,0:T(1,128)}, u32[]{:S(2)}) copy-start(f32[1,1,9216]{2,1,0:T(1,128)} %param.13) | copy-start | bytes 110596
  4.2 4.5 %collective-permute-start = (f32[7,72,128]{2,1,0:T(8,128)S(1)}, f32[7,72,128]{2,1,0:T(8,128)S(1)}, u32[]{:S(2)}, u32[]{:S(2)}) collective-permute-start(f32[7,72,128]{2,1,0:T(8,128)S(1)} %pad_maximum_fusion.4), channel_id=1, source_target_pairs={{0,1},{1,0},{2,3},{3,2},{4,5},{5,4},{6,7},{7,6},{8,9},{9,8},{10,11... | collective-permute-start | bytes 774152 | tf_op jit(solution)/shard_map/ppermute | solution.py:297
  7.6 3.4 %collective-permute-start.3 = (f32[72,128]{1,0:T(8,128)S(1)}, f32[72,128]{1,0:T(8,128)S(1)}, u32[]{:S(2)}, u32[]{:S(2)}) collective-permute-start(f32[72,128]{1,0:T(8,128)S(1)} %broadcast_multiply_fusion.1.beta), channel_id=1, source_target_pairs={{0,15},{1,2},{2,1},{3,4},{4,3},{5,6},{6,5},{7,8},{8,7},{9,10},{10,... | collective-permute-start | bytes 110600 | tf_op jit(solution)/shard_map/ppermute | solution.py:323
  12.3 9.4 %copy-start.15 = (s32[3,4]{1,0:T(4,128)S(1)}, s32[3,4]{1,0:T(4,128)}, u32[]{:S(2)}) copy-start(s32[3,4]{1,0:T(4,128)} %param.16) | copy-start | bytes 148
  12.3 9.5 %copy-start.11 = (f32[1,9216]{1,0:T(1,128)S(1)}, f32[1,9216]{1,0:T(1,128)}, u32[]{:S(2)}) copy-start(f32[1,9216]{1,0:T(1,128)} %param.12) | copy-start | bytes 110596
  12.3 9.5 %copy-start.12 = (f32[1,9216]{1,0:T(1,128)S(1)}, f32[1,9216]{1,0:T(1,128)}, u32[]{:S(2)}) copy-start(f32[1,9216]{1,0:T(1,128)} %param.11) | copy-start | bytes 110596
  12.3 37.4 %all-to-all-start = ((f32[16,2,72,128]{3,2,1,0:T(8,128)}), f32[16,2,72,128]{3,2,1,0:T(8,128)S(1)}, u32[]{:S(2)}, u32[]{:S(2)}) async-start(f32[16,2,72,128]{3,2,1,0:T(8,128)} %broadcast_in_dim.12), calls=%async_computation | async-start | bytes 2359296 | tf_op jit(solution)/shard_map/all_to_all | solution.py:342
  21.6 32.8 %copy-start.16 = (f32[16]{0:T(128)S(1)}, f32[16]{0:T(128)}, u32[]{:S(2)}) copy-start(f32[16]{0:T(128)} %param.15) | copy-start | bytes 196
  22.7 31.8 %collective-permute-start.2 = (f32[10,72,128]{2,1,0:T(8,128)}, f32[10,72,128]{2,1,0:T(8,128)S(1)}, u32[]{:S(2)}, u32[]{:S(2)}) collective-permute-start(f32[10,72,128]{2,1,0:T(8,128)} %get-tuple-element.44), channel_id=1, source_target_pairs={{2,0},{15,1},{4,2},{1,3},{6,4},{3,5},{8,6},{5,7},{10,8},{7,9},{12,... | collective-permute-start | bytes 1105928 | tf_op jit(solution)/shard_map/ppermute | solution.py:337
  24.1 30.5 %collective-permute-start.1 = (f32[10,72,128]{2,1,0:T(8,128)}, f32[10,72,128]{2,1,0:T(8,128)}, u32[]{:S(2)}, u32[]{:S(2)}) collective-permute-start(f32[10,72,128]{2,1,0:T(8,128)} %get-tuple-element.45), channel_id=1, source_target_pairs={{0,2},{1,15},{2,4},{3,1},{4,6},{5,3},{6,8},{7,5},{8,10},{9,7},{10,... | collective-permute-start | bytes 1105928 | tf_op jit(solution)/shard_map/ppermute | solution.py:337
  49.7 11.6 %collective-permute-start.4 = (f32[16,2,72,128]{3,2,1,0:T(8,128)S(1)}, f32[16,2,72,128]{3,2,1,0:T(8,128)S(1)}, u32[]{:S(2)}, u32[]{:S(2)}) collective-permute-start(f32[16,2,72,128]{3,2,1,0:T(8,128)S(1)} %all-to-all-done.refs_6_.basis.basis_own), channel_id=1, source_target_pairs={{0,1},{1,0},{2,3},{3,2},{4,5},{5,4},{6,7},{7,6},{8,9},{9,8},{10,11... | collective-permute-start | bytes 3538952 | tf_op jit(solution)/shard_map/ppermute | solution.py:297
  67.2 0.7 copy-start.5
  67.9 0.7 copy-start.7
  69.3 10.8 %all-to-all-start.1 = ((f32[16,16,128]{2,1,0:T(8,128)}), f32[16,16,128]{2,1,0:T(8,128)S(1)}, u32[]{:S(2)}, u32[]{:S(2)}) async-start(f32[16,16,128]{2,1,0:T(8,128)} %broadcast_in_dim.13), calls=%async_computation.1 | async-start | bytes 262144 | tf_op jit(solution)/shard_map/all_to_all | solution.py:378
  81.2 1.0 copy-start.6
  82.2 1.0 copy-start.8
  85.8 7.8 %collective-permute-start.5 = (f32[8,72,128]{2,1,0:T(8,128)S(1)}, f32[8,72,128]{2,1,0:T(8,128)S(1)}, u32[]{:S(2)}, u32[]{:S(2)}) collective-permute-start(f32[8,72,128]{2,1,0:T(8,128)S(1)} %bitcast.81), channel_id=1, source_target_pairs={{0,2},{1,15},{2,4},{3,1},{4,6},{5,3},{6,8},{7,5},{8,10},{9,7},{10,... | collective-permute-start | bytes 884744 | tf_op jit(solution)/shard_map/ppermute | solution.py:337
  87.0 10.9 %collective-permute-start.6 = (f32[8,72,128]{2,1,0:T(8,128)S(1)}, f32[8,72,128]{2,1,0:T(8,128)S(1)}, u32[]{:S(2)}, u32[]{:S(2)}) collective-permute-start(f32[8,72,128]{2,1,0:T(8,128)S(1)} %bitcast.82), channel_id=1, source_target_pairs={{2,0},{15,1},{4,2},{1,3},{6,4},{3,5},{8,6},{5,7},{10,8},{7,9},{12,... | collective-permute-start | bytes 884744 | tf_op jit(solution)/shard_map/ppermute | solution.py:337
  88.5 17.1 %copy-start.13 = (f32[1,4,72,128]{3,2,1,0:T(8,128)S(1)}, f32[1,4,72,128]{3,2,1,0:T(8,128)}, u32[]{:S(2)}) copy-start(f32[1,4,72,128]{3,2,1,0:T(8,128)} %get-tuple-element.42) | copy-start | bytes 442372
  100.2 8.2 %collective-permute-start.7 = (f32[8,72,128]{2,1,0:T(8,128)S(1)}, f32[8,72,128]{2,1,0:T(8,128)S(1)}, u32[]{:S(2)}, u32[]{:S(2)}) collective-permute-start(f32[8,72,128]{2,1,0:T(8,128)S(1)} %bitcast.78), channel_id=1, source_target_pairs={{0,2},{1,15},{2,4},{3,1},{4,6},{5,3},{6,8},{7,5},{8,10},{9,7},{10,... | collective-permute-start | bytes 884744 | tf_op jit(solution)/shard_map/ppermute | solution.py:337
  100.3 10.5 %collective-permute-start.8 = (f32[8,72,128]{2,1,0:T(8,128)S(1)}, f32[8,72,128]{2,1,0:T(8,128)S(1)}, u32[]{:S(2)}, u32[]{:S(2)}) collective-permute-start(f32[8,72,128]{2,1,0:T(8,128)S(1)} %bitcast.79), channel_id=1, source_target_pairs={{2,0},{15,1},{4,2},{1,3},{6,4},{3,5},{8,6},{5,7},{10,8},{7,9},{12,... | collective-permute-start | bytes 884744 | tf_op jit(solution)/shard_map/ppermute | solution.py:337
  102.4 20.6 %collective-permute-start.12 = (f32[4,72,128]{2,1,0:T(8,128)}, f32[4,72,128]{2,1,0:T(8,128)}, u32[]{:S(2)}, u32[]{:S(2)}) collective-permute-start(f32[4,72,128]{2,1,0:T(8,128)} %slice_bitcast_fusion), channel_id=1, source_target_pairs={{0,1},{1,0},{2,3},{3,2},{4,5},{5,4},{6,7},{7,6},{8,9},{9,8},{10,11... | collective-permute-start | bytes 442376 | tf_op jit(solution)/shard_map/ppermute | solution.py:297
  116.4 0.7 copy-start.1
  117.1 0.7 copy-start.3
  118.6 11.7 %all-to-all-start.2 = ((f32[16,32,128]{2,1,0:T(8,128)}), f32[16,32,128]{2,1,0:T(8,128)S(1)}, u32[]{:S(2)}, u32[]{:S(2)}) async-start(f32[16,32,128]{2,1,0:T(8,128)} %broadcast_in_dim.15), calls=%async_computation.2 | async-start | bytes 524288 | tf_op jit(solution)/shard_map/all_to_all | solution.py:378
  130.3 1.2 copy-start.2
  130.3 1.2 copy-start.4
  134.9 0.7 copy-start.9
  135.6 18.3 %collective-permute-start.10 = (f32[8,72,128]{2,1,0:T(8,128)}, f32[8,72,128]{2,1,0:T(8,128)S(1)}, u32[]{:S(2)}, u32[]{:S(2)}) collective-permute-start(f32[8,72,128]{2,1,0:T(8,128)} %bitcast.30), channel_id=1, source_target_pairs={{2,0},{15,1},{4,2},{1,3},{6,4},{3,5},{8,6},{5,7},{10,8},{7,9},{12,... | collective-permute-start | bytes 884744 | tf_op jit(solution)/shard_map/ppermute | solution.py:337
  135.9 18.0 %collective-permute-start.9 = (f32[8,72,128]{2,1,0:T(8,128)}, f32[8,72,128]{2,1,0:T(8,128)S(1)}, u32[]{:S(2)}, u32[]{:S(2)}) collective-permute-start(f32[8,72,128]{2,1,0:T(8,128)} %bitcast.30), channel_id=1, source_target_pairs={{0,2},{1,15},{2,4},{3,1},{4,6},{5,3},{6,8},{7,5},{8,10},{9,7},{10,... | collective-permute-start | bytes 884744 | tf_op jit(solution)/shard_map/ppermute | solution.py:337
  153.9 1.0 copy-start.10
  157.7 1.5 collective-permute-start.11

commit v2 on v1

v2 whole, which is shorter than its diff:
```python
import functools
import math

import jax
import jax.numpy as jnp
import numpy as np
from jax import lax
from jax.experimental import pallas as pl
from jax.experimental.pallas import tpu as pltpu
from jax.sharding import PartitionSpec as P

NB = 32
NY = 96
NZ = 96
ROWS = 72
LANES = 128
PRJ = 16
PRJ_ATOM = 4

half_step = 0.025
kinetic_scale = 3.125
highest = lax.Precision.HIGHEST
f32 = jnp.float32

A2 = -(half_step**2) / 2.0
A3 = -(half_step**3) / 6.0
A4 = half_step**4 / 24.0


def columns():
    return (np.arange(ROWS * LANES, dtype=np.int32) % NZ).reshape(ROWS, LANES)


TILES = [slice(8 * t, 8 * t + 8) for t in range(ROWS // 8)]


def next_rows(ref, index, t, x, sub):
    if t < len(TILES) - 1:
        return ref[index + (slice(8 * t + 1, 8 * t + 9),)]
    wrapped = jnp.broadcast_to(ref[index + (slice(0, 1),)], (8, LANES))
    return jnp.where(sub == 7, wrapped, pltpu.roll(x, 7, 0))


def previous_rows(ref, index, t, x, sub):
    if t > 0:
        return ref[index + (slice(8 * t - 1, 8 * t + 7),)]
    wrapped = jnp.broadcast_to(ref[index + (slice(ROWS - 1, ROWS),)], (8, LANES))
    return jnp.where(sub == 0, wrapped, pltpu.roll(x, 1, 0))


def kinetic_plane(ref, index, column, beside, store, scratch):
    lane = lax.broadcasted_iota(jnp.int32, (8, LANES), 1)
    sub = lax.broadcasted_iota(jnp.int32, (8, LANES), 0)
    for t, rows in enumerate(TILES):
        x = ref[index + (rows,)]
        after, before = next_rows(ref, index, t, x, sub), previous_rows(ref, index, t, x, sub)
        up = pltpu.roll(jnp.where(lane >= 96, x, after), 32, 1)
        down = pltpu.roll(jnp.where(lane < 32, x, before), 96, 1)
        place = column[rows]
        scratch[0, rows] = up + down
        scratch[1, rows] = jnp.where(place == 0, down, x)
        scratch[2, rows] = jnp.where(place == NZ - 1, up, x)
    for t, rows in enumerate(TILES):
        ahead, behind = scratch[1, rows], scratch[2, rows]
        after = next_rows(scratch, (1,), t, ahead, sub)
        before = previous_rows(scratch, (2,), t, behind, sub)
        up = pltpu.roll(jnp.where(lane >= 1, ahead, after), 127, 1)
        down = pltpu.roll(jnp.where(lane < 127, behind, before), 1, 1)
        around = scratch[0, rows] + (up + down)
        x = ref[index + (rows,)]
        store(rows, x, kinetic_scale * (6.0 * x - around - beside(rows)))


def fold(x):
    return jnp.sum(x.reshape(ROWS // 8, 8, LANES), axis=0)


def rows8(parts):
    sub = lax.broadcasted_iota(jnp.int32, (8, LANES), 0)
    low = sub < 4
    parts = [
        jnp.where(low, a, b) + pltpu.roll(jnp.where(low, b, a), 4, 0)
        for a, b in zip(parts[:4], parts[4:])
    ]
    for step in (2, 1):
        first = (sub & step) == 0
        parts = [
            jnp.where(first, a + pltpu.roll(a, 8 - step, 0), b + pltpu.roll(b, step, 0))
            for a, b in zip(parts[:step], parts[step:])
        ]
    return parts[0]


def params(mib):
    return pltpu.CompilerParams(vmem_limit_bytes=mib * 2**20)


VMEM = pl.BlockSpec(memory_space=pltpu.VMEM)
SMEM = pl.BlockSpec(memory_space=pltpu.SMEM)


def call(kernel, outs, args, scratch=(), scalars=0, mib=8, cost=None):
    specs = [SMEM] * scalars + [VMEM] * (len(args) - scalars)
    single = not isinstance(outs, list)
    shapes = [
        o if hasattr(o, "dtype") else jax.ShapeDtypeStruct(o, f32)
        for o in ([outs] if single else outs)
    ]
    result = pl.pallas_call(
        kernel,
        out_shape=shapes,
        in_specs=specs,
        out_specs=[VMEM] * len(shapes),
        scratch_shapes=list(scratch),
        compiler_params=params(mib),
        cost_estimate=cost,
    )(*args)
    return result[0] if single else result


def mask_kernel(atom, values, tile_map, out):
    reach = tile_map[pl.ds(atom[0], 1)].astype(f32)
    row = lax.broadcasted_iota(jnp.int32, (ROWS, ROWS), 0)
    lane = lax.broadcasted_iota(jnp.int32, (ROWS, ROWS), 1)
    wide = jnp.where(row == lane, jnp.broadcast_to(reach, (ROWS, ROWS)), 0.0)
    share(out, values[...] * jnp.sum(wide, axis=1, keepdims=True))


def give_kernel(flags, psi, adjoint, now, later, kept, message, own):
    lower = flags[0] < 0.5
    for q in range(4):
        a, b = psi[q], adjoint[q]
        kept[q] = jnp.where(lower, a, b)
        message[q] = jnp.where(lower, b, a)
    own[0] = now[...]
    own[1] = later[...]
    message[4] = now[...]
    message[5] = later[...]


def pack_kernel(kept, own, other, near, far, center):
    center[0] = kept[...]
    center[1] = other[0:4]
    near[0:4] = kept[...]
    near[4:10] = other[...]
    far[0:4] = kept[...]
    far[4:8] = other[0:4]
    far[8:10] = own[...]


def kinetic_kernel(basis, basis_other, basis_near, column, out, work):
    def projector(pair, carry):
        for k in range(2):
            j = 2 * pair + k

            def store(rows, x, kinetic):
                out[j, rows] = kinetic

            def beside(rows):
                return basis_other[j, rows] + basis_near[j, rows]

            kinetic_plane(basis, (j,), column, beside, store, work.at[k])
        return carry

    lax.fori_loop(0, PRJ // 2, projector, 0)


def two_steps(near, far, center, potential, column, first, edge, second, work):
    def local(source, index, beside, v, out, place, k):
        def store(rows, x, kinetic):
            out[place + (rows,)] = kinetic + v[rows] * x

        kinetic_plane(source, index, column, beside, store, work.at[k])

    def row(q, carry):
        own, other = (0, q), (1, q)
        local(
            center, own, lambda r: near[4 + q, r] + center[1, q, r], potential.at[0], first, own, 0
        )
        local(center, other, lambda r: center[0, q, r] + far[q, r], potential.at[1], first, other, 1)
        local(
            near, (4 + q,), lambda r: near[q, r] + center[0, q, r], potential.at[2], edge, own, 2
        )
        local(
            far, (q,), lambda r: center[1, q, r] + far[4 + q, r], potential.at[3], edge, other, 3
        )
        local(first, own, lambda r: edge[0, q, r] + first[1, q, r], potential.at[0], second, own, 0)
        local(
            first, other, lambda r: first[0, q, r] + edge[1, q, r], potential.at[1], second, other, 1
        )
        return carry

    lax.fori_loop(0, 4, row, 0)


def spread(parts, lanes):
    total = jnp.concatenate([rows8(parts[k : k + 8]) for k in range(0, len(parts), 8)], 0)
    summed = jnp.sum(total, axis=1, keepdims=True)
    lane = lax.broadcasted_iota(jnp.int32, total.shape, 1)
    return jnp.where(lane == lanes, summed, 0.0)


def start_kernel(flags, near, far, center, own, other, column, first, second, early, late, edge, work):
    lower = flags[0] < 0.5
    pairs = [(own.at[0], own.at[1]), (other.at[4], other.at[5])]
    pairs += [(near.at[8], near.at[9]), (far.at[8], far.at[9])]
    for k, (a, b) in enumerate(pairs):
        a, b = a[...], b[...]
        early[k] = jnp.where(lower, a, b)
        late[k] = jnp.where(lower, b, a)
    two_steps(near, far, center, early, column, first, edge, second, work)


def project(basis, potential, kinds, count):
    def projector(j, total):
        parts = [[None] * 4 for _ in kinds]
        for plane in range(2):
            beta = basis[plane][j]
            wide = None if len(basis) == 2 else basis[2 + plane][j] + potential[plane] * beta
            for k, (field, by) in enumerate(kinds):
                factor = wide if by == "wide" else beta if by is None else by(plane, j, beta)
                for q in range(4):
                    value = fold(field[plane, q] * factor)
                    parts[k][q] = value if plane == 0 else parts[k][q] + value
        flat = [value for part in parts for value in part]
        flat += [jnp.zeros((8, LANES), f32)] * (count - len(flat))
        return total + spread(flat, j)

    return lax.fori_loop(0, PRJ, projector, jnp.zeros((count, LANES), f32))


def share(out, value):
    def copy(k, carry):
        out[k] = value
        return carry

    lax.fori_loop(0, 16, copy, 0)


def split(x):
    high = x.astype(jnp.bfloat16)
    return high, (x - high.astype(f32)).astype(jnp.bfloat16)


def put(target, row, lanes, value, offset):
    high, low = split(value)
    target[row : row + PRJ, lanes] = high
    target[row + offset : row + offset + PRJ, lanes] = low


def flat_rows(ref, s, count):
    return ref[pl.ds(s, count, stride=ROWS)]


def lanes_at(s):
    return pl.ds(pl.multiple_of(s * LANES, LANES), LANES)


def products(a, b):
    return lax.dot_general(a[...], b[...], (((1,), (1,)), ((), ())), preferred_element_type=f32)


def gram_kernel(basis, kinetic, early, late, out, flat):
    def row(s, carry):
        beta, moved = flat_rows(basis, s, PRJ), flat_rows(kinetic, s, PRJ)
        at = lanes_at(s)
        put(flat, 0, at, beta, 64)
        for k, v in enumerate((early, late)):
            put(flat, PRJ * (k + 1), at, moved + v[0, pl.ds(s, 1)] * beta, 64)
        return carry

    for k in (48, 112):
        flat[k : k + PRJ] = jnp.zeros((PRJ, ROWS * LANES), jnp.bfloat16)
    lax.fori_loop(0, ROWS, row, 0, unroll=8)
    both = products(flat, flat)
    both = both[:64] + both[64:]
    both = both + pltpu.roll(both, 64, 1)
    lane = lax.broadcasted_iota(jnp.int32, (PRJ, LANES), 1)
    out[...] = (
        jnp.where((lane >= 16) & (lane < 64), pltpu.roll(both[:16], 16, 1), 0.0)
        + jnp.where((lane >= 64) & (lane < 80), pltpu.roll(both[16:32], 48, 1), 0.0)
        + jnp.where((lane >= 80) & (lane < 96), pltpu.roll(both[32:48], 48, 1), 0.0)
    )


def put_fields(fields, flat):
    def row(s, carry):
        at = lanes_at(s)
        values = [flat_rows(field, s, 8) for field in fields]
        for k in range(0, len(values), 2):
            pair = values[k : k + 2]
            pair = pair if len(pair) == 2 else pair * 2
            put(flat, 8 * k, at, jnp.concatenate(pair, 0), 32)
        return carry

    lax.fori_loop(0, ROWS, row, 0, unroll=8)


def put_basis(own, other, own_k, other_k, potential, flat):
    def row(s, carry):
        at = lanes_at(s)
        for plane, (b, k) in enumerate(((own, own_k), (other, other_k))):
            beta, moved = flat_rows(b, s, PRJ), flat_rows(k, s, PRJ)
            put(flat, 2 * PRJ * plane, at, beta, 64)
            put(flat, 2 * PRJ * plane + PRJ, at, moved + potential[plane, pl.ds(s, 1)] * beta, 64)
        return carry

    lax.fori_loop(0, ROWS, row, 0, unroll=8)


def field_moments(fields_flat, basis_flat, count):
    both = products(fields_flat, basis_flat)
    both = both[:32] + both[32:]
    both = both + pltpu.roll(both, 64, 1)
    result = []
    for k in range(count):
        part = both[8 * k : 8 * k + 8]
        result.append(part + pltpu.roll(pltpu.roll(part, 96, 1), 4, 0))
    return result


def stack_rows(a, b):
    sub = lax.broadcasted_iota(jnp.int32, (8, LANES), 0)
    lane = lax.broadcasted_iota(jnp.int32, (8, LANES), 1)
    return jnp.where(lane < PRJ, jnp.where(sub < 4, a, pltpu.roll(b, 4, 0)), 0.0)


def early_moments_kernel(center, first, second, own, other, out, ahead_flat, fields_flat, basis_flat):
    put_fields((center, first, second), fields_flat)

    def row(s, carry):
        at = lanes_at(s)
        for plane, b in enumerate((own, other)):
            put(basis_flat, 2 * PRJ * plane, at, flat_rows(b, s, PRJ), 64)
        return carry

    for k in (16, 48, 80, 112):
        basis_flat[k : k + PRJ] = jnp.zeros((PRJ, ROWS * LANES), jnp.bfloat16)
    lax.fori_loop(0, ROWS, row, 0, unroll=8)
    found = field_moments(fields_flat, basis_flat, 3)
    out[...] = jnp.concatenate([stack_rows(found[0], found[1]), stack_rows(found[2], 0.0 * found[2])], 0)
    ahead_flat[0:16] = fields_flat[16:32]
    ahead_flat[16:32] = fields_flat[48:64]


def moments_kernel(known, ahead_flat, own, other, own_k, other_k, potential, gram, out, basis_flat):
    def row(s, carry):
        at = lanes_at(s)
        for plane, (b, k) in enumerate(((own, own_k), (other, other_k))):
            wide = flat_rows(k, s, PRJ) + potential[plane, pl.ds(s, 1)] * flat_rows(b, s, PRJ)
            put(basis_flat, PRJ * plane, at, wide, 32)
        return carry

    lax.fori_loop(0, ROWS, row, 0, unroll=8)
    both = products(ahead_flat, basis_flat)
    both = both[:8] + both[16:24]
    both = both[:, :32] + both[:, 32:]
    both = jnp.concatenate([both, jnp.zeros((8, LANES - 32), f32)], 1)
    wide = both + pltpu.roll(pltpu.roll(both, LANES - PRJ, 1), 4, 0)
    moments = jnp.concatenate([known[...][:8], known[...][8:] + stack_rows(0.0 * wide, wide)], 0)
    share(out, moments + gram[...])


def middle_moments_kernel(
    center, potential, own, other, own_k, other_k, wave_x, wave_y, wave_z, out, basis_flat
):
    kinds = [
        (center, None),
        (center, "wide"),
        (center, lambda plane, j, beta: beta * wave_x[plane, j // PRJ_ATOM, 0:1]),
        (center, lambda plane, j, beta: beta * wave_y[j // PRJ_ATOM]),
        (center, lambda plane, j, beta: beta * wave_z[j // PRJ_ATOM]),
    ]
    out[...] = project((own, other, own_k, other_k), potential, kinds, 24)
    flat = [x.reshape(PRJ * ROWS, LANES) for x in (own, other, own_k, other_k)]
    put_basis(*flat, potential, basis_flat)


def second_kernel(
    near, far, center, potential, column, basis_flat, known, first, second, out, edge, work, fields_flat
):
    two_steps(near, far, center, potential, column, first, edge, second, work)
    put_fields([x.reshape(8 * ROWS, LANES) for x in (first, second)], fields_flat)
    found = [pltpu.roll(x, LANES - PRJ, 1) for x in field_moments(fields_flat, basis_flat, 2)]
    value = known[...]
    share(out, jnp.concatenate([value[:8], stack_rows(*found), value[8:]], 0))


def times_i(x):
    row = lax.broadcasted_iota(jnp.int32, (8, LANES), 0)
    return jnp.where(row < 2, -pltpu.roll(x, 6, 0), pltpu.roll(x, 2, 0))


def coefficients(later, flags, received, strengths, gram):
    upper, sign = flags[0], flags[1]
    sums = []
    for core in range(2):
        acc = received[core]
        for k in range(core + 2, 16, 2):
            acc = acc + received[k]
        sums.append(acc)
    mine = jnp.where(upper > 0.5, sums[1], sums[0])[:PRJ]
    lane = lax.broadcasted_iota(jnp.int32, (PRJ, LANES), 1)
    valid = lane < PRJ
    if later:
        grams = gram[...]
    else:
        theirs = jnp.where(upper > 0.5, sums[0], sums[1])[:PRJ]
        turned = jnp.where(
            (lane >= 48) & (lane < 64) | (lane >= 80),
            pltpu.roll(theirs, PRJ, 1),
            pltpu.roll(theirs, LANES - PRJ, 1),
        )
        grams = mine + jnp.where(lane < 32, theirs, turned)
        gram[...] = grams

    def block(k):
        return jnp.where(valid, pltpu.roll(grams, LANES - PRJ * (k + 1), 1), 0.0)

    g0 = block(0)
    g1, g2 = (block(2), block(4)) if later else (block(1), block(3))
    weight = strengths[...]

    def moment(k):
        rolled = mine if k == 0 else pltpu.roll(mine, PRJ - 4 * k, 0)
        return jnp.where(valid, rolled, 0.0)[:8]

    def apply(c, g):
        return jnp.dot(c[:, :PRJ], g, precision=highest, preferred_element_type=f32)

    c0 = weight * moment(0)
    c1 = weight * (moment(1) + apply(c0, g0))
    c2 = weight * (moment(2) + apply(c0, g1) + apply(c1, g0))
    c3 = weight * (moment(3) + apply(c0, g2) + apply(c1, g1) + apply(c2, g0))
    e0 = times_i((sign * half_step) * c0 + (sign * A3) * c2) + A2 * c1 + A4 * c3
    e1 = A2 * c0 + A4 * c2
    return c0, c1, e0, e1


def spread_table(table, sets):
    row = lax.broadcasted_iota(jnp.int32, (PRJ, LANES), 0)
    lane = lax.broadcasted_iota(jnp.int32, (PRJ, LANES), 1)
    for k, c in enumerate(sets):
        for q in range(4):
            wide = jnp.broadcast_to(c[q : q + 1], (PRJ, LANES))
            column = jnp.sum(jnp.where(row == lane, wide, 0.0), axis=1, keepdims=True)
            for j in range(PRJ):
                table[j, k, q] = jnp.broadcast_to(column[j : j + 1], (8, LANES))


def combine(out, start, basis, potential, table):
    def tile(i, carry):
        rows = pl.ds(pl.multiple_of(i * 8, 8), 8)
        for plane in range(2):
            v = potential[plane, rows]
            total = start(plane, rows)
            for j in range(PRJ):
                beta = basis[plane][j, rows]
                wide = basis[2 + plane][j, rows] + v * beta
                for q in range(4):
                    total[q] = total[q] + table[j, 0, q] * wide + table[j, 1, q] * beta
            for q in range(4):
                out[plane, q, rows] = total[q]
        return carry

    lax.fori_loop(0, ROWS // 8, tile, 0)


def advance_kernel(later, flags, received, strengths, second, own, other, own_k, other_k, potential, *refs):
    if later:
        gram, out, rest, table = refs
    else:
        out, rest, gram, table = refs
    c0, c1, e0, e1 = coefficients(later, flags, received, strengths, gram)
    rest[0] = e1
    rest[1] = e0
    spread_table(table, (c0, c1))

    def start(plane, rows):
        return [second[plane, q, rows] for q in range(4)]

    combine(out, start, (own, other, own_k, other_k), potential, table)


def partial_kernel(flags, center, first, second, own, other, own_k, other_k, potential, rest, out, table):
    sign = flags[1]
    spread_table(table, (rest[0], rest[1]))

    def start(plane, rows):
        moved = [first[plane, q, rows] for q in range(4)]
        mixed = [-moved[2], -moved[3], moved[0], moved[1]]
        return [
            center[plane, q, rows] + (sign * half_step) * mixed[q] + A2 * second[plane, q, rows]
            for q in range(4)
        ]

    combine(out, start, (own, other, own_k, other_k), potential, table)


def last_kernel(flags, near, far, center, potential, column, partial, out, first, edge, second, work):
    two_steps(near, far, center, potential, column, first, edge, second, work)
    sign = flags[1]
    for plane in range(2):
        for q in range(4):
            mixed = -first[plane, q + 2] if q < 2 else first[plane, q - 2]
            out[plane, q] = partial[plane, q] + (sign * A3) * mixed + A4 * second[plane, q]


def payload_kernel(flags, mine, yours, received, strengths, out):
    turned = [mine[0, q] * yours[q + 2] - mine[0, q + 2] * yours[q] for q in range(2)]
    density = (-2.0 * half_step * flags[1]) * (turned[0] + turned[1])
    sums = []
    for core in range(2):
        acc = received[core]
        for k in range(core + 2, 16, 2):
            acc = acc + received[k]
        sums.append(acc)
    forces = []
    for q in range(3):
        rows = slice(16 + 4 * q, 20 + 4 * q)
        products = sums[0][:4] * sums[1][rows] + sums[1][:4] * sums[0][rows]
        forces.append(strengths[...] * jnp.sum(products, axis=0, keepdims=True))
    for k in range(16):
        first = 9 * k // 2
        out[k] = jnp.concatenate([density[first : first + 5]] + forces, 0)


def outcome_kernel(odd, received, density, forces):
    total = received[0]
    for k in range(1, 16):
        total = total + received[k]
    lane = lax.broadcasted_iota(jnp.int32, (1, LANES), 1)
    moved = pltpu.roll(total, 64, 1)
    for k in range(5):
        start = total[k : k + 1]
        shifted = jnp.where(lane < 64, moved[k : k + 1], moved[min(k + 1, 4) : min(k + 1, 4) + 1])
        row = jnp.where(odd[0] > 0, shifted, start)
        width = min(LANES, 576 - k * LANES)
        density[:, k * LANES : k * LANES + width] = row[:, :width]
    atom = lax.broadcasted_iota(jnp.int32, (3, LANES), 1) // PRJ_ATOM
    column = lax.broadcasted_iota(jnp.int32, (3, 4), 1)
    result = jnp.zeros((3, 4), f32)
    for a in range(4):
        part = jnp.sum(jnp.where(atom == a, total[5:8], 0.0), axis=1, keepdims=True)
        result = jnp.where(column == a, part * (1.0 / NB), result)
    forces[...] = result


def swap_core(x):
    return lax.ppermute(x, "space", [(i, i ^ 1) for i in range(16)])


def fence(*values):
    return lax.optimization_barrier(values)


def body(
    psi_start,
    adjoint_end,
    potential_now,
    potential_next,
    projector_tiles,
    tile_map,
    strengths,
    positions,
):
    space, band = lax.axis_index("space"), lax.axis_index("band")
    lower = (space % 2) == 0
    column = jnp.asarray(columns())
    plane_shape = (ROWS, LANES)
    fields_shape = (2, 4) + plane_shape
    rows_shape = (PRJ,) + plane_shape
    flags = jnp.stack([jnp.where(lower, 0.0, 1.0), jnp.where(lower, -1.0, 1.0)]).astype(f32)
    atom = (band // PRJ_ATOM).astype(jnp.int32).reshape(1)
    odd = (band % 2).astype(jnp.int32).reshape(1)

    payload = call(
        mask_kernel,
        rows_shape,
        [atom, projector_tiles.reshape(plane_shape), tile_map.reshape(4, ROWS)],
        scalars=1,
    )
    basis_own = lax.all_to_all(payload, "band", 0, 0, tiled=True)

    kept, given, own = call(
        give_kernel,
        [(4,) + plane_shape, (6,) + plane_shape, (2,) + plane_shape],
        [
            flags,
            psi_start.reshape((4,) + plane_shape),
            adjoint_end.reshape((4,) + plane_shape),
            potential_now.reshape(plane_shape),
            potential_next.reshape(plane_shape),
        ],
        scalars=1,
    )
    other = swap_core(given)
    near_message, far_message, center = call(
        pack_kernel,
        [(10,) + plane_shape, (10,) + plane_shape, fields_shape],
        [kept, own, other],
    )

    from_near = [(i, (i + 2) % 16 if i % 2 == 0 else (i - 2) % 16) for i in range(16)]
    from_far = [(j, i) for i, j in from_near]
    beside = [(i, (i + 1) % 16 if i % 2 else (i - 1) % 16) for i in range(16)]

    def exchange(fields):
        flat = fields.reshape((8,) + plane_shape)
        return (lax.ppermute(flat, "space", from_near), lax.ppermute(flat, "space", from_far))

    near = lax.ppermute(near_message, "space", from_near)
    far = lax.ppermute(far_message, "space", from_far)

    basis_own, near, far, strengths, positions = fence(
        basis_own, near, far, strengths, positions
    )
    basis_near = lax.ppermute(basis_own, "space", beside)
    basis_other = swap_core(basis_own)

    field_scratch = pltpu.VMEM(fields_shape, f32)
    work_scratch = pltpu.VMEM((4, 3) + plane_shape, f32)
    first, second, early, late = call(
        start_kernel,
        [fields_shape, fields_shape, (4,) + plane_shape, (4,) + plane_shape],
        [flags, near, far, center, own, other, column],
        scratch=[field_scratch, work_scratch],
        scalars=1,
    )
    flat_shape = (PRJ * ROWS, LANES)
    fields_flat = (8 * ROWS, LANES)
    known, ahead_flat = call(
        early_moments_kernel,
        [(16, LANES), jax.ShapeDtypeStruct((32, ROWS * LANES), jnp.bfloat16)],
        [x.reshape(fields_flat) for x in (center, first, second)]
        + [x.reshape(flat_shape) for x in (basis_own, basis_other)],
        scratch=[
            pltpu.VMEM((64, ROWS * LANES), jnp.bfloat16),
            pltpu.VMEM((128, ROWS * LANES), jnp.bfloat16),
        ],
        mib=12,
    )
    basis_near, first, second, early, late, known = fence(
        basis_near, first, second, early, late, known
    )
    kinetic_own = call(
        kinetic_kernel,
        rows_shape,
        [basis_own, basis_other, basis_near, column],
        scratch=[work_scratch],
    )
    kinetic_other = swap_core(kinetic_own)
    gram_part = call(
        gram_kernel,
        (PRJ, LANES),
        [basis_own.reshape(flat_shape), kinetic_own.reshape(flat_shape), early, late],
        scratch=[pltpu.VMEM((128, ROWS * LANES), jnp.bfloat16)],
        mib=12,
    )
    kinetic_other, gram_part = fence(kinetic_other, gram_part)
    basis = [basis_own, basis_other, kinetic_own, kinetic_other]
    part = call(
        moments_kernel,
        (16, 16, LANES),
        [known, ahead_flat] + [x.reshape(flat_shape) for x in basis] + [early, gram_part],
        scratch=[pltpu.VMEM((64, ROWS * LANES), jnp.bfloat16)],
        mib=12,
    )

    table_scratch = pltpu.VMEM((PRJ, 2, 4, 8, LANES), f32)
    rest_shape = (2, 8, LANES)
    received = lax.all_to_all(part, "space", 0, 0, tiled=True)
    received, strengths, positions, space, first, second, early, late, center = fence(
        received, strengths, positions, space, first, second, early, late, center
    )
    plane = space + jnp.stack([jnp.int32(0), 1 - 2 * (space % 2)])
    flat = np.arange(ROWS * LANES, dtype=np.int32)
    wave_x = jnp.sin(
        2.0 * math.pi / 16 * (plane[:, None] - positions[0][None, :]).astype(f32)
    )
    wave_x = jnp.broadcast_to(wave_x[:, :, None, None], (2, 4, 8, LANES))
    wave_y = jnp.sin(
        2.0 * math.pi / NY * (jnp.asarray(flat // NZ)[None, :] - positions[1][:, None]).astype(f32)
    ).reshape((4,) + plane_shape)
    wave_z = jnp.sin(
        2.0 * math.pi / NZ * (jnp.asarray(flat % NZ)[None, :] - positions[2][:, None]).astype(f32)
    ).reshape((4,) + plane_shape)
    weight = jnp.pad(strengths, (0, LANES - PRJ)).reshape(1, LANES)
    u2, rest, gram = call(
        functools.partial(advance_kernel, False),
        [fields_shape, rest_shape, (PRJ, LANES)],
        [flags, received, weight, second] + basis + [early],
        scratch=[table_scratch],
        scalars=1,
    )

    def finish(center, first, second, around, u2, rest, parts=None):
        flat = u2.reshape((8,) + plane_shape)
        near = lax.ppermute(flat, "space", from_near)
        shared = None
        if parts is not None:
            flat, parts = fence(flat, parts)
            far = lax.ppermute(flat, "space", from_far)
            shared = lax.all_to_all(parts, "band", 0, 0, tiled=True)
            rest, shared = fence(rest, shared)
        partial = call(
            partial_kernel,
            fields_shape,
            [flags, center, first, second] + basis + [around, rest],
            scratch=[table_scratch],
            scalars=1,
        )
        if parts is None:
            flat, partial = fence(flat, partial)
            far = lax.ppermute(flat, "space", from_far)
        return shared, call(
            last_kernel,
            fields_shape,
            [flags, near, far, u2, around, column, partial],
            scratch=[field_scratch] * 3 + [work_scratch],
            scalars=1,
        )

    _, mid = finish(center, first, second, early, u2, rest)
    near, far = exchange(mid)
    yours = swap_core(mid[1])
    known, basis_flat = call(
        middle_moments_kernel,
        [(24, LANES), jax.ShapeDtypeStruct((128, ROWS * LANES), jnp.bfloat16)],
        [mid, late] + basis + [wave_x, wave_y, wave_z],
    )
    first, second, part = call(
        second_kernel,
        [fields_shape, fields_shape, (16, 32, LANES)],
        [near, far, mid, late, column, basis_flat, known],
        scratch=[
            field_scratch,
            work_scratch,
            pltpu.VMEM((64, ROWS * LANES), jnp.bfloat16),
        ],
    )
    part, yours = fence(part, yours)
    received = lax.all_to_all(part, "space", 0, 0, tiled=True)
    received, first, second, late, mid, yours = fence(received, first, second, late, mid, yours)
    u2, rest = call(
        functools.partial(advance_kernel, True),
        [fields_shape, rest_shape],
        [flags, received, weight, second] + basis + [late, gram],
        scratch=[table_scratch],
        scalars=1,
    )

    parts = call(
        payload_kernel, (16, 8, LANES), [flags, mid, yours, received, weight], scalars=1
    )
    shared, end = finish(mid, first, second, late, u2, rest, parts)
    density, forces = call(outcome_kernel, [(1, 576), (3, 4)], [odd, shared], scalars=1)

    swapped = swap_core(end[1])
    psi_end = jnp.where(lower, end[0], swapped).reshape(psi_start.shape)
    adjoint_start = jnp.where(lower, swapped, end[0]).reshape(adjoint_end.shape)
    return (psi_end, adjoint_start, density, forces)


def solution(mesh):
    return jax.shard_map(
        body,
        mesh=mesh,
        in_specs=(
            P(None, "band", "space", None),
            P(None, "band", "space", None),
            P("space", None),
            P("space", None),
            P("band", "space", None),
            P(None, "space", None),
            P(),
            P(),
        ),
        out_specs=(
            P(None, "band", "space", None),
            P(None, "band", "space", None),
            P("space", "band"),
            P(),
        ),
        check_vma=False,
    )
```

time: 161 us -> 137 us (0.85)
  waiting for transfers between devices: 52.7 us -> 25.7 us
  blocking collectives: 13.6 us -> 38.2 us
  starting transfers between devices: 41.6 us -> 27.6 us
  other arithmetic: 9.04 us -> 2.03 us
  local copies, waits for them, and re-layouts: 11.8 us -> 8.38 us
  Pallas kernels: 30.3 us -> 33.3 us
    all_to_all x3 -> x1, waiting for transfers between devices: 34.2 us -> 0.01 us  [body(): basis_own = lax.all_to_all(payload, 'band', 0, 0, tiled=True)]
    all_to_all x1 -> x3, blocking collectives: 13.6 us -> 38.2 us  [the longest x2 20.3 us: body(): received = lax.all_to_all(part, 'space', 0, 0, tiled=True)]
    ppermute x9, waiting for transfers between devices: 17 us -> 24.2 us  [the longest x1 7.92 us: body(): near = lax.ppermute(near_message, 'space', from_near)]
    all_to_all x3 -> x1, starting transfers between devices: 18.5 us -> 11.7 us  [body(): basis_own = lax.all_to_all(payload, 'band', 0, 0, tiled=True)]
    ppermute x4 -> x5, starting transfers between devices: 11.6 us -> 6.32 us  [swap_core(): return lax.ppermute(x, 'space', [(i, i ^ 1) for i in range(16)])]
    pallas_call x10 -> x18, Pallas kernels: 30.3 us -> 33.3 us  [call(): pl.pallas_call(kernel, out_shape=shapes, in_specs=specs, out_specs=[VMEM]...]
    broadcast_in_dim x4 -> x0, local copies, waits for them, and re-layouts: 2.6 us -> none  [the longest x2 1.4 us: total(): jnp.broadcast_to(part[None], (16,) + part.shape)]
    ppermute x9, starting transfers between devices: 11.5 us -> 9.48 us  [the longest x2 4.41 us: finish(): near = lax.ppermute(flat, 'space', from_near)]
  transfers between devices with their start and end apart: 16 -> 15, of which waited for: 10 -> 7; matrix products, arithmetic and copies ran while one was open for 5% -> 1% of each run, Pallas kernels for 7% -> 14%
where the time goes in v2:
time: 137 us; the launch traced here: 136 us
  blocking collectives  38.2 us (28%)
  Pallas kernels  33.3 us (24%)
  starting transfers between devices  27.6 us (20%)
  waiting for transfers between devices  25.7 us (19%)
  local copies, waits for them, and re-layouts  8.38 us (6%)
  other arithmetic  2.03 us (1%)
    pallas_call x18, Pallas kernels, call(): pl.pallas_call(kernel, out_shape=shapes, in_specs=specs, out_specs=[VMEM]...  33.3 us
    all_to_all x2, blocking collectives, body(): received = lax.all_to_all(part, 'space', 0, 0, tiled=True)  20.3 us
    all_to_all x1, blocking collectives, finish(): shared = lax.all_to_all(parts, 'band', 0, 0, tiled=True)  17.8 us
    all_to_all x1, starting transfers between devices, body(): basis_own = lax.all_to_all(payload, 'band', 0, 0, tiled=True)  11.7 us
    unnamed x32, local copies, waits for them, and re-layouts  8.28 us
    ppermute x1, waiting for transfers between devices, body(): near = lax.ppermute(near_message, 'space', from_near)  7.92 us
    ppermute x2, waiting for transfers between devices, finish(): far = lax.ppermute(flat, 'space', from_far)  7.37 us
    ppermute x5, starting transfers between devices, swap_core(): return lax.ppermute(x, 'space', [(i, i ^ 1) for i in range(16)])  6.32 us
  transfers between devices with their start and end apart: 15, of which 7 were waited for; matrix products, arithmetic and copies ran while one was open for 1% of the time, Pallas kernels for 14%

profile of v2, /device:TPU:1, one launch (start us, length us, event | category | flops | bytes accessed | tf_op | source)
XLA Modules:
  0.0 136.1 jit_solution(17557278951909172361)
XLA Ops:
  0.7 0.8 copy-done.9
  1.4 0.7 copy-done.12
  2.1 1.0 shard_map.138
  3.1 11.7 %all-to-all-start = ((f32[16,72,128]{2,1,0:T(8,128)}), f32[16,72,128]{2,1,0:T(8,128)S(1)}, u32[]{:S(2)}, u32[]{:S(2)}) async-start(f32[16,72,128]{2,1,0:T(8,128)} %shard_map.138), calls=%async_computation | async-start | bytes 1179648 | tf_op jit(solution)/shard_map/all_to_all | solution.py:583
  14.9 0.9 copy-done.7
  15.9 0.9 copy-done.8
  16.8 0.8 copy-done.10
  17.5 0.8 copy-done.11
  18.3 0.6 shard_map.139
  18.9 1.0 collective-permute-start
  19.9 1.1 collective-permute-done.other
  21.1 2.7 %collective-permute-start.1 = (f32[10,72,128]{2,1,0:T(8,128)S(1)}, f32[10,72,128]{2,1,0:T(8,128)S(1)}, u32[]{:S(2)}, u32[]{:S(2)}) collective-permute-start(f32[10,72,128]{2,1,0:T(8,128)S(1)} %get-tuple-element.67), channel_id=1, source_target_pairs={{0,2},{1,15},{2,4},{3,1},{4,6},{5,3},{6,8},{7,5},{8,10},{9,7},{10,... | collective-permute-start | bytes 1105928 | tf_op jit(solution)/shard_map/ppermute | solution.py:612
  23.8 7.9 %collective-permute-done.1.near = f32[10,72,128]{2,1,0:T(8,128)S(1)} collective-permute-done((f32[10,72,128]{2,1,0:T(8,128)S(1)}, f32[10,72,128]{2,1,0:T(8,128)S(1)}, u32[]{:S(2)}, u32[]{:S(2)}) %collective-permute-start.1) | collective-permute-done | bytes 368672 | tf_op jit(solution)/shard_map/ppermute | solution.py:612
  31.7 0.7 copy-done.3
  32.4 3.8 %collective-permute-done.2.far = f32[10,72,128]{2,1,0:T(8,128)S(1)} collective-permute-done((f32[10,72,128]{2,1,0:T(8,128)S(1)}, f32[10,72,128]{2,1,0:T(8,128)S(1)}, u32[]{:S(2)}, u32[]{:S(2)}) %collective-permute-start.2) | collective-permute-done | bytes 368672 | tf_op jit(solution)/shard_map/ppermute | solution.py:613
  36.3 0.7 copy-done.5
  37.0 1.0 copy-done.4
  38.0 1.0 copy-done.6
  39.0 2.8 %shard_map.141 = (f32[2,4,72,128]{3,2,1,0:T(8,128)S(1)}, f32[2,4,72,128]{3,2,1,0:T(8,128)S(1)}, f32[4,72,128]{2,1,0:T(8,128)S(1)}, f32[4,72,128]{2,1,0:T(8,128)S(1)}) custom-call(f32[2]{0:T(128)S(1)} %pad_maximum_fusion.flags, f32[10,72,128]{2,1,0:T(8,128)S(1)} %copy-done.4, f32[10,72,128]{2,1,0:T(8,128)S(1)} %copy-done.6, ...), custom_call_target="tpu_custom_call" | custom-call | tf_op jit(solution)/shard_map/pallas_call | solution.py:109
  41.9 1.8 %shard_map.142 = (f32[16,128]{1,0:T(8,128)S(1)}, bf16[32,9216]{1,0:T(8,128)(2,1)S(1)}) custom-call(f32[576,128]{1,0:T(8,128)S(1)} %bitcast.51, f32[576,128]{1,0:T(8,128)S(1)} %bitcast.53, f32[576,128]{1,0:T(8,128)S(1)} %bitcast.52, f32[1152,128]{1,0:T(8,128)S(1)} %bitcast.41, f32[1152,128]{1,0:T(8,128)S(1)} %bitcast.44), custom_call_target="tpu_custom_call" | custom-call | tf_op jit(solution)/shard_map/pallas_call | solution.py:109
  43.6 3.0 %collective-permute-done.3.basis_near = f32[16,72,128]{2,1,0:T(8,128)S(1)} collective-permute-done((f32[16,72,128]{2,1,0:T(8,128)S(1)}, f32[16,72,128]{2,1,0:T(8,128)S(1)}, u32[]{:S(2)}, u32[]{:S(2)}) %collective-permute-start.3) | collective-permute-done | bytes 589856 | tf_op jit(solution)/shard_map/ppermute | solution.py:618
  46.6 1.7 %shard_map.143.own_k = f32[16,72,128]{2,1,0:T(8,128)S(1)} custom-call(f32[16,72,128]{2,1,0:T(8,128)S(1)} %all-to-all-done.basis.own, f32[16,72,128]{2,1,0:T(8,128)S(1)} %collective-permute-done.4.basis_other.other, f32[16,72,128]{2,1,0:T(8,128)S(1)} %collective-permute-done.3.basis_near, s32[72,128]{1,0:T(8,128)S(1)} %copy-done), custom_call_target="tpu_custom_call" | custom-call | tf_op jit(solution)/shard_map/pallas_call | solution.py:109
  48.3 2.4 %collective-permute-start.5 = (f32[16,72,128]{2,1,0:T(8,128)S(1)}, f32[16,72,128]{2,1,0:T(8,128)S(1)}, u32[]{:S(2)}, u32[]{:S(2)}) collective-permute-start(f32[16,72,128]{2,1,0:T(8,128)S(1)} %shard_map.143.own_k), channel_id=1, source_target_pairs={{0,1},{1,0},{2,3},{3,2},{4,5},{5,4},{6,7},{7,6},{8,9},{9,8},{10,11... | collective-permute-start | bytes 1769480 | tf_op jit(solution)/shard_map/ppermute | solution.py:550
  50.7 1.6 %shard_map.144.gram = f32[16,128]{1,0:T(8,128)S(1)} custom-call(f32[1152,128]{1,0:T(8,128)S(1)} %bitcast.42, f32[1152,128]{1,0:T(8,128)S(1)} %bitcast.46, f32[4,72,128]{2,1,0:T(8,128)S(1)} %get-tuple-element.92.early.potential, f32[4,72,128]{2,1,0:T(8,128)S(1)} %get-tuple-element.111.late.potential), custom_call_target="tpu_custom_call" | custom-call | tf_op jit(solution)/shard_map/pallas_call | solution.py:109
  52.3 1.2 shard_map.145
  53.5 10.3 %all_to_all.20.received = f32[16,16,128]{2,1,0:T(8,128)S(1)} all-to-all(f32[16,16,128]{2,1,0:T(8,128)S(1)} %shard_map.145), channel_id=1, replica_groups=mesh['band'=16,'space'=16] {'space'}, dimensions={0} | all-to-all | bytes 262144 | tf_op jit(solution)/shard_map/all_to_all | solution.py:672
  63.8 2.1 %shard_map.146 = (f32[2,4,72,128]{3,2,1,0:T(8,128)S(1)}, f32[2,8,128]{2,1,0:T(8,128)S(1)}, f32[16,128]{1,0:T(8,128)S(1)}) custom-call(f32[2]{0:T(128)S(1)} %pad_maximum_fusion.flags, f32[16,16,128]{2,1,0:T(8,128)S(1)} %all_to_all.20.received, f32[1,128]{1,0:T(1,128)S(1)} %pad_bitcast_fusion.strengths, f32[2,4,72,128]{3,2,1,0:T(8,128)S(1)} %get-tuple-element.91.second, ...), custom_call_target="tpu_custom_call" | custom-call | tf_op jit(solution)/shard_map/pallas_call | solution.py:109
  65.9 1.1 collective-permute-start.6
  67.1 1.7 %shard_map.147.partial = f32[2,4,72,128]{3,2,1,0:T(8,128)S(1)} custom-call(f32[2]{0:T(128)S(1)} %pad_maximum_fusion.flags, f32[2,4,72,128]{3,2,1,0:T(8,128)S(1)} %get-tuple-element.94.center, f32[2,4,72,128]{3,2,1,0:T(8,128)S(1)} %copy-done.2, f32[2,4,72,128]{3,2,1,0:T(8,128)S(1)} %get-tuple-element.91.second, f32[16,72,128]{2,1,0:T(8,128)S(1)} %all-to-all-done.basis.own, ...), custom_call_target="tpu_custom_call" | custom-call | tf_op jit(solution)/shard_map/pallas_call | solution.py:109
  68.8 0.5 collective-permute-start.7
  69.4 1.0 multiply_sine_fusion
  70.4 7.4 %collective-permute-done.7.far = f32[8,72,128]{2,1,0:T(8,128)S(1)} collective-permute-done((f32[8,72,128]{2,1,0:T(8,128)S(1)}, f32[8,72,128]{2,1,0:T(8,128)S(1)}, u32[]{:S(2)}, u32[]{:S(2)}) %collective-permute-start.7) | collective-permute-done | bytes 294944 | tf_op jit(solution)/shard_map/ppermute | solution.py:715
  77.8 2.8 %shard_map.148.center.mine = f32[2,4,72,128]{3,2,1,0:T(8,128)S(1)} custom-call(f32[2]{0:T(128)S(1)} %pad_maximum_fusion.flags, f32[8,72,128]{2,1,0:T(8,128)S(1)} %collective-permute-done.6.near, f32[8,72,128]{2,1,0:T(8,128)S(1)} %collective-permute-done.7.far, f32[2,4,72,128]{3,2,1,0:T(8,128)S(1)} %get-tuple-element.93.center, ...), custom_call_target="tpu_custom_call" | custom-call | tf_op jit(solution)/shard_map/pallas_call | solution.py:109
  80.7 1.5 %collective-permute-start.9 = (f32[8,72,128]{2,1,0:T(8,128)S(1)}, f32[8,72,128]{2,1,0:T(8,128)S(1)}, u32[]{:S(2)}, u32[]{:S(2)}) collective-permute-start(f32[8,72,128]{2,1,0:T(8,128)S(1)} %bitcast.50), channel_id=1, source_target_pairs={{2,0},{15,1},{4,2},{1,3},{6,4},{3,5},{8,6},{5,7},{10,8},{7,9},{12,... | collective-permute-start | bytes 884744 | tf_op jit(solution)/shard_map/ppermute | solution.py:610
  82.2 2.4 %collective-permute-start.10 = (f32[4,72,128]{2,1,0:T(8,128)S(1)}, f32[4,72,128]{2,1,0:T(8,128)S(1)}, u32[]{:S(2)}, u32[]{:S(2)}) collective-permute-start(f32[4,72,128]{2,1,0:T(8,128)S(1)} %slice_bitcast_fusion.2), channel_id=1, source_target_pairs={{0,1},{1,0},{2,3},{3,2},{4,5},{5,4},{6,7},{7,6},{8,9},{9,8},{10,11... | collective-permute-start | bytes 442376 | tf_op jit(solution)/shard_map/ppermute | solution.py:550
  84.8 4.5 %shard_map.149 = (f32[24,128]{1,0:T(8,128)S(1)}, bf16[128,9216]{1,0:T(8,128)(2,1)S(1)}) custom-call(f32[2,4,72,128]{3,2,1,0:T(8,128)S(1)} %shard_map.148.center.mine, f32[4,72,128]{2,1,0:T(8,128)S(1)} %get-tuple-element.111.late.potential, f32[16,72,128]{2,1,0:T(8,128)S(1)} %all-to-all-done.basis.own, ...), custom_call_target="tpu_custom_call" | custom-call | tf_op jit(solution)/shard_map/pallas_call | solution.py:109
  89.2 2.1 %collective-permute-done.9.far = f32[8,72,128]{2,1,0:T(8,128)S(1)} collective-permute-done((f32[8,72,128]{2,1,0:T(8,128)S(1)}, f32[8,72,128]{2,1,0:T(8,128)S(1)}, u32[]{:S(2)}, u32[]{:S(2)}) %collective-permute-start.9) | collective-permute-done | bytes 294944 | tf_op jit(solution)/shard_map/ppermute | solution.py:610
  91.4 3.7 %shard_map.150 = (f32[2,4,72,128]{3,2,1,0:T(8,128)S(1)}, f32[2,4,72,128]{3,2,1,0:T(8,128)S(1)}, f32[16,32,128]{2,1,0:T(8,128)S(1)}) custom-call(f32[8,72,128]{2,1,0:T(8,128)S(1)} %collective-permute-done.8.near, f32[8,72,128]{2,1,0:T(8,128)S(1)} %collective-permute-done.9.far, f32[2,4,72,128]{3,2,1,0:T(8,128)S(1)} %shard_map.148.center.mine, ...), custom_call_target="tpu_custom_call" | custom-call | tf_op jit(solution)/shard_map/pallas_call | solution.py:109
  95.1 10.1 %all_to_all.21.received = f32[16,32,128]{2,1,0:T(8,128)S(1)} all-to-all(f32[16,32,128]{2,1,0:T(8,128)S(1)} %get-tuple-element.105), channel_id=1, replica_groups=mesh['band'=16,'space'=16] {'space'}, dimensions={0} | all-to-all | bytes 524288 | tf_op jit(solution)/shard_map/all_to_all | solution.py:743
  105.1 0.6 shard_map.152
  105.7 2.0 %shard_map.151 = (f32[2,4,72,128]{3,2,1,0:T(8,128)S(1)}, f32[2,8,128]{2,1,0:T(8,128)S(1)}) custom-call(f32[2]{0:T(128)S(1)} %pad_maximum_fusion.flags, f32[16,32,128]{2,1,0:T(8,128)S(1)} %all_to_all.21.received, f32[1,128]{1,0:T(1,128)S(1)} %pad_bitcast_fusion.strengths, f32[2,4,72,128]{3,2,1,0:T(8,128)S(1)} %get-tuple-element.110.second, ...), custom_call_target="tpu_custom_call" | custom-call | tf_op jit(solution)/shard_map/pallas_call | solution.py:109
  108.1 3.3 %collective-permute-start.11 = (f32[8,72,128]{2,1,0:T(8,128)S(1)}, f32[8,72,128]{2,1,0:T(8,128)S(1)}, u32[]{:S(2)}, u32[]{:S(2)}) collective-permute-start(f32[8,72,128]{2,1,0:T(8,128)S(1)} %bitcast.57), channel_id=1, source_target_pairs={{0,2},{1,15},{2,4},{3,1},{4,6},{5,3},{6,8},{7,5},{8,10},{9,7},{10,... | collective-permute-start | bytes 884744 | tf_op jit(solution)/shard_map/ppermute | solution.py:699
  111.4 17.8 %all_to_all.22.received = f32[16,8,128]{2,1,0:T(8,128)S(1)} all-to-all(f32[16,8,128]{2,1,0:T(8,128)S(1)} %shard_map.152), channel_id=1, replica_groups=mesh['band'=16,'space'=16] {'band'}, dimensions={0} | all-to-all | bytes 131072 | tf_op jit(solution)/shard_map/all_to_all | solution.py:704
  129.2 1.7 %shard_map.153.partial = f32[2,4,72,128]{3,2,1,0:T(8,128)S(1)} custom-call(f32[2]{0:T(128)S(1)} %pad_maximum_fusion.flags, f32[2,4,72,128]{3,2,1,0:T(8,128)S(1)} %shard_map.148.center.mine, f32[2,4,72,128]{3,2,1,0:T(8,128)S(1)} %get-tuple-element.117.first, f32[2,4,72,128]{3,2,1,0:T(8,128)S(1)} %get-tuple-element.110.second, ...), custom_call_target="tpu_custom_call" | custom-call | tf_op jit(solution)/shard_map/pallas_call | solution.py:109
  130.9 2.9 %shard_map.154 = f32[2,4,72,128]{3,2,1,0:T(8,128)S(1)} custom-call(f32[2]{0:T(128)S(1)} %pad_maximum_fusion.flags, f32[8,72,128]{2,1,0:T(8,128)S(1)} %collective-permute-done.11.near, f32[8,72,128]{2,1,0:T(8,128)S(1)} %collective-permute-done.12.far, f32[2,4,72,128]{3,2,1,0:T(8,128)S(1)} %get-tuple-element.113.center, ...), custom_call_target="tpu_custom_call" | custom-call | tf_op jit(solution)/shard_map/pallas_call | solution.py:109
  133.8 0.5 collective-permute-start.13
  134.3 0.7 shard_map.155
  135.3 0.7 fusion
  (45 shorter events, 1.3 us)
Async XLA Ops:
  0.6 36.4 %copy-start = (s32[72,128]{1,0:T(8,128)S(1)}, s32[72,128]{1,0:T(8,128)}, u32[]{:S(2)}) copy-start(s32[72,128]{1,0:T(8,128)} %constant.64.clone.column) | copy-start | bytes 110596
  0.7 0.8 copy-start.9
  1.4 0.7 copy-start.12
  3.1 33.9 %all-to-all-start = ((f32[16,72,128]{2,1,0:T(8,128)}), f32[16,72,128]{2,1,0:T(8,128)S(1)}, u32[]{:S(2)}, u32[]{:S(2)}) async-start(f32[16,72,128]{2,1,0:T(8,128)} %shard_map.138), calls=%async_computation | async-start | bytes 1179648 | tf_op jit(solution)/shard_map/all_to_all | solution.py:583
  14.9 0.9 copy-start.7
  15.9 0.9 copy-start.8
  16.8 0.8 copy-start.10
  17.5 0.8 copy-start.11
  18.9 2.1 %collective-permute-start = (f32[6,72,128]{2,1,0:T(8,128)S(1)}, f32[6,72,128]{2,1,0:T(8,128)S(1)}, u32[]{:S(2)}, u32[]{:S(2)}) collective-permute-start(f32[6,72,128]{2,1,0:T(8,128)S(1)} %get-tuple-element.66), channel_id=1, source_target_pairs={{0,1},{1,0},{2,3},{3,2},{4,5},{5,4},{6,7},{7,6},{8,9},{9,8},{10,11... | collective-permute-start | bytes 663560 | tf_op jit(solution)/shard_map/ppermute | solution.py:550
  21.1 10.6 %collective-permute-start.1 = (f32[10,72,128]{2,1,0:T(8,128)S(1)}, f32[10,72,128]{2,1,0:T(8,128)S(1)}, u32[]{:S(2)}, u32[]{:S(2)}) collective-permute-start(f32[10,72,128]{2,1,0:T(8,128)S(1)} %get-tuple-element.67), channel_id=1, source_target_pairs={{0,2},{1,15},{2,4},{3,1},{4,6},{5,3},{6,8},{7,5},{8,10},{9,7},{10,... | collective-permute-start | bytes 1105928 | tf_op jit(solution)/shard_map/ppermute | solution.py:612
  23.8 12.5 %collective-permute-start.2 = (f32[10,72,128]{2,1,0:T(8,128)S(1)}, f32[10,72,128]{2,1,0:T(8,128)S(1)}, u32[]{:S(2)}, u32[]{:S(2)}) collective-permute-start(f32[10,72,128]{2,1,0:T(8,128)S(1)} %get-tuple-element.68), channel_id=1, source_target_pairs={{2,0},{15,1},{4,2},{1,3},{6,4},{3,5},{8,6},{5,7},{10,8},{7,9},{12,... | collective-permute-start | bytes 1105928 | tf_op jit(solution)/shard_map/ppermute | solution.py:613
  31.7 0.7 copy-start.3
  36.3 0.7 copy-start.5
  37.0 4.8 %collective-permute-start.4 = (f32[16,72,128]{2,1,0:T(8,128)S(1)}, f32[16,72,128]{2,1,0:T(8,128)S(1)}, u32[]{:S(2)}, u32[]{:S(2)}) collective-permute-start(f32[16,72,128]{2,1,0:T(8,128)S(1)} %all-to-all-done.basis.own), channel_id=1, source_target_pairs={{0,1},{1,0},{2,3},{3,2},{4,5},{5,4},{6,7},{7,6},{8,9},{9,8},{10,11... | collective-permute-start | bytes 1769480 | tf_op jit(solution)/shard_map/ppermute | solution.py:550
  37.0 9.6 %collective-permute-start.3 = (f32[16,72,128]{2,1,0:T(8,128)S(1)}, f32[16,72,128]{2,1,0:T(8,128)S(1)}, u32[]{:S(2)}, u32[]{:S(2)}) collective-permute-start(f32[16,72,128]{2,1,0:T(8,128)S(1)} %all-to-all-done.basis.own), channel_id=1, source_target_pairs={{0,15},{1,2},{2,1},{3,4},{4,3},{5,6},{6,5},{7,8},{8,7},{9,10},{10,... | collective-permute-start | bytes 1769480 | tf_op jit(solution)/shard_map/ppermute | solution.py:618
  37.0 1.0 copy-start.4
  38.0 1.0 copy-start.6
  41.8 4.8 %copy-start.1 = (f32[2,4,72,128]{3,2,1,0:T(8,128)}, f32[2,4,72,128]{3,2,1,0:T(8,128)S(1)}, u32[]{:S(2)}) copy-start(f32[2,4,72,128]{3,2,1,0:T(8,128)S(1)} %get-tuple-element.95.first) | copy-start | bytes 884740
  48.3 4.0 %collective-permute-start.5 = (f32[16,72,128]{2,1,0:T(8,128)S(1)}, f32[16,72,128]{2,1,0:T(8,128)S(1)}, u32[]{:S(2)}, u32[]{:S(2)}) collective-permute-start(f32[16,72,128]{2,1,0:T(8,128)S(1)} %shard_map.143.own_k), channel_id=1, source_target_pairs={{0,1},{1,0},{2,3},{3,2},{4,5},{5,4},{6,7},{7,6},{8,9},{9,8},{10,11... | collective-permute-start | bytes 1769480 | tf_op jit(solution)/shard_map/ppermute | solution.py:550
  50.7 13.1 %copy-start.14 = (s32[3,4]{1,0:T(4,128)S(1)}, s32[3,4]{1,0:T(4,128)}, u32[]{:S(2)}) copy-start(s32[3,4]{1,0:T(4,128)} %param.18) | copy-start | bytes 148
  50.7 13.1 %copy-start.15 = (f32[16]{0:T(128)S(1)}, f32[16]{0:T(128)}, u32[]{:S(2)}) copy-start(f32[16]{0:T(128)} %param.17) | copy-start | bytes 196
  63.8 3.2 %copy-start.2 = (f32[2,4,72,128]{3,2,1,0:T(8,128)S(1)}, f32[2,4,72,128]{3,2,1,0:T(8,128)}, u32[]{:S(2)}) copy-start(f32[2,4,72,128]{3,2,1,0:T(8,128)} %copy-done.1) | copy-start | bytes 884740
  65.9 3.4 %copy-start.13 = (s32[72,128]{1,0:T(8,128)S(1)}, s32[72,128]{1,0:T(8,128)}, u32[]{:S(2)}) copy-start(s32[72,128]{1,0:T(8,128)} %constant.75) | copy-start | bytes 110596
  65.9 11.9 %collective-permute-start.6 = (f32[8,72,128]{2,1,0:T(8,128)S(1)}, f32[8,72,128]{2,1,0:T(8,128)S(1)}, u32[]{:S(2)}, u32[]{:S(2)}) collective-permute-start(f32[8,72,128]{2,1,0:T(8,128)S(1)} %bitcast.54), channel_id=1, source_target_pairs={{0,2},{1,15},{2,4},{3,1},{4,6},{5,3},{6,8},{7,5},{8,10},{9,7},{10,... | collective-permute-start | bytes 884744 | tf_op jit(solution)/shard_map/ppermute | solution.py:699
  68.8 9.0 %collective-permute-start.7 = (f32[8,72,128]{2,1,0:T(8,128)S(1)}, f32[8,72,128]{2,1,0:T(8,128)S(1)}, u32[]{:S(2)}, u32[]{:S(2)}) collective-permute-start(f32[8,72,128]{2,1,0:T(8,128)S(1)} %bitcast.55), channel_id=1, source_target_pairs={{2,0},{15,1},{4,2},{1,3},{6,4},{3,5},{8,6},{5,7},{10,8},{7,9},{12,... | collective-permute-start | bytes 884744 | tf_op jit(solution)/shard_map/ppermute | solution.py:715
  80.6 8.6 %collective-permute-start.8 = (f32[8,72,128]{2,1,0:T(8,128)S(1)}, f32[8,72,128]{2,1,0:T(8,128)S(1)}, u32[]{:S(2)}, u32[]{:S(2)}) collective-permute-start(f32[8,72,128]{2,1,0:T(8,128)S(1)} %bitcast.49), channel_id=1, source_target_pairs={{0,2},{1,15},{2,4},{3,1},{4,6},{5,3},{6,8},{7,5},{8,10},{9,7},{10,... | collective-permute-start | bytes 884744 | tf_op jit(solution)/shard_map/ppermute | solution.py:610
  80.7 10.6 %collective-permute-start.9 = (f32[8,72,128]{2,1,0:T(8,128)S(1)}, f32[8,72,128]{2,1,0:T(8,128)S(1)}, u32[]{:S(2)}, u32[]{:S(2)}) collective-permute-start(f32[8,72,128]{2,1,0:T(8,128)S(1)} %bitcast.50), channel_id=1, source_target_pairs={{2,0},{15,1},{4,2},{1,3},{6,4},{3,5},{8,6},{5,7},{10,8},{7,9},{12,... | collective-permute-start | bytes 884744 | tf_op jit(solution)/shard_map/ppermute | solution.py:610
  82.2 12.9 %collective-permute-start.10 = (f32[4,72,128]{2,1,0:T(8,128)S(1)}, f32[4,72,128]{2,1,0:T(8,128)S(1)}, u32[]{:S(2)}, u32[]{:S(2)}) collective-permute-start(f32[4,72,128]{2,1,0:T(8,128)S(1)} %slice_bitcast_fusion.2), channel_id=1, source_target_pairs={{0,1},{1,0},{2,3},{3,2},{4,5},{5,4},{6,7},{7,6},{8,9},{9,8},{10,11... | collective-permute-start | bytes 442376 | tf_op jit(solution)/shard_map/ppermute | solution.py:550
  107.7 23.2 %collective-permute-start.12 = (f32[8,72,128]{2,1,0:T(8,128)S(1)}, f32[8,72,128]{2,1,0:T(8,128)S(1)}, u32[]{:S(2)}, u32[]{:S(2)}) collective-permute-start(f32[8,72,128]{2,1,0:T(8,128)S(1)} %bitcast.56), channel_id=1, source_target_pairs={{2,0},{15,1},{4,2},{1,3},{6,4},{3,5},{8,6},{5,7},{10,8},{7,9},{12,... | collective-permute-start | bytes 884744 | tf_op jit(solution)/shard_map/ppermute | solution.py:703
  108.1 22.8 %collective-permute-start.11 = (f32[8,72,128]{2,1,0:T(8,128)S(1)}, f32[8,72,128]{2,1,0:T(8,128)S(1)}, u32[]{:S(2)}, u32[]{:S(2)}) collective-permute-start(f32[8,72,128]{2,1,0:T(8,128)S(1)} %bitcast.57), channel_id=1, source_target_pairs={{0,2},{1,15},{2,4},{3,1},{4,6},{5,3},{6,8},{7,5},{8,10},{9,7},{10,... | collective-permute-start | bytes 884744 | tf_op jit(solution)/shard_map/ppermute | solution.py:699
  133.8 1.5 %collective-permute-start.13 = (f32[4,72,128]{2,1,0:T(8,128)S(1)}, f32[4,72,128]{2,1,0:T(8,128)S(1)}, u32[]{:S(2)}, u32[]{:S(2)}) collective-permute-start(f32[4,72,128]{2,1,0:T(8,128)S(1)} %slice_bitcast_fusion), channel_id=1, source_target_pairs={{0,1},{1,0},{2,3},{3,2},{4,5},{5,4},{6,7},{7,6},{8,9},{9,8},{10,11... | collective-permute-start | bytes 442376 | tf_op jit(solution)/shard_map/ppermute | solution.py:550

commit v3 on v2

--- a/solution.py
+++ b/solution.py
@@ -383,7 +383,9 @@
     put_fields([x.reshape(8 * ROWS, LANES) for x in (first, second)], fields_flat)
     found = [pltpu.roll(x, LANES - PRJ, 1) for x in field_moments(fields_flat, basis_flat, 2)]
     value = known[...]
-    share(out, jnp.concatenate([value[:8], stack_rows(*found), value[8:]], 0))
+    packed = value[:8] + pltpu.roll(stack_rows(*found), PRJ, 1)
+    packed = packed + pltpu.roll(value[8:16], 2 * PRJ, 1) + pltpu.roll(value[16:], 3 * PRJ, 1)
+    share(out, packed)
 
 
 def times_i(x):
@@ -399,13 +401,15 @@
         for k in range(core + 2, 16, 2):
             acc = acc + received[k]
         sums.append(acc)
-    mine = jnp.where(upper > 0.5, sums[1], sums[0])[:PRJ]
+    mine = jnp.where(upper > 0.5, sums[1], sums[0])
+    if later:
+        mine = jnp.concatenate([mine, pltpu.roll(mine, LANES - PRJ, 1)], 0)
     lane = lax.broadcasted_iota(jnp.int32, (PRJ, LANES), 1)
     valid = lane < PRJ
     if later:
         grams = gram[...]
     else:
-        theirs = jnp.where(upper > 0.5, sums[0], sums[1])[:PRJ]
+        theirs = jnp.where(upper > 0.5, sums[0], sums[1])
         turned = jnp.where(
             (lane >= 48) & (lane < 64) | (lane >= 80),
             pltpu.roll(theirs, PRJ, 1),
@@ -517,8 +521,9 @@
         sums.append(acc)
     forces = []
     for q in range(3):
-        rows = slice(16 + 4 * q, 20 + 4 * q)
-        products = sums[0][:4] * sums[1][rows] + sums[1][:4] * sums[0][rows]
+        rows, shift = slice(4 * (q % 2), 4 * (q % 2) + 4), LANES - (2 + q // 2) * PRJ
+        slopes = [pltpu.roll(x, shift, 1)[rows] for x in sums]
+        products = sums[0][:4] * slopes[1] + sums[1][:4] * slopes[0]
         forces.append(strengths[...] * jnp.sum(products, axis=0, keepdims=True))
     for k in range(16):
         first = 9 * k // 2
@@ -731,7 +736,7 @@
     )
     first, second, part = call(
         second_kernel,
-        [fields_shape, fields_shape, (16, 32, LANES)],
+        [fields_shape, fields_shape, (16, 8, LANES)],
         [near, far, mid, late, column, basis_flat, known],
         scratch=[
             field_scratch,
@@ -750,6 +755,7 @@
         scalars=1,
     )
 
+    u2, yours = fence(u2, yours)
     parts = call(
         payload_kernel, (16, 8, LANES), [flags, mid, yours, received, weight], scalars=1
     )

time: 137 us -> 135 us (0.985)
  blocking collectives: 38.2 us -> 36.5 us
where the time goes in v3:
time: 135 us; the launch traced here: 134 us
  blocking collectives  36.5 us (27%)
  Pallas kernels  33.4 us (25%)
  starting transfers between devices  27.3 us (20%)
  waiting for transfers between devices  25.9 us (19%)
  local copies, waits for them, and re-layouts  8.38 us (6%)
  other arithmetic  2.03 us (2%)
    pallas_call x18, Pallas kernels, call(): pl.pallas_call(kernel, out_shape=shapes, in_specs=specs, out_specs=[VMEM]...  33.4 us
    all_to_all x2, blocking collectives, body(): received = lax.all_to_all(part, 'space', 0, 0, tiled=True)  19 us
    all_to_all x1, blocking collectives, finish(): shared = lax.all_to_all(parts, 'band', 0, 0, tiled=True)  17.5 us
    all_to_all x1, starting transfers between devices, body(): basis_own = lax.all_to_all(payload, 'band', 0, 0, tiled=True)  11.7 us
    unnamed x32, local copies, waits for them, and re-layouts  8.28 us
    ppermute x1, waiting for transfers between devices, body(): near = lax.ppermute(near_message, 'space', from_near)  7.92 us
    ppermute x2, waiting for transfers between devices, finish(): far = lax.ppermute(flat, 'space', from_far)  7.37 us
    ppermute x5, starting transfers between devices, swap_core(): return lax.ppermute(x, 'space', [(i, i ^ 1) for i in range(16)])  6.11 us
  transfers between devices with their start and end apart: 15, of which 7 were waited for; matrix products, arithmetic and copies ran while one was open for 1% of the time, Pallas kernels for 14%

profile of v3, /device:TPU:1, one launch (start us, length us, event | category | flops | bytes accessed | tf_op | source)
XLA Modules:
  0.0 134.5 jit_solution(17961851862692306693)
XLA Ops:
  0.7 0.8 copy-done.9
  1.4 0.7 copy-done.12
  2.1 1.0 shard_map.138
  3.1 11.7 %all-to-all-start = ((f32[16,72,128]{2,1,0:T(8,128)}), f32[16,72,128]{2,1,0:T(8,128)S(1)}, u32[]{:S(2)}, u32[]{:S(2)}) async-start(f32[16,72,128]{2,1,0:T(8,128)} %shard_map.138), calls=%async_computation | async-start | bytes 1179648 | tf_op jit(solution)/shard_map/all_to_all | solution.py:588
  14.9 0.9 copy-done.7
  15.9 0.9 copy-done.8
  16.8 0.8 copy-done.10
  17.5 0.8 copy-done.11
  18.3 0.6 shard_map.139
  18.9 1.0 collective-permute-start
  19.9 1.1 collective-permute-done.other
  21.1 2.7 %collective-permute-start.1 = (f32[10,72,128]{2,1,0:T(8,128)S(1)}, f32[10,72,128]{2,1,0:T(8,128)S(1)}, u32[]{:S(2)}, u32[]{:S(2)}) collective-permute-start(f32[10,72,128]{2,1,0:T(8,128)S(1)} %get-tuple-element.69), channel_id=1, source_target_pairs={{0,2},{1,15},{2,4},{3,1},{4,6},{5,3},{6,8},{7,5},{8,10},{9,7},{10,... | collective-permute-start | bytes 1105928 | tf_op jit(solution)/shard_map/ppermute | solution.py:617
  23.8 7.9 %collective-permute-done.1.near = f32[10,72,128]{2,1,0:T(8,128)S(1)} collective-permute-done((f32[10,72,128]{2,1,0:T(8,128)S(1)}, f32[10,72,128]{2,1,0:T(8,128)S(1)}, u32[]{:S(2)}, u32[]{:S(2)}) %collective-permute-start.1) | collective-permute-done | bytes 368672 | tf_op jit(solution)/shard_map/ppermute | solution.py:617
  31.7 0.7 copy-done.3
  32.4 3.8 %collective-permute-done.2.far = f32[10,72,128]{2,1,0:T(8,128)S(1)} collective-permute-done((f32[10,72,128]{2,1,0:T(8,128)S(1)}, f32[10,72,128]{2,1,0:T(8,128)S(1)}, u32[]{:S(2)}, u32[]{:S(2)}) %collective-permute-start.2) | collective-permute-done | bytes 368672 | tf_op jit(solution)/shard_map/ppermute | solution.py:618
  36.3 0.7 copy-done.5
  37.0 1.0 copy-done.4
  38.0 1.0 copy-done.6
  39.0 2.8 %shard_map.141 = (f32[2,4,72,128]{3,2,1,0:T(8,128)S(1)}, f32[2,4,72,128]{3,2,1,0:T(8,128)S(1)}, f32[4,72,128]{2,1,0:T(8,128)S(1)}, f32[4,72,128]{2,1,0:T(8,128)S(1)}) custom-call(f32[2]{0:T(128)S(1)} %pad_maximum_fusion.flags, f32[10,72,128]{2,1,0:T(8,128)S(1)} %copy-done.4, f32[10,72,128]{2,1,0:T(8,128)S(1)} %copy-done.6, ...), custom_call_target="tpu_custom_call" | custom-call | tf_op jit(solution)/shard_map/pallas_call | solution.py:109
  41.9 1.8 %shard_map.142 = (f32[16,128]{1,0:T(8,128)S(1)}, bf16[32,9216]{1,0:T(8,128)(2,1)S(1)}) custom-call(f32[576,128]{1,0:T(8,128)S(1)} %bitcast.51, f32[576,128]{1,0:T(8,128)S(1)} %bitcast.53, f32[576,128]{1,0:T(8,128)S(1)} %bitcast.52, f32[1152,128]{1,0:T(8,128)S(1)} %bitcast.41, f32[1152,128]{1,0:T(8,128)S(1)} %bitcast.44), custom_call_target="tpu_custom_call" | custom-call | tf_op jit(solution)/shard_map/pallas_call | solution.py:109
  43.6 3.0 %collective-permute-done.3.basis_near = f32[16,72,128]{2,1,0:T(8,128)S(1)} collective-permute-done((f32[16,72,128]{2,1,0:T(8,128)S(1)}, f32[16,72,128]{2,1,0:T(8,128)S(1)}, u32[]{:S(2)}, u32[]{:S(2)}) %collective-permute-start.3) | collective-permute-done | bytes 589856 | tf_op jit(solution)/shard_map/ppermute | solution.py:623
  46.6 1.7 %shard_map.143.own_k = f32[16,72,128]{2,1,0:T(8,128)S(1)} custom-call(f32[16,72,128]{2,1,0:T(8,128)S(1)} %all-to-all-done.basis.own, f32[16,72,128]{2,1,0:T(8,128)S(1)} %collective-permute-done.4.basis_other.other, f32[16,72,128]{2,1,0:T(8,128)S(1)} %collective-permute-done.3.basis_near, s32[72,128]{1,0:T(8,128)S(1)} %copy-done), custom_call_target="tpu_custom_call" | custom-call | tf_op jit(solution)/shard_map/pallas_call | solution.py:109
  48.3 2.4 %collective-permute-start.5 = (f32[16,72,128]{2,1,0:T(8,128)S(1)}, f32[16,72,128]{2,1,0:T(8,128)S(1)}, u32[]{:S(2)}, u32[]{:S(2)}) collective-permute-start(f32[16,72,128]{2,1,0:T(8,128)S(1)} %shard_map.143.own_k), channel_id=1, source_target_pairs={{0,1},{1,0},{2,3},{3,2},{4,5},{5,4},{6,7},{7,6},{8,9},{9,8},{10,11... | collective-permute-start | bytes 1769480 | tf_op jit(solution)/shard_map/ppermute | solution.py:555
  50.7 1.6 %shard_map.144.gram = f32[16,128]{1,0:T(8,128)S(1)} custom-call(f32[1152,128]{1,0:T(8,128)S(1)} %bitcast.42, f32[1152,128]{1,0:T(8,128)S(1)} %bitcast.46, f32[4,72,128]{2,1,0:T(8,128)S(1)} %get-tuple-element.94.early.potential, f32[4,72,128]{2,1,0:T(8,128)S(1)} %get-tuple-element.113.late.potential), custom_call_target="tpu_custom_call" | custom-call | tf_op jit(solution)/shard_map/pallas_call | solution.py:109
  52.3 1.2 shard_map.145
  53.5 10.3 %all_to_all.20.received = f32[16,16,128]{2,1,0:T(8,128)S(1)} all-to-all(f32[16,16,128]{2,1,0:T(8,128)S(1)} %shard_map.145), channel_id=1, replica_groups=mesh['band'=16,'space'=16] {'space'}, dimensions={0} | all-to-all | bytes 262144 | tf_op jit(solution)/shard_map/all_to_all | solution.py:677
  63.8 2.1 %shard_map.146 = (f32[2,4,72,128]{3,2,1,0:T(8,128)S(1)}, f32[2,8,128]{2,1,0:T(8,128)S(1)}, f32[16,128]{1,0:T(8,128)S(1)}) custom-call(f32[2]{0:T(128)S(1)} %pad_maximum_fusion.flags, f32[16,16,128]{2,1,0:T(8,128)S(1)} %all_to_all.20.received, f32[1,128]{1,0:T(1,128)S(1)} %pad_bitcast_fusion.strengths, f32[2,4,72,128]{3,2,1,0:T(8,128)S(1)} %get-tuple-element.93.second, ...), custom_call_target="tpu_custom_call" | custom-call | tf_op jit(solution)/shard_map/pallas_call | solution.py:109
  65.9 1.1 collective-permute-start.6
  67.1 1.7 %shard_map.147.partial = f32[2,4,72,128]{3,2,1,0:T(8,128)S(1)} custom-call(f32[2]{0:T(128)S(1)} %pad_maximum_fusion.flags, f32[2,4,72,128]{3,2,1,0:T(8,128)S(1)} %get-tuple-element.96.center, f32[2,4,72,128]{3,2,1,0:T(8,128)S(1)} %copy-done.2, f32[2,4,72,128]{3,2,1,0:T(8,128)S(1)} %get-tuple-element.93.second, f32[16,72,128]{2,1,0:T(8,128)S(1)} %all-to-all-done.basis.own, ...), custom_call_target="tpu_custom_call" | custom-call | tf_op jit(solution)/shard_map/pallas_call | solution.py:109
  68.8 0.5 collective-permute-start.7
  69.4 1.0 multiply_sine_fusion
  70.4 7.4 %collective-permute-done.7.far = f32[8,72,128]{2,1,0:T(8,128)S(1)} collective-permute-done((f32[8,72,128]{2,1,0:T(8,128)S(1)}, f32[8,72,128]{2,1,0:T(8,128)S(1)}, u32[]{:S(2)}, u32[]{:S(2)}) %collective-permute-start.7) | collective-permute-done | bytes 294944 | tf_op jit(solution)/shard_map/ppermute | solution.py:720
  77.8 2.8 %shard_map.148.center.mine = f32[2,4,72,128]{3,2,1,0:T(8,128)S(1)} custom-call(f32[2]{0:T(128)S(1)} %pad_maximum_fusion.flags, f32[8,72,128]{2,1,0:T(8,128)S(1)} %collective-permute-done.6.near, f32[8,72,128]{2,1,0:T(8,128)S(1)} %collective-permute-done.7.far, f32[2,4,72,128]{3,2,1,0:T(8,128)S(1)} %get-tuple-element.95.center, ...), custom_call_target="tpu_custom_call" | custom-call | tf_op jit(solution)/shard_map/pallas_call | solution.py:109
  80.7 1.5 %collective-permute-start.9 = (f32[8,72,128]{2,1,0:T(8,128)S(1)}, f32[8,72,128]{2,1,0:T(8,128)S(1)}, u32[]{:S(2)}, u32[]{:S(2)}) collective-permute-start(f32[8,72,128]{2,1,0:T(8,128)S(1)} %bitcast.50), channel_id=1, source_target_pairs={{2,0},{15,1},{4,2},{1,3},{6,4},{3,5},{8,6},{5,7},{10,8},{7,9},{12,... | collective-permute-start | bytes 884744 | tf_op jit(solution)/shard_map/ppermute | solution.py:615
  82.2 2.4 %collective-permute-start.10 = (f32[4,72,128]{2,1,0:T(8,128)S(1)}, f32[4,72,128]{2,1,0:T(8,128)S(1)}, u32[]{:S(2)}, u32[]{:S(2)}) collective-permute-start(f32[4,72,128]{2,1,0:T(8,128)S(1)} %slice_bitcast_fusion.2), channel_id=1, source_target_pairs={{0,1},{1,0},{2,3},{3,2},{4,5},{5,4},{6,7},{7,6},{8,9},{9,8},{10,11... | collective-permute-start | bytes 442376 | tf_op jit(solution)/shard_map/ppermute | solution.py:555
  84.8 4.5 %shard_map.149 = (f32[24,128]{1,0:T(8,128)S(1)}, bf16[128,9216]{1,0:T(8,128)(2,1)S(1)}) custom-call(f32[2,4,72,128]{3,2,1,0:T(8,128)S(1)} %shard_map.148.center.mine, f32[4,72,128]{2,1,0:T(8,128)S(1)} %get-tuple-element.113.late.potential, f32[16,72,128]{2,1,0:T(8,128)S(1)} %all-to-all-done.basis.own, ...), custom_call_target="tpu_custom_call" | custom-call | tf_op jit(solution)/shard_map/pallas_call | solution.py:109
  89.2 2.1 %collective-permute-done.9.far = f32[8,72,128]{2,1,0:T(8,128)S(1)} collective-permute-done((f32[8,72,128]{2,1,0:T(8,128)S(1)}, f32[8,72,128]{2,1,0:T(8,128)S(1)}, u32[]{:S(2)}, u32[]{:S(2)}) %collective-permute-start.9) | collective-permute-done | bytes 294944 | tf_op jit(solution)/shard_map/ppermute | solution.py:615
  91.4 3.7 %shard_map.150 = (f32[2,4,72,128]{3,2,1,0:T(8,128)S(1)}, f32[2,4,72,128]{3,2,1,0:T(8,128)S(1)}, f32[16,8,128]{2,1,0:T(8,128)S(1)}) custom-call(f32[8,72,128]{2,1,0:T(8,128)S(1)} %collective-permute-done.8.near, f32[8,72,128]{2,1,0:T(8,128)S(1)} %collective-permute-done.9.far, f32[2,4,72,128]{3,2,1,0:T(8,128)S(1)} %shard_map.148.center.mine, ...), custom_call_target="tpu_custom_call" | custom-call | tf_op jit(solution)/shard_map/pallas_call | solution.py:109
  95.1 8.7 %all_to_all.21.received = f32[16,8,128]{2,1,0:T(8,128)S(1)} all-to-all(f32[16,8,128]{2,1,0:T(8,128)S(1)} %get-tuple-element.107), channel_id=1, replica_groups=mesh['band'=16,'space'=16] {'space'}, dimensions={0} | all-to-all | bytes 131072 | tf_op jit(solution)/shard_map/all_to_all | solution.py:748
  103.8 2.0 %shard_map.151 = (f32[2,4,72,128]{3,2,1,0:T(8,128)S(1)}, f32[2,8,128]{2,1,0:T(8,128)S(1)}) custom-call(f32[2]{0:T(128)S(1)} %pad_maximum_fusion.flags, f32[16,8,128]{2,1,0:T(8,128)S(1)} %all_to_all.21.received, f32[1,128]{1,0:T(1,128)S(1)} %pad_bitcast_fusion.strengths, f32[2,4,72,128]{3,2,1,0:T(8,128)S(1)} %get-tuple-element.112.second, ...), custom_call_target="tpu_custom_call" | custom-call | tf_op jit(solution)/shard_map/pallas_call | solution.py:109
  105.8 0.6 shard_map.152
  106.8 3.3 %collective-permute-start.11 = (f32[8,72,128]{2,1,0:T(8,128)S(1)}, f32[8,72,128]{2,1,0:T(8,128)S(1)}, u32[]{:S(2)}, u32[]{:S(2)}) collective-permute-start(f32[8,72,128]{2,1,0:T(8,128)S(1)} %bitcast.55), channel_id=1, source_target_pairs={{0,2},{1,15},{2,4},{3,1},{4,6},{5,3},{6,8},{7,5},{8,10},{9,7},{10,... | collective-permute-start | bytes 884744 | tf_op jit(solution)/shard_map/ppermute | solution.py:704
  110.1 17.5 %all_to_all.22.received = f32[16,8,128]{2,1,0:T(8,128)S(1)} all-to-all(f32[16,8,128]{2,1,0:T(8,128)S(1)} %shard_map.152), channel_id=1, replica_groups=mesh['band'=16,'space'=16] {'band'}, dimensions={0} | all-to-all | bytes 131072 | tf_op jit(solution)/shard_map/all_to_all | solution.py:709
  127.6 1.7 %shard_map.153.partial = f32[2,4,72,128]{3,2,1,0:T(8,128)S(1)} custom-call(f32[2]{0:T(128)S(1)} %pad_maximum_fusion.flags, f32[2,4,72,128]{3,2,1,0:T(8,128)S(1)} %shard_map.148.center.mine, f32[2,4,72,128]{3,2,1,0:T(8,128)S(1)} %get-tuple-element.121.first, f32[2,4,72,128]{3,2,1,0:T(8,128)S(1)} %get-tuple-element.112.second, ...), custom_call_target="tpu_custom_call" | custom-call | tf_op jit(solution)/shard_map/pallas_call | solution.py:109
  129.4 2.8 %shard_map.154 = f32[2,4,72,128]{3,2,1,0:T(8,128)S(1)} custom-call(f32[2]{0:T(128)S(1)} %pad_maximum_fusion.flags, f32[8,72,128]{2,1,0:T(8,128)S(1)} %collective-permute-done.11.near, f32[8,72,128]{2,1,0:T(8,128)S(1)} %collective-permute-done.12.far, f32[2,4,72,128]{3,2,1,0:T(8,128)S(1)} %get-tuple-element.117.center, ...), custom_call_target="tpu_custom_call" | custom-call | tf_op jit(solution)/shard_map/pallas_call | solution.py:109
  132.6 0.7 shard_map.155
  133.2 0.5 collective-permute-done.13
  133.7 0.7 fusion
  (45 shorter events, 1.3 us)
Async XLA Ops:
  0.6 36.4 %copy-start = (s32[72,128]{1,0:T(8,128)S(1)}, s32[72,128]{1,0:T(8,128)}, u32[]{:S(2)}) copy-start(s32[72,128]{1,0:T(8,128)} %constant.64.clone.column) | copy-start | bytes 110596
  0.7 0.8 copy-start.9
  1.4 0.7 copy-start.12
  3.1 33.9 %all-to-all-start = ((f32[16,72,128]{2,1,0:T(8,128)}), f32[16,72,128]{2,1,0:T(8,128)S(1)}, u32[]{:S(2)}, u32[]{:S(2)}) async-start(f32[16,72,128]{2,1,0:T(8,128)} %shard_map.138), calls=%async_computation | async-start | bytes 1179648 | tf_op jit(solution)/shard_map/all_to_all | solution.py:588
  14.9 0.9 copy-start.7
  15.9 0.9 copy-start.8
  16.8 0.8 copy-start.10
  17.5 0.8 copy-start.11
  18.9 2.1 %collective-permute-start = (f32[6,72,128]{2,1,0:T(8,128)S(1)}, f32[6,72,128]{2,1,0:T(8,128)S(1)}, u32[]{:S(2)}, u32[]{:S(2)}) collective-permute-start(f32[6,72,128]{2,1,0:T(8,128)S(1)} %get-tuple-element.68), channel_id=1, source_target_pairs={{0,1},{1,0},{2,3},{3,2},{4,5},{5,4},{6,7},{7,6},{8,9},{9,8},{10,11... | collective-permute-start | bytes 663560 | tf_op jit(solution)/shard_map/ppermute | solution.py:555
  21.1 10.6 %collective-permute-start.1 = (f32[10,72,128]{2,1,0:T(8,128)S(1)}, f32[10,72,128]{2,1,0:T(8,128)S(1)}, u32[]{:S(2)}, u32[]{:S(2)}) collective-permute-start(f32[10,72,128]{2,1,0:T(8,128)S(1)} %get-tuple-element.69), channel_id=1, source_target_pairs={{0,2},{1,15},{2,4},{3,1},{4,6},{5,3},{6,8},{7,5},{8,10},{9,7},{10,... | collective-permute-start | bytes 1105928 | tf_op jit(solution)/shard_map/ppermute | solution.py:617
  23.8 12.5 %collective-permute-start.2 = (f32[10,72,128]{2,1,0:T(8,128)S(1)}, f32[10,72,128]{2,1,0:T(8,128)S(1)}, u32[]{:S(2)}, u32[]{:S(2)}) collective-permute-start(f32[10,72,128]{2,1,0:T(8,128)S(1)} %get-tuple-element.70), channel_id=1, source_target_pairs={{2,0},{15,1},{4,2},{1,3},{6,4},{3,5},{8,6},{5,7},{10,8},{7,9},{12,... | collective-permute-start | bytes 1105928 | tf_op jit(solution)/shard_map/ppermute | solution.py:618
  31.7 0.7 copy-start.3
  36.3 0.7 copy-start.5
  37.0 4.8 %collective-permute-start.4 = (f32[16,72,128]{2,1,0:T(8,128)S(1)}, f32[16,72,128]{2,1,0:T(8,128)S(1)}, u32[]{:S(2)}, u32[]{:S(2)}) collective-permute-start(f32[16,72,128]{2,1,0:T(8,128)S(1)} %all-to-all-done.basis.own), channel_id=1, source_target_pairs={{0,1},{1,0},{2,3},{3,2},{4,5},{5,4},{6,7},{7,6},{8,9},{9,8},{10,11... | collective-permute-start | bytes 1769480 | tf_op jit(solution)/shard_map/ppermute | solution.py:555
  37.0 9.6 %collective-permute-start.3 = (f32[16,72,128]{2,1,0:T(8,128)S(1)}, f32[16,72,128]{2,1,0:T(8,128)S(1)}, u32[]{:S(2)}, u32[]{:S(2)}) collective-permute-start(f32[16,72,128]{2,1,0:T(8,128)S(1)} %all-to-all-done.basis.own), channel_id=1, source_target_pairs={{0,15},{1,2},{2,1},{3,4},{4,3},{5,6},{6,5},{7,8},{8,7},{9,10},{10,... | collective-permute-start | bytes 1769480 | tf_op jit(solution)/shard_map/ppermute | solution.py:623
  37.0 1.0 copy-start.4
  38.0 1.0 copy-start.6
  41.8 4.8 %copy-start.1 = (f32[2,4,72,128]{3,2,1,0:T(8,128)}, f32[2,4,72,128]{3,2,1,0:T(8,128)S(1)}, u32[]{:S(2)}) copy-start(f32[2,4,72,128]{3,2,1,0:T(8,128)S(1)} %get-tuple-element.97.first) | copy-start | bytes 884740
  48.3 4.0 %collective-permute-start.5 = (f32[16,72,128]{2,1,0:T(8,128)S(1)}, f32[16,72,128]{2,1,0:T(8,128)S(1)}, u32[]{:S(2)}, u32[]{:S(2)}) collective-permute-start(f32[16,72,128]{2,1,0:T(8,128)S(1)} %shard_map.143.own_k), channel_id=1, source_target_pairs={{0,1},{1,0},{2,3},{3,2},{4,5},{5,4},{6,7},{7,6},{8,9},{9,8},{10,11... | collective-permute-start | bytes 1769480 | tf_op jit(solution)/shard_map/ppermute | solution.py:555
  50.7 13.1 %copy-start.14 = (s32[3,4]{1,0:T(4,128)S(1)}, s32[3,4]{1,0:T(4,128)}, u32[]{:S(2)}) copy-start(s32[3,4]{1,0:T(4,128)} %param.18) | copy-start | bytes 148
  50.7 13.1 %copy-start.15 = (f32[16]{0:T(128)S(1)}, f32[16]{0:T(128)}, u32[]{:S(2)}) copy-start(f32[16]{0:T(128)} %param.17) | copy-start | bytes 196
  63.8 3.2 %copy-start.2 = (f32[2,4,72,128]{3,2,1,0:T(8,128)S(1)}, f32[2,4,72,128]{3,2,1,0:T(8,128)}, u32[]{:S(2)}) copy-start(f32[2,4,72,128]{3,2,1,0:T(8,128)} %copy-done.1) | copy-start | bytes 884740
  65.9 3.4 %copy-start.13 = (s32[72,128]{1,0:T(8,128)S(1)}, s32[72,128]{1,0:T(8,128)}, u32[]{:S(2)}) copy-start(s32[72,128]{1,0:T(8,128)} %constant.75) | copy-start | bytes 110596
  65.9 11.9 %collective-permute-start.6 = (f32[8,72,128]{2,1,0:T(8,128)S(1)}, f32[8,72,128]{2,1,0:T(8,128)S(1)}, u32[]{:S(2)}, u32[]{:S(2)}) collective-permute-start(f32[8,72,128]{2,1,0:T(8,128)S(1)} %bitcast.56), channel_id=1, source_target_pairs={{0,2},{1,15},{2,4},{3,1},{4,6},{5,3},{6,8},{7,5},{8,10},{9,7},{10,... | collective-permute-start | bytes 884744 | tf_op jit(solution)/shard_map/ppermute | solution.py:704
  68.8 9.0 %collective-permute-start.7 = (f32[8,72,128]{2,1,0:T(8,128)S(1)}, f32[8,72,128]{2,1,0:T(8,128)S(1)}, u32[]{:S(2)}, u32[]{:S(2)}) collective-permute-start(f32[8,72,128]{2,1,0:T(8,128)S(1)} %bitcast.57), channel_id=1, source_target_pairs={{2,0},{15,1},{4,2},{1,3},{6,4},{3,5},{8,6},{5,7},{10,8},{7,9},{12,... | collective-permute-start | bytes 884744 | tf_op jit(solution)/shard_map/ppermute | solution.py:720
  80.6 8.6 %collective-permute-start.8 = (f32[8,72,128]{2,1,0:T(8,128)S(1)}, f32[8,72,128]{2,1,0:T(8,128)S(1)}, u32[]{:S(2)}, u32[]{:S(2)}) collective-permute-start(f32[8,72,128]{2,1,0:T(8,128)S(1)} %bitcast.49), channel_id=1, source_target_pairs={{0,2},{1,15},{2,4},{3,1},{4,6},{5,3},{6,8},{7,5},{8,10},{9,7},{10,... | collective-permute-start | bytes 884744 | tf_op jit(solution)/shard_map/ppermute | solution.py:615
  80.7 10.6 %collective-permute-start.9 = (f32[8,72,128]{2,1,0:T(8,128)S(1)}, f32[8,72,128]{2,1,0:T(8,128)S(1)}, u32[]{:S(2)}, u32[]{:S(2)}) collective-permute-start(f32[8,72,128]{2,1,0:T(8,128)S(1)} %bitcast.50), channel_id=1, source_target_pairs={{2,0},{15,1},{4,2},{1,3},{6,4},{3,5},{8,6},{5,7},{10,8},{7,9},{12,... | collective-permute-start | bytes 884744 | tf_op jit(solution)/shard_map/ppermute | solution.py:615
  82.2 12.9 %collective-permute-start.10 = (f32[4,72,128]{2,1,0:T(8,128)S(1)}, f32[4,72,128]{2,1,0:T(8,128)S(1)}, u32[]{:S(2)}, u32[]{:S(2)}) collective-permute-start(f32[4,72,128]{2,1,0:T(8,128)S(1)} %slice_bitcast_fusion.2), channel_id=1, source_target_pairs={{0,1},{1,0},{2,3},{3,2},{4,5},{5,4},{6,7},{7,6},{8,9},{9,8},{10,11... | collective-permute-start | bytes 442376 | tf_op jit(solution)/shard_map/ppermute | solution.py:555
  106.4 22.9 %collective-permute-start.12 = (f32[8,72,128]{2,1,0:T(8,128)S(1)}, f32[8,72,128]{2,1,0:T(8,128)S(1)}, u32[]{:S(2)}, u32[]{:S(2)}) collective-permute-start(f32[8,72,128]{2,1,0:T(8,128)S(1)} %bitcast.54), channel_id=1, source_target_pairs={{2,0},{15,1},{4,2},{1,3},{6,4},{3,5},{8,6},{5,7},{10,8},{7,9},{12,... | collective-permute-start | bytes 884744 | tf_op jit(solution)/shard_map/ppermute | solution.py:708
  106.8 22.6 %collective-permute-start.11 = (f32[8,72,128]{2,1,0:T(8,128)S(1)}, f32[8,72,128]{2,1,0:T(8,128)S(1)}, u32[]{:S(2)}, u32[]{:S(2)}) collective-permute-start(f32[8,72,128]{2,1,0:T(8,128)S(1)} %bitcast.55), channel_id=1, source_target_pairs={{0,2},{1,15},{2,4},{3,1},{4,6},{5,3},{6,8},{7,5},{8,10},{9,7},{10,... | collective-permute-start | bytes 884744 | tf_op jit(solution)/shard_map/ppermute | solution.py:704
  132.3 1.5 %collective-permute-start.13 = (f32[4,72,128]{2,1,0:T(8,128)S(1)}, f32[4,72,128]{2,1,0:T(8,128)S(1)}, u32[]{:S(2)}, u32[]{:S(2)}) collective-permute-start(f32[4,72,128]{2,1,0:T(8,128)S(1)} %slice_bitcast_fusion), channel_id=1, source_target_pairs={{0,1},{1,0},{2,3},{3,2},{4,5},{5,4},{6,7},{7,6},{8,9},{9,8},{10,11... | collective-permute-start | bytes 442376 | tf_op jit(solution)/shard_map/ppermute | solution.py:555

commit v4 on v3

--- a/solution.py
+++ b/solution.py
@@ -48,7 +48,7 @@
     return jnp.where(sub == 0, wrapped, pltpu.roll(x, 1, 0))
 
 
-def kinetic_plane(ref, index, column, beside, store, scratch):
+def around_plane(ref, index, column, store, scratch):
     lane = lax.broadcasted_iota(jnp.int32, (8, LANES), 1)
     sub = lax.broadcasted_iota(jnp.int32, (8, LANES), 0)
     for t, rows in enumerate(TILES):
@@ -66,9 +66,7 @@
         before = previous_rows(scratch, (2,), t, behind, sub)
         up = pltpu.roll(jnp.where(lane >= 1, ahead, after), 127, 1)
         down = pltpu.roll(jnp.where(lane < 127, behind, before), 1, 1)
-        around = scratch[0, rows] + (up + down)
-        x = ref[index + (rows,)]
-        store(rows, x, kinetic_scale * (6.0 * x - around - beside(rows)))
+        store(rows, scratch[0, rows] + (up + down))
 
 
 def fold(x):
@@ -153,41 +151,39 @@
         for k in range(2):
             j = 2 * pair + k
 
-            def store(rows, x, kinetic):
-                out[j, rows] = kinetic
-
-            def beside(rows):
-                return basis_other[j, rows] + basis_near[j, rows]
-
-            kinetic_plane(basis, (j,), column, beside, store, work.at[k])
+            def store(rows, around):
+                beside = basis_other[j, rows] + basis_near[j, rows]
+                out[j, rows] = kinetic_scale * (6.0 * basis[j, rows] - around - beside)
+
+            around_plane(basis, (j,), column, store, work.at[k])
         return carry
 
     lax.fori_loop(0, PRJ // 2, projector, 0)
 
 
-def two_steps(near, far, center, potential, column, first, edge, second, work):
-    def local(source, index, beside, v, out, place, k):
-        def store(rows, x, kinetic):
-            out[place + (rows,)] = kinetic + v[rows] * x
-
-        kinetic_plane(source, index, column, beside, store, work.at[k])
-
+def two_steps(near, far, center, potential, column, first, mixed, second, work):
     def row(q, carry):
-        own, other = (0, q), (1, q)
-        local(
-            center, own, lambda r: near[4 + q, r] + center[1, q, r], potential.at[0], first, own, 0
-        )
-        local(center, other, lambda r: center[0, q, r] + far[q, r], potential.at[1], first, other, 1)
-        local(
-            near, (4 + q,), lambda r: near[q, r] + center[0, q, r], potential.at[2], edge, own, 2
-        )
-        local(
-            far, (q,), lambda r: center[1, q, r] + far[4 + q, r], potential.at[3], edge, other, 3
-        )
-        local(first, own, lambda r: edge[0, q, r] + first[1, q, r], potential.at[0], second, own, 0)
-        local(
-            first, other, lambda r: first[0, q, r] + edge[1, q, r], potential.at[1], second, other, 1
-        )
+        sides = [(0, 1, near, 4 + q, q), (1, 0, far, q, 4 + q)]
+        for plane, across, message, edge, beyond in sides:
+
+            def store(r, around, plane=plane, across=across, message=message, edge=edge):
+                x, e = center[plane, q, r], message[edge, r]
+                value = kinetic_scale * (6.0 * x - around - (e + center[across, q, r]))
+                value = value + potential[plane, r] * x
+                first[plane, q, r] = value
+                mixed[plane, q, r] = value - kinetic_scale * e
+
+            around_plane(center, (plane, q), column, store, work.at[plane])
+        for plane, across, message, edge, beyond in sides:
+
+            def store(r, around, plane=plane, across=across, message=message, edge=edge, beyond=beyond):
+                f, e = first[plane, q, r], message[edge, r]
+                beside = kinetic_scale * (6.0 * e - message[beyond, r] - center[plane, q, r])
+                beside = beside + potential[2 + plane, r] * e + first[across, q, r]
+                value = kinetic_scale * (6.0 * f - around - beside)
+                second[plane, q, r] = value + potential[plane, r] * f
+
+            around_plane(mixed, (plane, q), column, store, work.at[2 + plane])
         return carry
 
     lax.fori_loop(0, 4, row, 0)

time: 135 us -> 133 us (0.985)
  Pallas kernels: 33.4 us -> 31 us
    pallas_call x18, Pallas kernels: 33.4 us -> 31 us  [call(): pl.pallas_call(kernel, out_shape=shapes, in_specs=specs, out_specs=[VMEM]...]
where the time goes in v4:
time: 133 us
  blocking collectives  36.5 us (27%)
  Pallas kernels  31 us (23%)
  starting transfers between devices  27.3 us (21%)
  waiting for transfers between devices  26.5 us (20%)
  local copies, waits for them, and re-layouts  8.38 us (6%)
  other arithmetic  2.03 us (2%)
    pallas_call x18, Pallas kernels, call(): pl.pallas_call(kernel, out_shape=shapes, in_specs=specs, out_specs=[VMEM]...  31 us
    all_to_all x2, blocking collectives, body(): received = lax.all_to_all(part, 'space', 0, 0, tiled=True)  19 us
    all_to_all x1, blocking collectives, finish(): shared = lax.all_to_all(parts, 'band', 0, 0, tiled=True)  17.5 us
    all_to_all x1, starting transfers between devices, body(): basis_own = lax.all_to_all(payload, 'band', 0, 0, tiled=True)  11.7 us
    unnamed x32, local copies, waits for them, and re-layouts  8.28 us
    ppermute x1, waiting for transfers between devices, body(): near = lax.ppermute(near_message, 'space', from_near)  7.92 us
    ppermute x2, waiting for transfers between devices, finish(): far = lax.ppermute(flat, 'space', from_far)  7.37 us
    ppermute x5, starting transfers between devices, swap_core(): return lax.ppermute(x, 'space', [(i, i ^ 1) for i in range(16)])  6.11 us
  transfers between devices with their start and end apart: 15, of which 7 were waited for; matrix products, arithmetic and copies ran while one was open for 1% of the time, Pallas kernels for 14%

profile of v4, /device:TPU:1, one launch (start us, length us, event | category | flops | bytes accessed | tf_op | source)
XLA Modules:
  0.0 132.7 jit_solution(1458712867943965870)
XLA Ops:
  0.7 0.8 copy-done.9
  1.4 0.7 copy-done.12
  2.1 1.0 shard_map.138
  3.1 11.7 %all-to-all-start = ((f32[16,72,128]{2,1,0:T(8,128)}), f32[16,72,128]{2,1,0:T(8,128)S(1)}, u32[]{:S(2)}, u32[]{:S(2)}) async-start(f32[16,72,128]{2,1,0:T(8,128)} %shard_map.138), calls=%async_computation | async-start | bytes 1179648 | tf_op jit(solution)/shard_map/all_to_all | solution.py:584
  14.9 0.9 copy-done.7
  15.9 0.9 copy-done.8
  16.8 0.8 copy-done.10
  17.5 0.8 copy-done.11
  18.3 0.6 shard_map.139
  18.9 1.0 collective-permute-start
  19.9 1.1 collective-permute-done.other
  21.1 2.7 %collective-permute-start.1 = (f32[10,72,128]{2,1,0:T(8,128)S(1)}, f32[10,72,128]{2,1,0:T(8,128)S(1)}, u32[]{:S(2)}, u32[]{:S(2)}) collective-permute-start(f32[10,72,128]{2,1,0:T(8,128)S(1)} %get-tuple-element.69), channel_id=1, source_target_pairs={{0,2},{1,15},{2,4},{3,1},{4,6},{5,3},{6,8},{7,5},{8,10},{9,7},{10,... | collective-permute-start | bytes 1105928 | tf_op jit(solution)/shard_map/ppermute | solution.py:613
  23.8 7.9 %collective-permute-done.1.near = f32[10,72,128]{2,1,0:T(8,128)S(1)} collective-permute-done((f32[10,72,128]{2,1,0:T(8,128)S(1)}, f32[10,72,128]{2,1,0:T(8,128)S(1)}, u32[]{:S(2)}, u32[]{:S(2)}) %collective-permute-start.1) | collective-permute-done | bytes 368672 | tf_op jit(solution)/shard_map/ppermute | solution.py:613
  31.7 0.7 copy-done.3
  32.4 3.8 %collective-permute-done.2.far = f32[10,72,128]{2,1,0:T(8,128)S(1)} collective-permute-done((f32[10,72,128]{2,1,0:T(8,128)S(1)}, f32[10,72,128]{2,1,0:T(8,128)S(1)}, u32[]{:S(2)}, u32[]{:S(2)}) %collective-permute-start.2) | collective-permute-done | bytes 368672 | tf_op jit(solution)/shard_map/ppermute | solution.py:614
  36.3 0.7 copy-done.5
  37.0 1.0 copy-done.4
  38.0 1.0 copy-done.6
  39.0 2.2 %shard_map.141 = (f32[2,4,72,128]{3,2,1,0:T(8,128)S(1)}, f32[2,4,72,128]{3,2,1,0:T(8,128)S(1)}, f32[4,72,128]{2,1,0:T(8,128)S(1)}, f32[4,72,128]{2,1,0:T(8,128)S(1)}) custom-call(f32[2]{0:T(128)S(1)} %pad_maximum_fusion.flags, f32[10,72,128]{2,1,0:T(8,128)S(1)} %copy-done.4, f32[10,72,128]{2,1,0:T(8,128)S(1)} %copy-done.6, ...), custom_call_target="tpu_custom_call" | custom-call | tf_op jit(solution)/shard_map/pallas_call | solution.py:107
  41.3 1.8 %shard_map.142 = (f32[16,128]{1,0:T(8,128)S(1)}, bf16[32,9216]{1,0:T(8,128)(2,1)S(1)}) custom-call(f32[576,128]{1,0:T(8,128)S(1)} %bitcast.51, f32[576,128]{1,0:T(8,128)S(1)} %bitcast.53, f32[576,128]{1,0:T(8,128)S(1)} %bitcast.52, f32[1152,128]{1,0:T(8,128)S(1)} %bitcast.41, f32[1152,128]{1,0:T(8,128)S(1)} %bitcast.44), custom_call_target="tpu_custom_call" | custom-call | tf_op jit(solution)/shard_map/pallas_call | solution.py:107
  43.0 3.6 %collective-permute-done.3.basis_near = f32[16,72,128]{2,1,0:T(8,128)S(1)} collective-permute-done((f32[16,72,128]{2,1,0:T(8,128)S(1)}, f32[16,72,128]{2,1,0:T(8,128)S(1)}, u32[]{:S(2)}, u32[]{:S(2)}) %collective-permute-start.3) | collective-permute-done | bytes 589856 | tf_op jit(solution)/shard_map/ppermute | solution.py:619
  46.6 1.7 %shard_map.143.own_k = f32[16,72,128]{2,1,0:T(8,128)S(1)} custom-call(f32[16,72,128]{2,1,0:T(8,128)S(1)} %all-to-all-done.basis.own, f32[16,72,128]{2,1,0:T(8,128)S(1)} %collective-permute-done.4.basis_other.other, f32[16,72,128]{2,1,0:T(8,128)S(1)} %collective-permute-done.3.basis_near, s32[72,128]{1,0:T(8,128)S(1)} %copy-done), custom_call_target="tpu_custom_call" | custom-call | tf_op jit(solution)/shard_map/pallas_call | solution.py:107
  48.3 2.4 %collective-permute-start.5 = (f32[16,72,128]{2,1,0:T(8,128)S(1)}, f32[16,72,128]{2,1,0:T(8,128)S(1)}, u32[]{:S(2)}, u32[]{:S(2)}) collective-permute-start(f32[16,72,128]{2,1,0:T(8,128)S(1)} %shard_map.143.own_k), channel_id=1, source_target_pairs={{0,1},{1,0},{2,3},{3,2},{4,5},{5,4},{6,7},{7,6},{8,9},{9,8},{10,11... | collective-permute-start | bytes 1769480 | tf_op jit(solution)/shard_map/ppermute | solution.py:551
  50.7 1.6 %shard_map.144.gram = f32[16,128]{1,0:T(8,128)S(1)} custom-call(f32[1152,128]{1,0:T(8,128)S(1)} %bitcast.42, f32[1152,128]{1,0:T(8,128)S(1)} %bitcast.46, f32[4,72,128]{2,1,0:T(8,128)S(1)} %get-tuple-element.94.early.potential, f32[4,72,128]{2,1,0:T(8,128)S(1)} %get-tuple-element.113.late.potential), custom_call_target="tpu_custom_call" | custom-call | tf_op jit(solution)/shard_map/pallas_call | solution.py:107
  52.3 1.2 shard_map.145
  53.5 10.3 %all_to_all.20.received = f32[16,16,128]{2,1,0:T(8,128)S(1)} all-to-all(f32[16,16,128]{2,1,0:T(8,128)S(1)} %shard_map.145), channel_id=1, replica_groups=mesh['band'=16,'space'=16] {'space'}, dimensions={0} | all-to-all | bytes 262144 | tf_op jit(solution)/shard_map/all_to_all | solution.py:673
  63.8 2.1 %shard_map.146 = (f32[2,4,72,128]{3,2,1,0:T(8,128)S(1)}, f32[2,8,128]{2,1,0:T(8,128)S(1)}, f32[16,128]{1,0:T(8,128)S(1)}) custom-call(f32[2]{0:T(128)S(1)} %pad_maximum_fusion.flags, f32[16,16,128]{2,1,0:T(8,128)S(1)} %all_to_all.20.received, f32[1,128]{1,0:T(1,128)S(1)} %pad_bitcast_fusion.strengths, f32[2,4,72,128]{3,2,1,0:T(8,128)S(1)} %get-tuple-element.93.second, ...), custom_call_target="tpu_custom_call" | custom-call | tf_op jit(solution)/shard_map/pallas_call | solution.py:107
  65.9 1.1 collective-permute-start.6
  67.1 1.7 %shard_map.147.partial = f32[2,4,72,128]{3,2,1,0:T(8,128)S(1)} custom-call(f32[2]{0:T(128)S(1)} %pad_maximum_fusion.flags, f32[2,4,72,128]{3,2,1,0:T(8,128)S(1)} %get-tuple-element.96.center, f32[2,4,72,128]{3,2,1,0:T(8,128)S(1)} %copy-done.2, f32[2,4,72,128]{3,2,1,0:T(8,128)S(1)} %get-tuple-element.93.second, f32[16,72,128]{2,1,0:T(8,128)S(1)} %all-to-all-done.basis.own, ...), custom_call_target="tpu_custom_call" | custom-call | tf_op jit(solution)/shard_map/pallas_call | solution.py:107
  68.8 0.5 collective-permute-start.7
  69.4 1.0 multiply_sine_fusion
  70.4 7.4 %collective-permute-done.7.far = f32[8,72,128]{2,1,0:T(8,128)S(1)} collective-permute-done((f32[8,72,128]{2,1,0:T(8,128)S(1)}, f32[8,72,128]{2,1,0:T(8,128)S(1)}, u32[]{:S(2)}, u32[]{:S(2)}) %collective-permute-start.7) | collective-permute-done | bytes 294944 | tf_op jit(solution)/shard_map/ppermute | solution.py:716
  77.8 2.3 %shard_map.148.center.mine = f32[2,4,72,128]{3,2,1,0:T(8,128)S(1)} custom-call(f32[2]{0:T(128)S(1)} %pad_maximum_fusion.flags, f32[8,72,128]{2,1,0:T(8,128)S(1)} %collective-permute-done.6.near, f32[8,72,128]{2,1,0:T(8,128)S(1)} %collective-permute-done.7.far, f32[2,4,72,128]{3,2,1,0:T(8,128)S(1)} %get-tuple-element.95.center, ...), custom_call_target="tpu_custom_call" | custom-call | tf_op jit(solution)/shard_map/pallas_call | solution.py:107
  80.1 1.5 %collective-permute-start.9 = (f32[8,72,128]{2,1,0:T(8,128)S(1)}, f32[8,72,128]{2,1,0:T(8,128)S(1)}, u32[]{:S(2)}, u32[]{:S(2)}) collective-permute-start(f32[8,72,128]{2,1,0:T(8,128)S(1)} %bitcast.50), channel_id=1, source_target_pairs={{2,0},{15,1},{4,2},{1,3},{6,4},{3,5},{8,6},{5,7},{10,8},{7,9},{12,... | collective-permute-start | bytes 884744 | tf_op jit(solution)/shard_map/ppermute | solution.py:611
  81.6 2.4 %collective-permute-start.10 = (f32[4,72,128]{2,1,0:T(8,128)S(1)}, f32[4,72,128]{2,1,0:T(8,128)S(1)}, u32[]{:S(2)}, u32[]{:S(2)}) collective-permute-start(f32[4,72,128]{2,1,0:T(8,128)S(1)} %slice_bitcast_fusion.2), channel_id=1, source_target_pairs={{0,1},{1,0},{2,3},{3,2},{4,5},{5,4},{6,7},{7,6},{8,9},{9,8},{10,11... | collective-permute-start | bytes 442376 | tf_op jit(solution)/shard_map/ppermute | solution.py:551
  84.2 4.5 %shard_map.149 = (f32[24,128]{1,0:T(8,128)S(1)}, bf16[128,9216]{1,0:T(8,128)(2,1)S(1)}) custom-call(f32[2,4,72,128]{3,2,1,0:T(8,128)S(1)} %shard_map.148.center.mine, f32[4,72,128]{2,1,0:T(8,128)S(1)} %get-tuple-element.113.late.potential, f32[16,72,128]{2,1,0:T(8,128)S(1)} %all-to-all-done.basis.own, ...), custom_call_target="tpu_custom_call" | custom-call | tf_op jit(solution)/shard_map/pallas_call | solution.py:107
  88.6 2.1 %collective-permute-done.9.far = f32[8,72,128]{2,1,0:T(8,128)S(1)} collective-permute-done((f32[8,72,128]{2,1,0:T(8,128)S(1)}, f32[8,72,128]{2,1,0:T(8,128)S(1)}, u32[]{:S(2)}, u32[]{:S(2)}) %collective-permute-start.9) | collective-permute-done | bytes 294944 | tf_op jit(solution)/shard_map/ppermute | solution.py:611
  90.8 3.1 %shard_map.150 = (f32[2,4,72,128]{3,2,1,0:T(8,128)S(1)}, f32[2,4,72,128]{3,2,1,0:T(8,128)S(1)}, f32[16,8,128]{2,1,0:T(8,128)S(1)}) custom-call(f32[8,72,128]{2,1,0:T(8,128)S(1)} %collective-permute-done.8.near, f32[8,72,128]{2,1,0:T(8,128)S(1)} %collective-permute-done.9.far, f32[2,4,72,128]{3,2,1,0:T(8,128)S(1)} %shard_map.148.center.mine, ...), custom_call_target="tpu_custom_call" | custom-call | tf_op jit(solution)/shard_map/pallas_call | solution.py:107
  93.9 8.7 %all_to_all.21.received = f32[16,8,128]{2,1,0:T(8,128)S(1)} all-to-all(f32[16,8,128]{2,1,0:T(8,128)S(1)} %get-tuple-element.107), channel_id=1, replica_groups=mesh['band'=16,'space'=16] {'space'}, dimensions={0} | all-to-all | bytes 131072 | tf_op jit(solution)/shard_map/all_to_all | solution.py:744
  102.6 2.0 %shard_map.151 = (f32[2,4,72,128]{3,2,1,0:T(8,128)S(1)}, f32[2,8,128]{2,1,0:T(8,128)S(1)}) custom-call(f32[2]{0:T(128)S(1)} %pad_maximum_fusion.flags, f32[16,8,128]{2,1,0:T(8,128)S(1)} %all_to_all.21.received, f32[1,128]{1,0:T(1,128)S(1)} %pad_bitcast_fusion.strengths, f32[2,4,72,128]{3,2,1,0:T(8,128)S(1)} %get-tuple-element.112.second, ...), custom_call_target="tpu_custom_call" | custom-call | tf_op jit(solution)/shard_map/pallas_call | solution.py:107
  104.6 0.6 shard_map.152
  105.6 3.3 %collective-permute-start.11 = (f32[8,72,128]{2,1,0:T(8,128)S(1)}, f32[8,72,128]{2,1,0:T(8,128)S(1)}, u32[]{:S(2)}, u32[]{:S(2)}) collective-permute-start(f32[8,72,128]{2,1,0:T(8,128)S(1)} %bitcast.55), channel_id=1, source_target_pairs={{0,2},{1,15},{2,4},{3,1},{4,6},{5,3},{6,8},{7,5},{8,10},{9,7},{10,... | collective-permute-start | bytes 884744 | tf_op jit(solution)/shard_map/ppermute | solution.py:700
  108.9 17.5 %all_to_all.22.received = f32[16,8,128]{2,1,0:T(8,128)S(1)} all-to-all(f32[16,8,128]{2,1,0:T(8,128)S(1)} %shard_map.152), channel_id=1, replica_groups=mesh['band'=16,'space'=16] {'band'}, dimensions={0} | all-to-all | bytes 131072 | tf_op jit(solution)/shard_map/all_to_all | solution.py:705
  126.4 1.7 %shard_map.153.partial = f32[2,4,72,128]{3,2,1,0:T(8,128)S(1)} custom-call(f32[2]{0:T(128)S(1)} %pad_maximum_fusion.flags, f32[2,4,72,128]{3,2,1,0:T(8,128)S(1)} %shard_map.148.center.mine, f32[2,4,72,128]{3,2,1,0:T(8,128)S(1)} %get-tuple-element.121.first, f32[2,4,72,128]{3,2,1,0:T(8,128)S(1)} %get-tuple-element.112.second, ...), custom_call_target="tpu_custom_call" | custom-call | tf_op jit(solution)/shard_map/pallas_call | solution.py:107
  128.2 2.3 %shard_map.154 = f32[2,4,72,128]{3,2,1,0:T(8,128)S(1)} custom-call(f32[2]{0:T(128)S(1)} %pad_maximum_fusion.flags, f32[8,72,128]{2,1,0:T(8,128)S(1)} %collective-permute-done.11.near, f32[8,72,128]{2,1,0:T(8,128)S(1)} %collective-permute-done.12.far, f32[2,4,72,128]{3,2,1,0:T(8,128)S(1)} %get-tuple-element.117.center, ...), custom_call_target="tpu_custom_call" | custom-call | tf_op jit(solution)/shard_map/pallas_call | solution.py:107
  130.8 0.7 shard_map.155
  131.5 0.5 collective-permute-done.13
  131.9 0.7 fusion
  (45 shorter events, 1.3 us)
Async XLA Ops:
  0.6 36.4 %copy-start = (s32[72,128]{1,0:T(8,128)S(1)}, s32[72,128]{1,0:T(8,128)}, u32[]{:S(2)}) copy-start(s32[72,128]{1,0:T(8,128)} %constant.64.clone.column) | copy-start | bytes 110596
  0.7 0.8 copy-start.9
  1.4 0.7 copy-start.12
  3.1 33.9 %all-to-all-start = ((f32[16,72,128]{2,1,0:T(8,128)}), f32[16,72,128]{2,1,0:T(8,128)S(1)}, u32[]{:S(2)}, u32[]{:S(2)}) async-start(f32[16,72,128]{2,1,0:T(8,128)} %shard_map.138), calls=%async_computation | async-start | bytes 1179648 | tf_op jit(solution)/shard_map/all_to_all | solution.py:584
  14.9 0.9 copy-start.7
  15.9 0.9 copy-start.8
  16.8 0.8 copy-start.10
  17.5 0.8 copy-start.11
  18.9 2.1 %collective-permute-start = (f32[6,72,128]{2,1,0:T(8,128)S(1)}, f32[6,72,128]{2,1,0:T(8,128)S(1)}, u32[]{:S(2)}, u32[]{:S(2)}) collective-permute-start(f32[6,72,128]{2,1,0:T(8,128)S(1)} %get-tuple-element.68), channel_id=1, source_target_pairs={{0,1},{1,0},{2,3},{3,2},{4,5},{5,4},{6,7},{7,6},{8,9},{9,8},{10,11... | collective-permute-start | bytes 663560 | tf_op jit(solution)/shard_map/ppermute | solution.py:551
  21.1 10.6 %collective-permute-start.1 = (f32[10,72,128]{2,1,0:T(8,128)S(1)}, f32[10,72,128]{2,1,0:T(8,128)S(1)}, u32[]{:S(2)}, u32[]{:S(2)}) collective-permute-start(f32[10,72,128]{2,1,0:T(8,128)S(1)} %get-tuple-element.69), channel_id=1, source_target_pairs={{0,2},{1,15},{2,4},{3,1},{4,6},{5,3},{6,8},{7,5},{8,10},{9,7},{10,... | collective-permute-start | bytes 1105928 | tf_op jit(solution)/shard_map/ppermute | solution.py:613
  23.8 12.5 %collective-permute-start.2 = (f32[10,72,128]{2,1,0:T(8,128)S(1)}, f32[10,72,128]{2,1,0:T(8,128)S(1)}, u32[]{:S(2)}, u32[]{:S(2)}) collective-permute-start(f32[10,72,128]{2,1,0:T(8,128)S(1)} %get-tuple-element.70), channel_id=1, source_target_pairs={{2,0},{15,1},{4,2},{1,3},{6,4},{3,5},{8,6},{5,7},{10,8},{7,9},{12,... | collective-permute-start | bytes 1105928 | tf_op jit(solution)/shard_map/ppermute | solution.py:614
  31.7 0.7 copy-start.3
  36.3 0.7 copy-start.5
  37.0 4.2 %collective-permute-start.4 = (f32[16,72,128]{2,1,0:T(8,128)S(1)}, f32[16,72,128]{2,1,0:T(8,128)S(1)}, u32[]{:S(2)}, u32[]{:S(2)}) collective-permute-start(f32[16,72,128]{2,1,0:T(8,128)S(1)} %all-to-all-done.basis.own), channel_id=1, source_target_pairs={{0,1},{1,0},{2,3},{3,2},{4,5},{5,4},{6,7},{7,6},{8,9},{9,8},{10,11... | collective-permute-start | bytes 1769480 | tf_op jit(solution)/shard_map/ppermute | solution.py:551
  37.0 9.6 %collective-permute-start.3 = (f32[16,72,128]{2,1,0:T(8,128)S(1)}, f32[16,72,128]{2,1,0:T(8,128)S(1)}, u32[]{:S(2)}, u32[]{:S(2)}) collective-permute-start(f32[16,72,128]{2,1,0:T(8,128)S(1)} %all-to-all-done.basis.own), channel_id=1, source_target_pairs={{0,15},{1,2},{2,1},{3,4},{4,3},{5,6},{6,5},{7,8},{8,7},{9,10},{10,... | collective-permute-start | bytes 1769480 | tf_op jit(solution)/shard_map/ppermute | solution.py:619
  37.0 1.0 copy-start.4
  38.0 1.0 copy-start.6
  41.2 5.4 %copy-start.1 = (f32[2,4,72,128]{3,2,1,0:T(8,128)}, f32[2,4,72,128]{3,2,1,0:T(8,128)S(1)}, u32[]{:S(2)}) copy-start(f32[2,4,72,128]{3,2,1,0:T(8,128)S(1)} %get-tuple-element.97.first) | copy-start | bytes 884740
  48.3 4.0 %collective-permute-start.5 = (f32[16,72,128]{2,1,0:T(8,128)S(1)}, f32[16,72,128]{2,1,0:T(8,128)S(1)}, u32[]{:S(2)}, u32[]{:S(2)}) collective-permute-start(f32[16,72,128]{2,1,0:T(8,128)S(1)} %shard_map.143.own_k), channel_id=1, source_target_pairs={{0,1},{1,0},{2,3},{3,2},{4,5},{5,4},{6,7},{7,6},{8,9},{9,8},{10,11... | collective-permute-start | bytes 1769480 | tf_op jit(solution)/shard_map/ppermute | solution.py:551
  50.7 13.1 %copy-start.14 = (s32[3,4]{1,0:T(4,128)S(1)}, s32[3,4]{1,0:T(4,128)}, u32[]{:S(2)}) copy-start(s32[3,4]{1,0:T(4,128)} %param.18) | copy-start | bytes 148
  50.7 13.1 %copy-start.15 = (f32[16]{0:T(128)S(1)}, f32[16]{0:T(128)}, u32[]{:S(2)}) copy-start(f32[16]{0:T(128)} %param.17) | copy-start | bytes 196
  63.8 3.2 %copy-start.2 = (f32[2,4,72,128]{3,2,1,0:T(8,128)S(1)}, f32[2,4,72,128]{3,2,1,0:T(8,128)}, u32[]{:S(2)}) copy-start(f32[2,4,72,128]{3,2,1,0:T(8,128)} %copy-done.1) | copy-start | bytes 884740
  65.9 3.4 %copy-start.13 = (s32[72,128]{1,0:T(8,128)S(1)}, s32[72,128]{1,0:T(8,128)}, u32[]{:S(2)}) copy-start(s32[72,128]{1,0:T(8,128)} %constant.75) | copy-start | bytes 110596
  65.9 11.9 %collective-permute-start.6 = (f32[8,72,128]{2,1,0:T(8,128)S(1)}, f32[8,72,128]{2,1,0:T(8,128)S(1)}, u32[]{:S(2)}, u32[]{:S(2)}) collective-permute-start(f32[8,72,128]{2,1,0:T(8,128)S(1)} %bitcast.56), channel_id=1, source_target_pairs={{0,2},{1,15},{2,4},{3,1},{4,6},{5,3},{6,8},{7,5},{8,10},{9,7},{10,... | collective-permute-start | bytes 884744 | tf_op jit(solution)/shard_map/ppermute | solution.py:700
  68.8 9.0 %collective-permute-start.7 = (f32[8,72,128]{2,1,0:T(8,128)S(1)}, f32[8,72,128]{2,1,0:T(8,128)S(1)}, u32[]{:S(2)}, u32[]{:S(2)}) collective-permute-start(f32[8,72,128]{2,1,0:T(8,128)S(1)} %bitcast.57), channel_id=1, source_target_pairs={{2,0},{15,1},{4,2},{1,3},{6,4},{3,5},{8,6},{5,7},{10,8},{7,9},{12,... | collective-permute-start | bytes 884744 | tf_op jit(solution)/shard_map/ppermute | solution.py:716
  80.1 8.6 %collective-permute-start.8 = (f32[8,72,128]{2,1,0:T(8,128)S(1)}, f32[8,72,128]{2,1,0:T(8,128)S(1)}, u32[]{:S(2)}, u32[]{:S(2)}) collective-permute-start(f32[8,72,128]{2,1,0:T(8,128)S(1)} %bitcast.49), channel_id=1, source_target_pairs={{0,2},{1,15},{2,4},{3,1},{4,6},{5,3},{6,8},{7,5},{8,10},{9,7},{10,... | collective-permute-start | bytes 884744 | tf_op jit(solution)/shard_map/ppermute | solution.py:611
  80.1 10.6 %collective-permute-start.9 = (f32[8,72,128]{2,1,0:T(8,128)S(1)}, f32[8,72,128]{2,1,0:T(8,128)S(1)}, u32[]{:S(2)}, u32[]{:S(2)}) collective-permute-start(f32[8,72,128]{2,1,0:T(8,128)S(1)} %bitcast.50), channel_id=1, source_target_pairs={{2,0},{15,1},{4,2},{1,3},{6,4},{3,5},{8,6},{5,7},{10,8},{7,9},{12,... | collective-permute-start | bytes 884744 | tf_op jit(solution)/shard_map/ppermute | solution.py:611
  81.6 12.3 %collective-permute-start.10 = (f32[4,72,128]{2,1,0:T(8,128)S(1)}, f32[4,72,128]{2,1,0:T(8,128)S(1)}, u32[]{:S(2)}, u32[]{:S(2)}) collective-permute-start(f32[4,72,128]{2,1,0:T(8,128)S(1)} %slice_bitcast_fusion.2), channel_id=1, source_target_pairs={{0,1},{1,0},{2,3},{3,2},{4,5},{5,4},{6,7},{7,6},{8,9},{9,8},{10,11... | collective-permute-start | bytes 442376 | tf_op jit(solution)/shard_map/ppermute | solution.py:551
  105.3 22.9 %collective-permute-start.12 = (f32[8,72,128]{2,1,0:T(8,128)S(1)}, f32[8,72,128]{2,1,0:T(8,128)S(1)}, u32[]{:S(2)}, u32[]{:S(2)}) collective-permute-start(f32[8,72,128]{2,1,0:T(8,128)S(1)} %bitcast.54), channel_id=1, source_target_pairs={{2,0},{15,1},{4,2},{1,3},{6,4},{3,5},{8,6},{5,7},{10,8},{7,9},{12,... | collective-permute-start | bytes 884744 | tf_op jit(solution)/shard_map/ppermute | solution.py:704
  105.6 22.6 %collective-permute-start.11 = (f32[8,72,128]{2,1,0:T(8,128)S(1)}, f32[8,72,128]{2,1,0:T(8,128)S(1)}, u32[]{:S(2)}, u32[]{:S(2)}) collective-permute-start(f32[8,72,128]{2,1,0:T(8,128)S(1)} %bitcast.55), channel_id=1, source_target_pairs={{0,2},{1,15},{2,4},{3,1},{4,6},{5,3},{6,8},{7,5},{8,10},{9,7},{10,... | collective-permute-start | bytes 884744 | tf_op jit(solution)/shard_map/ppermute | solution.py:700
  130.5 1.5 %collective-permute-start.13 = (f32[4,72,128]{2,1,0:T(8,128)S(1)}, f32[4,72,128]{2,1,0:T(8,128)S(1)}, u32[]{:S(2)}, u32[]{:S(2)}) collective-permute-start(f32[4,72,128]{2,1,0:T(8,128)S(1)} %slice_bitcast_fusion), channel_id=1, source_target_pairs={{0,1},{1,0},{2,3},{3,2},{4,5},{5,4},{6,7},{7,6},{8,9},{9,8},{10,11... | collective-permute-start | bytes 442376 | tf_op jit(solution)/shard_map/ppermute | solution.py:551

commit v5 on v4

--- a/solution.py
+++ b/solution.py
@@ -116,7 +116,15 @@
     return result[0] if single else result
 
 
-def mask_kernel(atom, values, tile_map, out):
+def mask_kernel(atom, values_hbm, tile_map_hbm, out, values, tile_map, sems):
+    copies = [
+        pltpu.make_async_copy(source, target, sems.at[k])
+        for k, (source, target) in enumerate([(values_hbm, values), (tile_map_hbm, tile_map)])
+    ]
+    for copy in copies:
+        copy.start()
+    for copy in copies:
+        copy.wait()
     reach = tile_map[pl.ds(atom[0], 1)].astype(f32)
     row = lax.broadcasted_iota(jnp.int32, (ROWS, ROWS), 0)
     lane = lax.broadcasted_iota(jnp.int32, (ROWS, ROWS), 1)
@@ -451,14 +459,17 @@
 def combine(out, start, basis, potential, table):
     def tile(i, carry):
         rows = pl.ds(pl.multiple_of(i * 8, 8), 8)
-        for plane in range(2):
-            v = potential[plane, rows]
-            total = start(plane, rows)
-            for j in range(PRJ):
+        totals = [start(plane, rows) for plane in range(2)]
+        v = [potential[plane, rows] for plane in range(2)]
+        for j in range(PRJ):
+            by_wide = [table[j, 0, q] for q in range(4)]
+            by_beta = [table[j, 1, q] for q in range(4)]
+            for plane, total in enumerate(totals):
                 beta = basis[plane][j, rows]
-                wide = basis[2 + plane][j, rows] + v * beta
+                wide = basis[2 + plane][j, rows] + v[plane] * beta
                 for q in range(4):
-                    total[q] = total[q] + table[j, 0, q] * wide + table[j, 1, q] * beta
+                    total[q] = total[q] + by_wide[q] * wide + by_beta[q] * beta
+        for plane, total in enumerate(totals):
             for q in range(4):
                 out[plane, q, rows] = total[q]
         return carry
@@ -575,12 +586,19 @@
     atom = (band // PRJ_ATOM).astype(jnp.int32).reshape(1)
     odd = (band % 2).astype(jnp.int32).reshape(1)
 
-    payload = call(
+    far_memory = pl.BlockSpec(memory_space=pltpu.HBM)
+    payload = pl.pallas_call(
         mask_kernel,
-        rows_shape,
-        [atom, projector_tiles.reshape(plane_shape), tile_map.reshape(4, ROWS)],
-        scalars=1,
-    )
+        out_shape=jax.ShapeDtypeStruct(rows_shape, f32),
+        in_specs=[SMEM, far_memory, far_memory],
+        out_specs=VMEM,
+        scratch_shapes=[
+            pltpu.VMEM(plane_shape, f32),
+            pltpu.VMEM((4, ROWS), jnp.int32),
+            pltpu.SemaphoreType.DMA((2,)),
+        ],
+        compiler_params=params(60),
+    )(atom, projector_tiles.reshape(plane_shape), tile_map.reshape(4, ROWS))
     basis_own = lax.all_to_all(payload, "band", 0, 0, tiled=True)
 
     kept, given, own = call(

time: 133 us -> 133 us (level)
  local copies, waits for them, and re-layouts: 8.38 us -> 6.95 us
    pallas_call x0 -> x1, Pallas kernels: none -> 1.77 us  [body(): pl.pallas_call(mask_kernel, out_shape=jax.ShapeDtypeStruct(rows_shape, f3...]
    unnamed x32 -> x28, local copies, waits for them, and re-layouts: 8.28 us -> 6.84 us
    pallas_call x18 -> x17, Pallas kernels: 31 us -> 30.1 us  [call(): pl.pallas_call(kernel, out_shape=shapes, in_specs=specs, out_specs=[VMEM]...]
where the time goes in v5:
time: 133 us; the launch traced here: 132 us
  blocking collectives  36.5 us (27%)
  Pallas kernels  31.8 us (24%)
  starting transfers between devices  27.4 us (21%)
  waiting for transfers between devices  26.5 us (20%)
  local copies, waits for them, and re-layouts  6.95 us (5%)
  other arithmetic  2.03 us (2%)
    pallas_call x17, Pallas kernels, call(): pl.pallas_call(kernel, out_shape=shapes, in_specs=specs, out_specs=[VMEM]...  30.1 us
    all_to_all x2, blocking collectives, body(): received = lax.all_to_all(part, 'space', 0, 0, tiled=True)  19 us
    all_to_all x1, blocking collectives, finish(): shared = lax.all_to_all(parts, 'band', 0, 0, tiled=True)  17.5 us
    all_to_all x1, starting transfers between devices, body(): basis_own = lax.all_to_all(payload, 'band', 0, 0, tiled=True)  11.8 us
    ppermute x1, waiting for transfers between devices, body(): near = lax.ppermute(near_message, 'space', from_near)  7.92 us
    ppermute x2, waiting for transfers between devices, finish(): far = lax.ppermute(flat, 'space', from_far)  7.37 us
    unnamed x28, local copies, waits for them, and re-layouts  6.84 us
    ppermute x5, starting transfers between devices, swap_core(): return lax.ppermute(x, 'space', [(i, i ^ 1) for i in range(16)])  6.12 us
  transfers between devices with their start and end apart: 15, of which 7 were waited for; matrix products, arithmetic and copies ran while one was open for 1% of the time, Pallas kernels for 14%

profile of v5, /device:TPU:1, one launch (start us, length us, event | category | flops | bytes accessed | tf_op | source)
XLA Modules:
  0.0 132.1 jit_solution(2955375003345086990)
XLA Ops:
  0.7 1.8 %shard_map.138 = f32[16,72,128]{2,1,0:T(8,128)} custom-call(s32[1]{0:T(128)} %bitcast.2.atom, f32[72,128]{1,0:T(8,128)} %bitcast.64, s32[4,72]{1,0:T(4,128)} %bitcast.65), custom_call_target="tpu_custom_call" | custom-call | tf_op jit(solution)/shard_map/pallas_call | solution.py:590
  2.4 11.8 %all-to-all-start = ((f32[16,72,128]{2,1,0:T(8,128)}), f32[16,72,128]{2,1,0:T(8,128)S(1)}, u32[]{:S(2)}, u32[]{:S(2)}) async-start(f32[16,72,128]{2,1,0:T(8,128)} %shard_map.138), calls=%async_computation | async-start | bytes 1179648 | tf_op jit(solution)/shard_map/all_to_all | solution.py:602
  14.3 0.9 copy-done.7
  15.2 0.9 copy-done.8
  16.1 0.8 copy-done.9
  16.9 0.8 copy-done.10
  17.7 0.6 shard_map.139
  18.2 1.0 collective-permute-start
  19.3 1.1 collective-permute-done.other
  20.5 2.7 %collective-permute-start.1 = (f32[10,72,128]{2,1,0:T(8,128)S(1)}, f32[10,72,128]{2,1,0:T(8,128)S(1)}, u32[]{:S(2)}, u32[]{:S(2)}) collective-permute-start(f32[10,72,128]{2,1,0:T(8,128)S(1)} %get-tuple-element.69), channel_id=1, source_target_pairs={{0,2},{1,15},{2,4},{3,1},{4,6},{5,3},{6,8},{7,5},{8,10},{9,7},{10,... | collective-permute-start | bytes 1105928 | tf_op jit(solution)/shard_map/ppermute | solution.py:631
  23.1 7.9 %collective-permute-done.1.near = f32[10,72,128]{2,1,0:T(8,128)S(1)} collective-permute-done((f32[10,72,128]{2,1,0:T(8,128)S(1)}, f32[10,72,128]{2,1,0:T(8,128)S(1)}, u32[]{:S(2)}, u32[]{:S(2)}) %collective-permute-start.1) | collective-permute-done | bytes 368672 | tf_op jit(solution)/shard_map/ppermute | solution.py:631
  31.1 0.8 copy-done.3
  31.8 3.8 %collective-permute-done.2.far = f32[10,72,128]{2,1,0:T(8,128)S(1)} collective-permute-done((f32[10,72,128]{2,1,0:T(8,128)S(1)}, f32[10,72,128]{2,1,0:T(8,128)S(1)}, u32[]{:S(2)}, u32[]{:S(2)}) %collective-permute-start.2) | collective-permute-done | bytes 368672 | tf_op jit(solution)/shard_map/ppermute | solution.py:632
  35.6 0.7 copy-done.5
  36.4 1.0 copy-done.4
  37.4 1.0 copy-done.6
  38.4 2.2 %shard_map.141 = (f32[2,4,72,128]{3,2,1,0:T(8,128)S(1)}, f32[2,4,72,128]{3,2,1,0:T(8,128)S(1)}, f32[4,72,128]{2,1,0:T(8,128)S(1)}, f32[4,72,128]{2,1,0:T(8,128)S(1)}) custom-call(f32[2]{0:T(128)S(1)} %pad_maximum_fusion.flags, f32[10,72,128]{2,1,0:T(8,128)S(1)} %copy-done.4, f32[10,72,128]{2,1,0:T(8,128)S(1)} %copy-done.6, ...), custom_call_target="tpu_custom_call" | custom-call | tf_op jit(solution)/shard_map/pallas_call | solution.py:107
  40.6 1.8 %shard_map.142 = (f32[16,128]{1,0:T(8,128)S(1)}, bf16[32,9216]{1,0:T(8,128)(2,1)S(1)}) custom-call(f32[576,128]{1,0:T(8,128)S(1)} %bitcast.51, f32[576,128]{1,0:T(8,128)S(1)} %bitcast.53, f32[576,128]{1,0:T(8,128)S(1)} %bitcast.52, f32[1152,128]{1,0:T(8,128)S(1)} %bitcast.41, f32[1152,128]{1,0:T(8,128)S(1)} %bitcast.44), custom_call_target="tpu_custom_call" | custom-call | tf_op jit(solution)/shard_map/pallas_call | solution.py:107
  42.4 3.6 %collective-permute-done.3.basis_near = f32[16,72,128]{2,1,0:T(8,128)S(1)} collective-permute-done((f32[16,72,128]{2,1,0:T(8,128)S(1)}, f32[16,72,128]{2,1,0:T(8,128)S(1)}, u32[]{:S(2)}, u32[]{:S(2)}) %collective-permute-start.3) | collective-permute-done | bytes 589856 | tf_op jit(solution)/shard_map/ppermute | solution.py:637
  46.0 1.7 %shard_map.143.own_k = f32[16,72,128]{2,1,0:T(8,128)S(1)} custom-call(f32[16,72,128]{2,1,0:T(8,128)S(1)} %all-to-all-done.basis.own, f32[16,72,128]{2,1,0:T(8,128)S(1)} %collective-permute-done.4.basis_other.other, f32[16,72,128]{2,1,0:T(8,128)S(1)} %collective-permute-done.3.basis_near, s32[72,128]{1,0:T(8,128)S(1)} %copy-done), custom_call_target="tpu_custom_call" | custom-call | tf_op jit(solution)/shard_map/pallas_call | solution.py:107
  47.7 2.4 %collective-permute-start.5 = (f32[16,72,128]{2,1,0:T(8,128)S(1)}, f32[16,72,128]{2,1,0:T(8,128)S(1)}, u32[]{:S(2)}, u32[]{:S(2)}) collective-permute-start(f32[16,72,128]{2,1,0:T(8,128)S(1)} %shard_map.143.own_k), channel_id=1, source_target_pairs={{0,1},{1,0},{2,3},{3,2},{4,5},{5,4},{6,7},{7,6},{8,9},{9,8},{10,11... | collective-permute-start | bytes 1769480 | tf_op jit(solution)/shard_map/ppermute | solution.py:562
  50.1 1.6 %shard_map.144.gram = f32[16,128]{1,0:T(8,128)S(1)} custom-call(f32[1152,128]{1,0:T(8,128)S(1)} %bitcast.42, f32[1152,128]{1,0:T(8,128)S(1)} %bitcast.46, f32[4,72,128]{2,1,0:T(8,128)S(1)} %get-tuple-element.94.early.potential, f32[4,72,128]{2,1,0:T(8,128)S(1)} %get-tuple-element.113.late.potential), custom_call_target="tpu_custom_call" | custom-call | tf_op jit(solution)/shard_map/pallas_call | solution.py:107
  51.7 1.2 shard_map.145
  52.9 10.3 %all_to_all.20.received = f32[16,16,128]{2,1,0:T(8,128)S(1)} all-to-all(f32[16,16,128]{2,1,0:T(8,128)S(1)} %shard_map.145), channel_id=1, replica_groups=mesh['band'=16,'space'=16] {'space'}, dimensions={0} | all-to-all | bytes 262144 | tf_op jit(solution)/shard_map/all_to_all | solution.py:691
  63.2 2.1 %shard_map.146 = (f32[2,4,72,128]{3,2,1,0:T(8,128)S(1)}, f32[2,8,128]{2,1,0:T(8,128)S(1)}, f32[16,128]{1,0:T(8,128)S(1)}) custom-call(f32[2]{0:T(128)S(1)} %pad_maximum_fusion.flags, f32[16,16,128]{2,1,0:T(8,128)S(1)} %all_to_all.20.received, f32[1,128]{1,0:T(1,128)S(1)} %pad_bitcast_fusion.strengths, f32[2,4,72,128]{3,2,1,0:T(8,128)S(1)} %get-tuple-element.93.second, ...), custom_call_target="tpu_custom_call" | custom-call | tf_op jit(solution)/shard_map/pallas_call | solution.py:107
  65.3 1.1 collective-permute-start.6
  66.5 1.7 %shard_map.147.partial = f32[2,4,72,128]{3,2,1,0:T(8,128)S(1)} custom-call(f32[2]{0:T(128)S(1)} %pad_maximum_fusion.flags, f32[2,4,72,128]{3,2,1,0:T(8,128)S(1)} %get-tuple-element.96.center, f32[2,4,72,128]{3,2,1,0:T(8,128)S(1)} %copy-done.2, f32[2,4,72,128]{3,2,1,0:T(8,128)S(1)} %get-tuple-element.93.second, f32[16,72,128]{2,1,0:T(8,128)S(1)} %all-to-all-done.basis.own, ...), custom_call_target="tpu_custom_call" | custom-call | tf_op jit(solution)/shard_map/pallas_call | solution.py:107
  68.2 0.5 collective-permute-start.7
  68.8 1.0 multiply_sine_fusion
  69.8 7.4 %collective-permute-done.7.far = f32[8,72,128]{2,1,0:T(8,128)S(1)} collective-permute-done((f32[8,72,128]{2,1,0:T(8,128)S(1)}, f32[8,72,128]{2,1,0:T(8,128)S(1)}, u32[]{:S(2)}, u32[]{:S(2)}) %collective-permute-start.7) | collective-permute-done | bytes 294944 | tf_op jit(solution)/shard_map/ppermute | solution.py:734
  77.2 2.3 %shard_map.148.center.mine = f32[2,4,72,128]{3,2,1,0:T(8,128)S(1)} custom-call(f32[2]{0:T(128)S(1)} %pad_maximum_fusion.flags, f32[8,72,128]{2,1,0:T(8,128)S(1)} %collective-permute-done.6.near, f32[8,72,128]{2,1,0:T(8,128)S(1)} %collective-permute-done.7.far, f32[2,4,72,128]{3,2,1,0:T(8,128)S(1)} %get-tuple-element.95.center, ...), custom_call_target="tpu_custom_call" | custom-call | tf_op jit(solution)/shard_map/pallas_call | solution.py:107
  79.5 1.5 %collective-permute-start.9 = (f32[8,72,128]{2,1,0:T(8,128)S(1)}, f32[8,72,128]{2,1,0:T(8,128)S(1)}, u32[]{:S(2)}, u32[]{:S(2)}) collective-permute-start(f32[8,72,128]{2,1,0:T(8,128)S(1)} %bitcast.50), channel_id=1, source_target_pairs={{2,0},{15,1},{4,2},{1,3},{6,4},{3,5},{8,6},{5,7},{10,8},{7,9},{12,... | collective-permute-start | bytes 884744 | tf_op jit(solution)/shard_map/ppermute | solution.py:629
  81.0 2.4 %collective-permute-start.10 = (f32[4,72,128]{2,1,0:T(8,128)S(1)}, f32[4,72,128]{2,1,0:T(8,128)S(1)}, u32[]{:S(2)}, u32[]{:S(2)}) collective-permute-start(f32[4,72,128]{2,1,0:T(8,128)S(1)} %slice_bitcast_fusion.2), channel_id=1, source_target_pairs={{0,1},{1,0},{2,3},{3,2},{4,5},{5,4},{6,7},{7,6},{8,9},{9,8},{10,11... | collective-permute-start | bytes 442376 | tf_op jit(solution)/shard_map/ppermute | solution.py:562
  83.6 4.4 %shard_map.149 = (f32[24,128]{1,0:T(8,128)S(1)}, bf16[128,9216]{1,0:T(8,128)(2,1)S(1)}) custom-call(f32[2,4,72,128]{3,2,1,0:T(8,128)S(1)} %shard_map.148.center.mine, f32[4,72,128]{2,1,0:T(8,128)S(1)} %get-tuple-element.113.late.potential, f32[16,72,128]{2,1,0:T(8,128)S(1)} %all-to-all-done.basis.own, ...), custom_call_target="tpu_custom_call" | custom-call | tf_op jit(solution)/shard_map/pallas_call | solution.py:107
  88.0 2.2 %collective-permute-done.9.far = f32[8,72,128]{2,1,0:T(8,128)S(1)} collective-permute-done((f32[8,72,128]{2,1,0:T(8,128)S(1)}, f32[8,72,128]{2,1,0:T(8,128)S(1)}, u32[]{:S(2)}, u32[]{:S(2)}) %collective-permute-start.9) | collective-permute-done | bytes 294944 | tf_op jit(solution)/shard_map/ppermute | solution.py:629
  90.2 3.1 %shard_map.150 = (f32[2,4,72,128]{3,2,1,0:T(8,128)S(1)}, f32[2,4,72,128]{3,2,1,0:T(8,128)S(1)}, f32[16,8,128]{2,1,0:T(8,128)S(1)}) custom-call(f32[8,72,128]{2,1,0:T(8,128)S(1)} %collective-permute-done.8.near, f32[8,72,128]{2,1,0:T(8,128)S(1)} %collective-permute-done.9.far, f32[2,4,72,128]{3,2,1,0:T(8,128)S(1)} %shard_map.148.center.mine, ...), custom_call_target="tpu_custom_call" | custom-call | tf_op jit(solution)/shard_map/pallas_call | solution.py:107
  93.3 8.7 %all_to_all.21.received = f32[16,8,128]{2,1,0:T(8,128)S(1)} all-to-all(f32[16,8,128]{2,1,0:T(8,128)S(1)} %get-tuple-element.107), channel_id=1, replica_groups=mesh['band'=16,'space'=16] {'space'}, dimensions={0} | all-to-all | bytes 131072 | tf_op jit(solution)/shard_map/all_to_all | solution.py:762
  102.0 2.0 %shard_map.151 = (f32[2,4,72,128]{3,2,1,0:T(8,128)S(1)}, f32[2,8,128]{2,1,0:T(8,128)S(1)}) custom-call(f32[2]{0:T(128)S(1)} %pad_maximum_fusion.flags, f32[16,8,128]{2,1,0:T(8,128)S(1)} %all_to_all.21.received, f32[1,128]{1,0:T(1,128)S(1)} %pad_bitcast_fusion.strengths, f32[2,4,72,128]{3,2,1,0:T(8,128)S(1)} %get-tuple-element.112.second, ...), custom_call_target="tpu_custom_call" | custom-call | tf_op jit(solution)/shard_map/pallas_call | solution.py:107
  104.0 0.6 shard_map.152
  104.7 0.4 collective-permute-start.12
  105.1 3.3 %collective-permute-start.11 = (f32[8,72,128]{2,1,0:T(8,128)S(1)}, f32[8,72,128]{2,1,0:T(8,128)S(1)}, u32[]{:S(2)}, u32[]{:S(2)}) collective-permute-start(f32[8,72,128]{2,1,0:T(8,128)S(1)} %bitcast.55), channel_id=1, source_target_pairs={{0,2},{1,15},{2,4},{3,1},{4,6},{5,3},{6,8},{7,5},{8,10},{9,7},{10,... | collective-permute-start | bytes 884744 | tf_op jit(solution)/shard_map/ppermute | solution.py:718
  108.3 17.5 %all_to_all.22.received = f32[16,8,128]{2,1,0:T(8,128)S(1)} all-to-all(f32[16,8,128]{2,1,0:T(8,128)S(1)} %shard_map.152), channel_id=1, replica_groups=mesh['band'=16,'space'=16] {'band'}, dimensions={0} | all-to-all | bytes 131072 | tf_op jit(solution)/shard_map/all_to_all | solution.py:723
  125.9 1.7 %shard_map.153.partial = f32[2,4,72,128]{3,2,1,0:T(8,128)S(1)} custom-call(f32[2]{0:T(128)S(1)} %pad_maximum_fusion.flags, f32[2,4,72,128]{3,2,1,0:T(8,128)S(1)} %shard_map.148.center.mine, f32[2,4,72,128]{3,2,1,0:T(8,128)S(1)} %get-tuple-element.121.first, f32[2,4,72,128]{3,2,1,0:T(8,128)S(1)} %get-tuple-element.112.second, ...), custom_call_target="tpu_custom_call" | custom-call | tf_op jit(solution)/shard_map/pallas_call | solution.py:107
  127.6 2.2 %shard_map.154 = f32[2,4,72,128]{3,2,1,0:T(8,128)S(1)} custom-call(f32[2]{0:T(128)S(1)} %pad_maximum_fusion.flags, f32[8,72,128]{2,1,0:T(8,128)S(1)} %collective-permute-done.11.near, f32[8,72,128]{2,1,0:T(8,128)S(1)} %collective-permute-done.12.far, f32[2,4,72,128]{3,2,1,0:T(8,128)S(1)} %get-tuple-element.117.center, ...), custom_call_target="tpu_custom_call" | custom-call | tf_op jit(solution)/shard_map/pallas_call | solution.py:107
  129.9 0.3 collective-permute-start.13
  130.2 0.7 shard_map.155
  130.9 0.5 collective-permute-done.13
  131.4 0.7 fusion
  (41 shorter events, 0.6 us)
Async XLA Ops:
  0.6 35.7 %copy-start = (s32[72,128]{1,0:T(8,128)S(1)}, s32[72,128]{1,0:T(8,128)}, u32[]{:S(2)}) copy-start(s32[72,128]{1,0:T(8,128)} %constant.64.clone.column) | copy-start | bytes 110596
  2.4 33.9 %all-to-all-start = ((f32[16,72,128]{2,1,0:T(8,128)}), f32[16,72,128]{2,1,0:T(8,128)S(1)}, u32[]{:S(2)}, u32[]{:S(2)}) async-start(f32[16,72,128]{2,1,0:T(8,128)} %shard_map.138), calls=%async_computation | async-start | bytes 1179648 | tf_op jit(solution)/shard_map/all_to_all | solution.py:602
  14.3 0.9 copy-start.7
  15.2 0.9 copy-start.8
  16.1 0.8 copy-start.9
  16.9 0.8 copy-start.10
  18.2 2.1 %collective-permute-start = (f32[6,72,128]{2,1,0:T(8,128)S(1)}, f32[6,72,128]{2,1,0:T(8,128)S(1)}, u32[]{:S(2)}, u32[]{:S(2)}) collective-permute-start(f32[6,72,128]{2,1,0:T(8,128)S(1)} %get-tuple-element.68), channel_id=1, source_target_pairs={{0,1},{1,0},{2,3},{3,2},{4,5},{5,4},{6,7},{7,6},{8,9},{9,8},{10,11... | collective-permute-start | bytes 663560 | tf_op jit(solution)/shard_map/ppermute | solution.py:562
  20.5 10.6 %collective-permute-start.1 = (f32[10,72,128]{2,1,0:T(8,128)S(1)}, f32[10,72,128]{2,1,0:T(8,128)S(1)}, u32[]{:S(2)}, u32[]{:S(2)}) collective-permute-start(f32[10,72,128]{2,1,0:T(8,128)S(1)} %get-tuple-element.69), channel_id=1, source_target_pairs={{0,2},{1,15},{2,4},{3,1},{4,6},{5,3},{6,8},{7,5},{8,10},{9,7},{10,... | collective-permute-start | bytes 1105928 | tf_op jit(solution)/shard_map/ppermute | solution.py:631
  23.1 12.5 %collective-permute-start.2 = (f32[10,72,128]{2,1,0:T(8,128)S(1)}, f32[10,72,128]{2,1,0:T(8,128)S(1)}, u32[]{:S(2)}, u32[]{:S(2)}) collective-permute-start(f32[10,72,128]{2,1,0:T(8,128)S(1)} %get-tuple-element.70), channel_id=1, source_target_pairs={{2,0},{15,1},{4,2},{1,3},{6,4},{3,5},{8,6},{5,7},{10,8},{7,9},{12,... | collective-permute-start | bytes 1105928 | tf_op jit(solution)/shard_map/ppermute | solution.py:632
  31.0 0.8 copy-start.3
  35.6 0.7 copy-start.5
  36.4 4.2 %collective-permute-start.4 = (f32[16,72,128]{2,1,0:T(8,128)S(1)}, f32[16,72,128]{2,1,0:T(8,128)S(1)}, u32[]{:S(2)}, u32[]{:S(2)}) collective-permute-start(f32[16,72,128]{2,1,0:T(8,128)S(1)} %all-to-all-done.basis.own), channel_id=1, source_target_pairs={{0,1},{1,0},{2,3},{3,2},{4,5},{5,4},{6,7},{7,6},{8,9},{9,8},{10,11... | collective-permute-start | bytes 1769480 | tf_op jit(solution)/shard_map/ppermute | solution.py:562
  36.4 9.6 %collective-permute-start.3 = (f32[16,72,128]{2,1,0:T(8,128)S(1)}, f32[16,72,128]{2,1,0:T(8,128)S(1)}, u32[]{:S(2)}, u32[]{:S(2)}) collective-permute-start(f32[16,72,128]{2,1,0:T(8,128)S(1)} %all-to-all-done.basis.own), channel_id=1, source_target_pairs={{0,15},{1,2},{2,1},{3,4},{4,3},{5,6},{6,5},{7,8},{8,7},{9,10},{10,... | collective-permute-start | bytes 1769480 | tf_op jit(solution)/shard_map/ppermute | solution.py:637
  36.4 1.0 copy-start.4
  37.4 1.0 copy-start.6
  40.6 5.4 %copy-start.1 = (f32[2,4,72,128]{3,2,1,0:T(8,128)}, f32[2,4,72,128]{3,2,1,0:T(8,128)S(1)}, u32[]{:S(2)}) copy-start(f32[2,4,72,128]{3,2,1,0:T(8,128)S(1)} %get-tuple-element.97.first) | copy-start | bytes 884740
  47.7 4.0 %collective-permute-start.5 = (f32[16,72,128]{2,1,0:T(8,128)S(1)}, f32[16,72,128]{2,1,0:T(8,128)S(1)}, u32[]{:S(2)}, u32[]{:S(2)}) collective-permute-start(f32[16,72,128]{2,1,0:T(8,128)S(1)} %shard_map.143.own_k), channel_id=1, source_target_pairs={{0,1},{1,0},{2,3},{3,2},{4,5},{5,4},{6,7},{7,6},{8,9},{9,8},{10,11... | collective-permute-start | bytes 1769480 | tf_op jit(solution)/shard_map/ppermute | solution.py:562
  50.1 13.1 %copy-start.12 = (s32[3,4]{1,0:T(4,128)S(1)}, s32[3,4]{1,0:T(4,128)}, u32[]{:S(2)}) copy-start(s32[3,4]{1,0:T(4,128)} %param.18) | copy-start | bytes 148
  50.1 13.1 %copy-start.13 = (f32[16]{0:T(128)S(1)}, f32[16]{0:T(128)}, u32[]{:S(2)}) copy-start(f32[16]{0:T(128)} %param.17) | copy-start | bytes 196
  63.2 3.3 %copy-start.2 = (f32[2,4,72,128]{3,2,1,0:T(8,128)S(1)}, f32[2,4,72,128]{3,2,1,0:T(8,128)}, u32[]{:S(2)}) copy-start(f32[2,4,72,128]{3,2,1,0:T(8,128)} %copy-done.1) | copy-start | bytes 884740
  65.3 3.5 %copy-start.11 = (s32[72,128]{1,0:T(8,128)S(1)}, s32[72,128]{1,0:T(8,128)}, u32[]{:S(2)}) copy-start(s32[72,128]{1,0:T(8,128)} %constant.75) | copy-start | bytes 110596
  65.3 11.9 %collective-permute-start.6 = (f32[8,72,128]{2,1,0:T(8,128)S(1)}, f32[8,72,128]{2,1,0:T(8,128)S(1)}, u32[]{:S(2)}, u32[]{:S(2)}) collective-permute-start(f32[8,72,128]{2,1,0:T(8,128)S(1)} %bitcast.56), channel_id=1, source_target_pairs={{0,2},{1,15},{2,4},{3,1},{4,6},{5,3},{6,8},{7,5},{8,10},{9,7},{10,... | collective-permute-start | bytes 884744 | tf_op jit(solution)/shard_map/ppermute | solution.py:718
  68.2 9.0 %collective-permute-start.7 = (f32[8,72,128]{2,1,0:T(8,128)S(1)}, f32[8,72,128]{2,1,0:T(8,128)S(1)}, u32[]{:S(2)}, u32[]{:S(2)}) collective-permute-start(f32[8,72,128]{2,1,0:T(8,128)S(1)} %bitcast.57), channel_id=1, source_target_pairs={{2,0},{15,1},{4,2},{1,3},{6,4},{3,5},{8,6},{5,7},{10,8},{7,9},{12,... | collective-permute-start | bytes 884744 | tf_op jit(solution)/shard_map/ppermute | solution.py:734
  79.5 8.6 %collective-permute-start.8 = (f32[8,72,128]{2,1,0:T(8,128)S(1)}, f32[8,72,128]{2,1,0:T(8,128)S(1)}, u32[]{:S(2)}, u32[]{:S(2)}) collective-permute-start(f32[8,72,128]{2,1,0:T(8,128)S(1)} %bitcast.49), channel_id=1, source_target_pairs={{0,2},{1,15},{2,4},{3,1},{4,6},{5,3},{6,8},{7,5},{8,10},{9,7},{10,... | collective-permute-start | bytes 884744 | tf_op jit(solution)/shard_map/ppermute | solution.py:629
  79.5 10.7 %collective-permute-start.9 = (f32[8,72,128]{2,1,0:T(8,128)S(1)}, f32[8,72,128]{2,1,0:T(8,128)S(1)}, u32[]{:S(2)}, u32[]{:S(2)}) collective-permute-start(f32[8,72,128]{2,1,0:T(8,128)S(1)} %bitcast.50), channel_id=1, source_target_pairs={{2,0},{15,1},{4,2},{1,3},{6,4},{3,5},{8,6},{5,7},{10,8},{7,9},{12,... | collective-permute-start | bytes 884744 | tf_op jit(solution)/shard_map/ppermute | solution.py:629
  81.0 12.3 %collective-permute-start.10 = (f32[4,72,128]{2,1,0:T(8,128)S(1)}, f32[4,72,128]{2,1,0:T(8,128)S(1)}, u32[]{:S(2)}, u32[]{:S(2)}) collective-permute-start(f32[4,72,128]{2,1,0:T(8,128)S(1)} %slice_bitcast_fusion.2), channel_id=1, source_target_pairs={{0,1},{1,0},{2,3},{3,2},{4,5},{5,4},{6,7},{7,6},{8,9},{9,8},{10,11... | collective-permute-start | bytes 442376 | tf_op jit(solution)/shard_map/ppermute | solution.py:562
  104.7 22.9 %collective-permute-start.12 = (f32[8,72,128]{2,1,0:T(8,128)S(1)}, f32[8,72,128]{2,1,0:T(8,128)S(1)}, u32[]{:S(2)}, u32[]{:S(2)}) collective-permute-start(f32[8,72,128]{2,1,0:T(8,128)S(1)} %bitcast.54), channel_id=1, source_target_pairs={{2,0},{15,1},{4,2},{1,3},{6,4},{3,5},{8,6},{5,7},{10,8},{7,9},{12,... | collective-permute-start | bytes 884744 | tf_op jit(solution)/shard_map/ppermute | solution.py:722
  105.1 22.6 %collective-permute-start.11 = (f32[8,72,128]{2,1,0:T(8,128)S(1)}, f32[8,72,128]{2,1,0:T(8,128)S(1)}, u32[]{:S(2)}, u32[]{:S(2)}) collective-permute-start(f32[8,72,128]{2,1,0:T(8,128)S(1)} %bitcast.55), channel_id=1, source_target_pairs={{0,2},{1,15},{2,4},{3,1},{4,6},{5,3},{6,8},{7,5},{8,10},{9,7},{10,... | collective-permute-start | bytes 884744 | tf_op jit(solution)/shard_map/ppermute | solution.py:718
  129.9 1.5 %collective-permute-start.13 = (f32[4,72,128]{2,1,0:T(8,128)S(1)}, f32[4,72,128]{2,1,0:T(8,128)S(1)}, u32[]{:S(2)}, u32[]{:S(2)}) collective-permute-start(f32[4,72,128]{2,1,0:T(8,128)S(1)} %slice_bitcast_fusion), channel_id=1, source_target_pairs={{0,1},{1,0},{2,3},{3,2},{4,5},{5,4},{6,7},{7,6},{8,9},{9,8},{10,11... | collective-permute-start | bytes 442376 | tf_op jit(solution)/shard_map/ppermute | solution.py:562

commit v6 on v5

--- a/solution.py
+++ b/solution.py
@@ -366,7 +366,7 @@
 
 
 def middle_moments_kernel(
-    center, potential, own, other, own_k, other_k, wave_x, wave_y, wave_z, out, basis_flat
+    center, potential, own, other, own_k, other_k, wave_x, wave_y, wave_z, out
 ):
     kinds = [
         (center, None),
@@ -376,8 +376,10 @@
         (center, lambda plane, j, beta: beta * wave_z[j // PRJ_ATOM]),
     ]
     out[...] = project((own, other, own_k, other_k), potential, kinds, 24)
-    flat = [x.reshape(PRJ * ROWS, LANES) for x in (own, other, own_k, other_k)]
-    put_basis(*flat, potential, basis_flat)
+
+
+def basis_kernel(own, other, own_k, other_k, potential, out):
+    put_basis(own, other, own_k, other_k, potential, out)
 
 
 def second_kernel(
@@ -741,11 +743,20 @@
         )
 
     _, mid = finish(center, first, second, early, u2, rest)
-    near, far = exchange(mid)
+    flat = mid.reshape((8,) + plane_shape)
+    near = lax.ppermute(flat, "space", from_near)
+    flat, late = fence(flat, late)
+    basis_flat = call(
+        basis_kernel,
+        jax.ShapeDtypeStruct((128, ROWS * LANES), jnp.bfloat16),
+        [x.reshape(flat_shape) for x in basis] + [late],
+    )
+    flat, basis_flat = fence(flat, basis_flat)
+    far = lax.ppermute(flat, "space", from_far)
     yours = swap_core(mid[1])
-    known, basis_flat = call(
+    known = call(
         middle_moments_kernel,
-        [(24, LANES), jax.ShapeDtypeStruct((128, ROWS * LANES), jnp.bfloat16)],
+        (24, LANES),
         [mid, late] + basis + [wave_x, wave_y, wave_z],
     )
     first, second, part = call(

time: 133 us -> 134 us (level)
    pallas_call x17 -> x18, Pallas kernels: 30.1 us -> 30.1 us  [call(): pl.pallas_call(kernel, out_shape=shapes, in_specs=specs, out_specs=[VMEM]...]
  transfers between devices with their start and end apart: 15 -> 15, of which waited for: 7 -> 7; matrix products, arithmetic and copies ran while one was open for 1% -> 1% of each run, Pallas kernels for 14% -> 13%
where the time goes in v6:
time: 134 us; the launch traced here: 133 us
  blocking collectives  37.4 us (28%)
  Pallas kernels  31.9 us (24%)
  starting transfers between devices  27.4 us (20%)
  waiting for transfers between devices  26.5 us (20%)
  local copies, waits for them, and re-layouts  6.95 us (5%)
  other arithmetic  2.03 us (2%)
    pallas_call x18, Pallas kernels, call(): pl.pallas_call(kernel, out_shape=shapes, in_specs=specs, out_specs=[VMEM]...  30.1 us
    all_to_all x2, blocking collectives, body(): received = lax.all_to_all(part, 'space', 0, 0, tiled=True)  19.9 us
    all_to_all x1, blocking collectives, finish(): shared = lax.all_to_all(parts, 'band', 0, 0, tiled=True)  17.5 us
    all_to_all x1, starting transfers between devices, body(): basis_own = lax.all_to_all(payload, 'band', 0, 0, tiled=True)  11.8 us
    ppermute x1, waiting for transfers between devices, body(): near = lax.ppermute(near_message, 'space', from_near)  7.92 us
    ppermute x2, waiting for transfers between devices, finish(): far = lax.ppermute(flat, 'space', from_far)  7.36 us
    unnamed x28, local copies, waits for them, and re-layouts  6.85 us
    ppermute x5, starting transfers between devices, swap_core(): return lax.ppermute(x, 'space', [(i, i ^ 1) for i in range(16)])  6.05 us
  transfers between devices with their start and end apart: 15, of which 7 were waited for; matrix products, arithmetic and copies ran while one was open for 1% of the time, Pallas kernels for 13%

profile of v6, /device:TPU:1, one launch (start us, length us, event | category | flops | bytes accessed | tf_op | source)
XLA Modules:
  0.0 133.0 jit_solution(5442327447543122623)
XLA Ops:
  0.7 1.8 %shard_map.138 = f32[16,72,128]{2,1,0:T(8,128)} custom-call(s32[1]{0:T(128)} %bitcast.2.atom, f32[72,128]{1,0:T(8,128)} %bitcast.68, s32[4,72]{1,0:T(4,128)} %bitcast.69), custom_call_target="tpu_custom_call" | custom-call | tf_op jit(solution)/shard_map/pallas_call | solution.py:592
  2.5 11.8 %all-to-all-start = ((f32[16,72,128]{2,1,0:T(8,128)}), f32[16,72,128]{2,1,0:T(8,128)S(1)}, u32[]{:S(2)}, u32[]{:S(2)}) async-start(f32[16,72,128]{2,1,0:T(8,128)} %shard_map.138), calls=%async_computation | async-start | bytes 1179648 | tf_op jit(solution)/shard_map/all_to_all | solution.py:604
  14.3 0.9 copy-done.7
  15.2 0.9 copy-done.8
  16.1 0.8 copy-done.9
  16.9 0.8 copy-done.10
  17.7 0.6 shard_map.139
  18.3 1.0 collective-permute-start
  19.3 1.1 collective-permute-done.other
  20.5 2.7 %collective-permute-start.1 = (f32[10,72,128]{2,1,0:T(8,128)S(1)}, f32[10,72,128]{2,1,0:T(8,128)S(1)}, u32[]{:S(2)}, u32[]{:S(2)}) collective-permute-start(f32[10,72,128]{2,1,0:T(8,128)S(1)} %get-tuple-element.71), channel_id=1, source_target_pairs={{0,2},{1,15},{2,4},{3,1},{4,6},{5,3},{6,8},{7,5},{8,10},{9,7},{10,... | collective-permute-start | bytes 1105928 | tf_op jit(solution)/shard_map/ppermute | solution.py:633
  23.2 7.9 %collective-permute-done.1.near = f32[10,72,128]{2,1,0:T(8,128)S(1)} collective-permute-done((f32[10,72,128]{2,1,0:T(8,128)S(1)}, f32[10,72,128]{2,1,0:T(8,128)S(1)}, u32[]{:S(2)}, u32[]{:S(2)}) %collective-permute-start.1) | collective-permute-done | bytes 368672 | tf_op jit(solution)/shard_map/ppermute | solution.py:633
  31.1 0.7 copy-done.3
  31.8 3.8 %collective-permute-done.2.far = f32[10,72,128]{2,1,0:T(8,128)S(1)} collective-permute-done((f32[10,72,128]{2,1,0:T(8,128)S(1)}, f32[10,72,128]{2,1,0:T(8,128)S(1)}, u32[]{:S(2)}, u32[]{:S(2)}) %collective-permute-start.2) | collective-permute-done | bytes 368672 | tf_op jit(solution)/shard_map/ppermute | solution.py:634
  35.6 0.7 copy-done.5
  36.4 1.0 copy-done.4
  37.4 1.0 copy-done.6
  38.4 2.2 %shard_map.141 = (f32[2,4,72,128]{3,2,1,0:T(8,128)S(1)}, f32[2,4,72,128]{3,2,1,0:T(8,128)S(1)}, f32[4,72,128]{2,1,0:T(8,128)S(1)}, f32[4,72,128]{2,1,0:T(8,128)S(1)}) custom-call(f32[2]{0:T(128)S(1)} %pad_maximum_fusion.flags, f32[10,72,128]{2,1,0:T(8,128)S(1)} %copy-done.4, f32[10,72,128]{2,1,0:T(8,128)S(1)} %copy-done.6, ...), custom_call_target="tpu_custom_call" | custom-call | tf_op jit(solution)/shard_map/pallas_call | solution.py:107
  40.6 1.8 %shard_map.142 = (f32[16,128]{1,0:T(8,128)S(1)}, bf16[32,9216]{1,0:T(8,128)(2,1)S(1)}) custom-call(f32[576,128]{1,0:T(8,128)S(1)} %bitcast.55, f32[576,128]{1,0:T(8,128)S(1)} %bitcast.57, f32[576,128]{1,0:T(8,128)S(1)} %bitcast.56, f32[1152,128]{1,0:T(8,128)S(1)} %bitcast.41, f32[1152,128]{1,0:T(8,128)S(1)} %bitcast.45), custom_call_target="tpu_custom_call" | custom-call | tf_op jit(solution)/shard_map/pallas_call | solution.py:107
  42.4 3.6 %collective-permute-done.3.basis_near = f32[16,72,128]{2,1,0:T(8,128)S(1)} collective-permute-done((f32[16,72,128]{2,1,0:T(8,128)S(1)}, f32[16,72,128]{2,1,0:T(8,128)S(1)}, u32[]{:S(2)}, u32[]{:S(2)}) %collective-permute-start.3) | collective-permute-done | bytes 589856 | tf_op jit(solution)/shard_map/ppermute | solution.py:639
  46.0 1.7 %shard_map.143.own_k = f32[16,72,128]{2,1,0:T(8,128)S(1)} custom-call(f32[16,72,128]{2,1,0:T(8,128)S(1)} %all-to-all-done.basis.own, f32[16,72,128]{2,1,0:T(8,128)S(1)} %collective-permute-done.4.basis_other.other, f32[16,72,128]{2,1,0:T(8,128)S(1)} %collective-permute-done.3.basis_near, s32[72,128]{1,0:T(8,128)S(1)} %copy-done), custom_call_target="tpu_custom_call" | custom-call | tf_op jit(solution)/shard_map/pallas_call | solution.py:107
  47.7 2.4 %collective-permute-start.5 = (f32[16,72,128]{2,1,0:T(8,128)S(1)}, f32[16,72,128]{2,1,0:T(8,128)S(1)}, u32[]{:S(2)}, u32[]{:S(2)}) collective-permute-start(f32[16,72,128]{2,1,0:T(8,128)S(1)} %shard_map.143.own_k), channel_id=1, source_target_pairs={{0,1},{1,0},{2,3},{3,2},{4,5},{5,4},{6,7},{7,6},{8,9},{9,8},{10,11... | collective-permute-start | bytes 1769480 | tf_op jit(solution)/shard_map/ppermute | solution.py:564
  50.1 1.6 %shard_map.144.gram = f32[16,128]{1,0:T(8,128)S(1)} custom-call(f32[1152,128]{1,0:T(8,128)S(1)} %bitcast.42, f32[1152,128]{1,0:T(8,128)S(1)} %bitcast.48, f32[4,72,128]{2,1,0:T(8,128)S(1)} %get-tuple-element.96.early.potential, f32[4,72,128]{2,1,0:T(8,128)S(1)} %get-tuple-element.117.late.potential), custom_call_target="tpu_custom_call" | custom-call | tf_op jit(solution)/shard_map/pallas_call | solution.py:107
  51.7 1.2 shard_map.145
  52.9 10.3 %all_to_all.20.received = f32[16,16,128]{2,1,0:T(8,128)S(1)} all-to-all(f32[16,16,128]{2,1,0:T(8,128)S(1)} %shard_map.145), channel_id=1, replica_groups=mesh['band'=16,'space'=16] {'space'}, dimensions={0} | all-to-all | bytes 262144 | tf_op jit(solution)/shard_map/all_to_all | solution.py:693
  63.2 2.1 %shard_map.146 = (f32[2,4,72,128]{3,2,1,0:T(8,128)S(1)}, f32[2,8,128]{2,1,0:T(8,128)S(1)}, f32[16,128]{1,0:T(8,128)S(1)}) custom-call(f32[2]{0:T(128)S(1)} %pad_maximum_fusion.flags, f32[16,16,128]{2,1,0:T(8,128)S(1)} %all_to_all.20.received, f32[1,128]{1,0:T(1,128)S(1)} %pad_bitcast_fusion.strengths, f32[2,4,72,128]{3,2,1,0:T(8,128)S(1)} %get-tuple-element.95.second, ...), custom_call_target="tpu_custom_call" | custom-call | tf_op jit(solution)/shard_map/pallas_call | solution.py:107
  65.4 1.1 collective-permute-start.6
  66.5 1.7 %shard_map.147.partial = f32[2,4,72,128]{3,2,1,0:T(8,128)S(1)} custom-call(f32[2]{0:T(128)S(1)} %pad_maximum_fusion.flags, f32[2,4,72,128]{3,2,1,0:T(8,128)S(1)} %get-tuple-element.98.center, f32[2,4,72,128]{3,2,1,0:T(8,128)S(1)} %copy-done.2, f32[2,4,72,128]{3,2,1,0:T(8,128)S(1)} %get-tuple-element.95.second, f32[16,72,128]{2,1,0:T(8,128)S(1)} %all-to-all-done.basis.own, ...), custom_call_target="tpu_custom_call" | custom-call | tf_op jit(solution)/shard_map/pallas_call | solution.py:107
  68.2 0.5 collective-permute-start.7
  68.8 1.0 multiply_sine_fusion
  69.9 7.4 %collective-permute-done.7.far = f32[8,72,128]{2,1,0:T(8,128)S(1)} collective-permute-done((f32[8,72,128]{2,1,0:T(8,128)S(1)}, f32[8,72,128]{2,1,0:T(8,128)S(1)}, u32[]{:S(2)}, u32[]{:S(2)}) %collective-permute-start.7) | collective-permute-done | bytes 294944 | tf_op jit(solution)/shard_map/ppermute | solution.py:736
  77.2 2.3 %shard_map.148.center.mine = f32[2,4,72,128]{3,2,1,0:T(8,128)S(1)} custom-call(f32[2]{0:T(128)S(1)} %pad_maximum_fusion.flags, f32[8,72,128]{2,1,0:T(8,128)S(1)} %collective-permute-done.6.near, f32[8,72,128]{2,1,0:T(8,128)S(1)} %collective-permute-done.7.far, f32[2,4,72,128]{3,2,1,0:T(8,128)S(1)} %get-tuple-element.97.center, ...), custom_call_target="tpu_custom_call" | custom-call | tf_op jit(solution)/shard_map/pallas_call | solution.py:107
  79.6 0.9 shard_map.149.basis_flat
  80.5 1.5 %collective-permute-start.9 = (f32[8,72,128]{2,1,0:T(8,128)S(1)}, f32[8,72,128]{2,1,0:T(8,128)S(1)}, u32[]{:S(2)}, u32[]{:S(2)}) collective-permute-start(f32[8,72,128]{2,1,0:T(8,128)S(1)} %bitcast.54), channel_id=1, source_target_pairs={{2,0},{15,1},{4,2},{1,3},{6,4},{3,5},{8,6},{5,7},{10,8},{7,9},{12,... | collective-permute-start | bytes 884744 | tf_op jit(solution)/shard_map/ppermute | solution.py:755
  82.1 2.3 %collective-permute-start.10 = (f32[4,72,128]{2,1,0:T(8,128)S(1)}, f32[4,72,128]{2,1,0:T(8,128)S(1)}, u32[]{:S(2)}, u32[]{:S(2)}) collective-permute-start(f32[4,72,128]{2,1,0:T(8,128)S(1)} %slice_bitcast_fusion.2), channel_id=1, source_target_pairs={{0,1},{1,0},{2,3},{3,2},{4,5},{5,4},{6,7},{7,6},{8,9},{9,8},{10,11... | collective-permute-start | bytes 442376 | tf_op jit(solution)/shard_map/ppermute | solution.py:564
  84.6 3.5 %shard_map.150.known = f32[24,128]{1,0:T(8,128)S(1)} custom-call(f32[2,4,72,128]{3,2,1,0:T(8,128)S(1)} %shard_map.148.center.mine, f32[4,72,128]{2,1,0:T(8,128)S(1)} %get-tuple-element.117.late.potential, f32[16,72,128]{2,1,0:T(8,128)S(1)} %all-to-all-done.basis.own, f32[16,72,128]{2,1,0:T(8,128)S(1)} %collective-permute-done.4.basis_other.other, ...), custom_call_target="tpu_custom_call" | custom-call | tf_op jit(solution)/shard_map/pallas_call | solution.py:107
  88.1 2.2 %collective-permute-done.9.far = f32[8,72,128]{2,1,0:T(8,128)S(1)} collective-permute-done((f32[8,72,128]{2,1,0:T(8,128)S(1)}, f32[8,72,128]{2,1,0:T(8,128)S(1)}, u32[]{:S(2)}, u32[]{:S(2)}) %collective-permute-start.9) | collective-permute-done | bytes 294944 | tf_op jit(solution)/shard_map/ppermute | solution.py:755
  90.2 3.1 %shard_map.151 = (f32[2,4,72,128]{3,2,1,0:T(8,128)S(1)}, f32[2,4,72,128]{3,2,1,0:T(8,128)S(1)}, f32[16,8,128]{2,1,0:T(8,128)S(1)}) custom-call(f32[8,72,128]{2,1,0:T(8,128)S(1)} %collective-permute-done.8.near, f32[8,72,128]{2,1,0:T(8,128)S(1)} %collective-permute-done.9.far, f32[2,4,72,128]{3,2,1,0:T(8,128)S(1)} %shard_map.148.center.mine, ...), custom_call_target="tpu_custom_call" | custom-call | tf_op jit(solution)/shard_map/pallas_call | solution.py:107
  93.3 9.6 %all_to_all.21.received = f32[16,8,128]{2,1,0:T(8,128)S(1)} all-to-all(f32[16,8,128]{2,1,0:T(8,128)S(1)} %get-tuple-element.111), channel_id=1, replica_groups=mesh['band'=16,'space'=16] {'space'}, dimensions={0} | all-to-all | bytes 131072 | tf_op jit(solution)/shard_map/all_to_all | solution.py:773
  102.9 2.0 %shard_map.152 = (f32[2,4,72,128]{3,2,1,0:T(8,128)S(1)}, f32[2,8,128]{2,1,0:T(8,128)S(1)}) custom-call(f32[2]{0:T(128)S(1)} %pad_maximum_fusion.flags, f32[16,8,128]{2,1,0:T(8,128)S(1)} %all_to_all.21.received, f32[1,128]{1,0:T(1,128)S(1)} %pad_bitcast_fusion.strengths, f32[2,4,72,128]{3,2,1,0:T(8,128)S(1)} %get-tuple-element.116.second, ...), custom_call_target="tpu_custom_call" | custom-call | tf_op jit(solution)/shard_map/pallas_call | solution.py:107
  105.0 0.6 shard_map.153
  105.6 0.4 collective-permute-start.12
  106.0 3.3 %collective-permute-start.11 = (f32[8,72,128]{2,1,0:T(8,128)S(1)}, f32[8,72,128]{2,1,0:T(8,128)S(1)}, u32[]{:S(2)}, u32[]{:S(2)}) collective-permute-start(f32[8,72,128]{2,1,0:T(8,128)S(1)} %bitcast.59), channel_id=1, source_target_pairs={{0,2},{1,15},{2,4},{3,1},{4,6},{5,3},{6,8},{7,5},{8,10},{9,7},{10,... | collective-permute-start | bytes 884744 | tf_op jit(solution)/shard_map/ppermute | solution.py:720
  109.3 17.5 %all_to_all.22.received = f32[16,8,128]{2,1,0:T(8,128)S(1)} all-to-all(f32[16,8,128]{2,1,0:T(8,128)S(1)} %shard_map.153), channel_id=1, replica_groups=mesh['band'=16,'space'=16] {'band'}, dimensions={0} | all-to-all | bytes 131072 | tf_op jit(solution)/shard_map/all_to_all | solution.py:725
  126.8 1.7 %shard_map.154.partial = f32[2,4,72,128]{3,2,1,0:T(8,128)S(1)} custom-call(f32[2]{0:T(128)S(1)} %pad_maximum_fusion.flags, f32[2,4,72,128]{3,2,1,0:T(8,128)S(1)} %shard_map.148.center.mine, f32[2,4,72,128]{3,2,1,0:T(8,128)S(1)} %get-tuple-element.125.first, f32[2,4,72,128]{3,2,1,0:T(8,128)S(1)} %get-tuple-element.116.second, ...), custom_call_target="tpu_custom_call" | custom-call | tf_op jit(solution)/shard_map/pallas_call | solution.py:107
  128.6 2.2 %shard_map.155 = f32[2,4,72,128]{3,2,1,0:T(8,128)S(1)} custom-call(f32[2]{0:T(128)S(1)} %pad_maximum_fusion.flags, f32[8,72,128]{2,1,0:T(8,128)S(1)} %collective-permute-done.11.near, f32[8,72,128]{2,1,0:T(8,128)S(1)} %collective-permute-done.12.far, f32[2,4,72,128]{3,2,1,0:T(8,128)S(1)} %get-tuple-element.121.center, ...), custom_call_target="tpu_custom_call" | custom-call | tf_op jit(solution)/shard_map/pallas_call | solution.py:107
  131.1 0.7 shard_map.156
  131.8 0.5 collective-permute-done.13
  132.3 0.7 fusion
  (42 shorter events, 0.9 us)
Async XLA Ops:
  0.6 35.8 %copy-start = (s32[72,128]{1,0:T(8,128)S(1)}, s32[72,128]{1,0:T(8,128)}, u32[]{:S(2)}) copy-start(s32[72,128]{1,0:T(8,128)} %constant.64.clone.column) | copy-start | bytes 110596
  2.5 33.9 %all-to-all-start = ((f32[16,72,128]{2,1,0:T(8,128)}), f32[16,72,128]{2,1,0:T(8,128)S(1)}, u32[]{:S(2)}, u32[]{:S(2)}) async-start(f32[16,72,128]{2,1,0:T(8,128)} %shard_map.138), calls=%async_computation | async-start | bytes 1179648 | tf_op jit(solution)/shard_map/all_to_all | solution.py:604
  14.3 0.9 copy-start.7
  15.2 0.9 copy-start.8
  16.1 0.8 copy-start.9
  16.9 0.8 copy-start.10
  18.3 2.1 %collective-permute-start = (f32[6,72,128]{2,1,0:T(8,128)S(1)}, f32[6,72,128]{2,1,0:T(8,128)S(1)}, u32[]{:S(2)}, u32[]{:S(2)}) collective-permute-start(f32[6,72,128]{2,1,0:T(8,128)S(1)} %get-tuple-element.70), channel_id=1, source_target_pairs={{0,1},{1,0},{2,3},{3,2},{4,5},{5,4},{6,7},{7,6},{8,9},{9,8},{10,11... | collective-permute-start | bytes 663560 | tf_op jit(solution)/shard_map/ppermute | solution.py:564
  20.5 10.6 %collective-permute-start.1 = (f32[10,72,128]{2,1,0:T(8,128)S(1)}, f32[10,72,128]{2,1,0:T(8,128)S(1)}, u32[]{:S(2)}, u32[]{:S(2)}) collective-permute-start(f32[10,72,128]{2,1,0:T(8,128)S(1)} %get-tuple-element.71), channel_id=1, source_target_pairs={{0,2},{1,15},{2,4},{3,1},{4,6},{5,3},{6,8},{7,5},{8,10},{9,7},{10,... | collective-permute-start | bytes 1105928 | tf_op jit(solution)/shard_map/ppermute | solution.py:633
  23.1 12.5 %collective-permute-start.2 = (f32[10,72,128]{2,1,0:T(8,128)S(1)}, f32[10,72,128]{2,1,0:T(8,128)S(1)}, u32[]{:S(2)}, u32[]{:S(2)}) collective-permute-start(f32[10,72,128]{2,1,0:T(8,128)S(1)} %get-tuple-element.72), channel_id=1, source_target_pairs={{2,0},{15,1},{4,2},{1,3},{6,4},{3,5},{8,6},{5,7},{10,8},{7,9},{12,... | collective-permute-start | bytes 1105928 | tf_op jit(solution)/shard_map/ppermute | solution.py:634
  31.1 0.7 copy-start.3
  35.6 0.7 copy-start.5
  36.4 4.2 %collective-permute-start.4 = (f32[16,72,128]{2,1,0:T(8,128)S(1)}, f32[16,72,128]{2,1,0:T(8,128)S(1)}, u32[]{:S(2)}, u32[]{:S(2)}) collective-permute-start(f32[16,72,128]{2,1,0:T(8,128)S(1)} %all-to-all-done.basis.own), channel_id=1, source_target_pairs={{0,1},{1,0},{2,3},{3,2},{4,5},{5,4},{6,7},{7,6},{8,9},{9,8},{10,11... | collective-permute-start | bytes 1769480 | tf_op jit(solution)/shard_map/ppermute | solution.py:564
  36.4 9.6 %collective-permute-start.3 = (f32[16,72,128]{2,1,0:T(8,128)S(1)}, f32[16,72,128]{2,1,0:T(8,128)S(1)}, u32[]{:S(2)}, u32[]{:S(2)}) collective-permute-start(f32[16,72,128]{2,1,0:T(8,128)S(1)} %all-to-all-done.basis.own), channel_id=1, source_target_pairs={{0,15},{1,2},{2,1},{3,4},{4,3},{5,6},{6,5},{7,8},{8,7},{9,10},{10,... | collective-permute-start | bytes 1769480 | tf_op jit(solution)/shard_map/ppermute | solution.py:639
  36.4 1.0 copy-start.4
  37.4 1.0 copy-start.6
  40.6 5.4 %copy-start.1 = (f32[2,4,72,128]{3,2,1,0:T(8,128)}, f32[2,4,72,128]{3,2,1,0:T(8,128)S(1)}, u32[]{:S(2)}) copy-start(f32[2,4,72,128]{3,2,1,0:T(8,128)S(1)} %get-tuple-element.99.first) | copy-start | bytes 884740
  47.7 4.0 %collective-permute-start.5 = (f32[16,72,128]{2,1,0:T(8,128)S(1)}, f32[16,72,128]{2,1,0:T(8,128)S(1)}, u32[]{:S(2)}, u32[]{:S(2)}) collective-permute-start(f32[16,72,128]{2,1,0:T(8,128)S(1)} %shard_map.143.own_k), channel_id=1, source_target_pairs={{0,1},{1,0},{2,3},{3,2},{4,5},{5,4},{6,7},{7,6},{8,9},{9,8},{10,11... | collective-permute-start | bytes 1769480 | tf_op jit(solution)/shard_map/ppermute | solution.py:564
  50.1 13.1 %copy-start.12 = (s32[3,4]{1,0:T(4,128)S(1)}, s32[3,4]{1,0:T(4,128)}, u32[]{:S(2)}) copy-start(s32[3,4]{1,0:T(4,128)} %param.18) | copy-start | bytes 148
  50.1 13.1 %copy-start.13 = (f32[16]{0:T(128)S(1)}, f32[16]{0:T(128)}, u32[]{:S(2)}) copy-start(f32[16]{0:T(128)} %param.17) | copy-start | bytes 196
  63.2 3.3 %copy-start.2 = (f32[2,4,72,128]{3,2,1,0:T(8,128)S(1)}, f32[2,4,72,128]{3,2,1,0:T(8,128)}, u32[]{:S(2)}) copy-start(f32[2,4,72,128]{3,2,1,0:T(8,128)} %copy-done.1) | copy-start | bytes 884740
  65.4 3.5 %copy-start.11 = (s32[72,128]{1,0:T(8,128)S(1)}, s32[72,128]{1,0:T(8,128)}, u32[]{:S(2)}) copy-start(s32[72,128]{1,0:T(8,128)} %constant.75) | copy-start | bytes 110596
  65.4 11.9 %collective-permute-start.6 = (f32[8,72,128]{2,1,0:T(8,128)S(1)}, f32[8,72,128]{2,1,0:T(8,128)S(1)}, u32[]{:S(2)}, u32[]{:S(2)}) collective-permute-start(f32[8,72,128]{2,1,0:T(8,128)S(1)} %bitcast.60), channel_id=1, source_target_pairs={{0,2},{1,15},{2,4},{3,1},{4,6},{5,3},{6,8},{7,5},{8,10},{9,7},{10,... | collective-permute-start | bytes 884744 | tf_op jit(solution)/shard_map/ppermute | solution.py:720
  68.2 9.0 %collective-permute-start.7 = (f32[8,72,128]{2,1,0:T(8,128)S(1)}, f32[8,72,128]{2,1,0:T(8,128)S(1)}, u32[]{:S(2)}, u32[]{:S(2)}) collective-permute-start(f32[8,72,128]{2,1,0:T(8,128)S(1)} %bitcast.61), channel_id=1, source_target_pairs={{2,0},{15,1},{4,2},{1,3},{6,4},{3,5},{8,6},{5,7},{10,8},{7,9},{12,... | collective-permute-start | bytes 884744 | tf_op jit(solution)/shard_map/ppermute | solution.py:736
  79.5 10.7 %collective-permute-start.8 = (f32[8,72,128]{2,1,0:T(8,128)S(1)}, f32[8,72,128]{2,1,0:T(8,128)S(1)}, u32[]{:S(2)}, u32[]{:S(2)}) collective-permute-start(f32[8,72,128]{2,1,0:T(8,128)S(1)} %bitcast.53), channel_id=1, source_target_pairs={{0,2},{1,15},{2,4},{3,1},{4,6},{5,3},{6,8},{7,5},{8,10},{9,7},{10,... | collective-permute-start | bytes 884744 | tf_op jit(solution)/shard_map/ppermute | solution.py:747
  80.5 9.7 %collective-permute-start.9 = (f32[8,72,128]{2,1,0:T(8,128)S(1)}, f32[8,72,128]{2,1,0:T(8,128)S(1)}, u32[]{:S(2)}, u32[]{:S(2)}) collective-permute-start(f32[8,72,128]{2,1,0:T(8,128)S(1)} %bitcast.54), channel_id=1, source_target_pairs={{2,0},{15,1},{4,2},{1,3},{6,4},{3,5},{8,6},{5,7},{10,8},{7,9},{12,... | collective-permute-start | bytes 884744 | tf_op jit(solution)/shard_map/ppermute | solution.py:755
  82.1 11.3 %collective-permute-start.10 = (f32[4,72,128]{2,1,0:T(8,128)S(1)}, f32[4,72,128]{2,1,0:T(8,128)S(1)}, u32[]{:S(2)}, u32[]{:S(2)}) collective-permute-start(f32[4,72,128]{2,1,0:T(8,128)S(1)} %slice_bitcast_fusion.2), channel_id=1, source_target_pairs={{0,1},{1,0},{2,3},{3,2},{4,5},{5,4},{6,7},{7,6},{8,9},{9,8},{10,11... | collective-permute-start | bytes 442376 | tf_op jit(solution)/shard_map/ppermute | solution.py:564
  105.6 22.9 %collective-permute-start.12 = (f32[8,72,128]{2,1,0:T(8,128)S(1)}, f32[8,72,128]{2,1,0:T(8,128)S(1)}, u32[]{:S(2)}, u32[]{:S(2)}) collective-permute-start(f32[8,72,128]{2,1,0:T(8,128)S(1)} %bitcast.58), channel_id=1, source_target_pairs={{2,0},{15,1},{4,2},{1,3},{6,4},{3,5},{8,6},{5,7},{10,8},{7,9},{12,... | collective-permute-start | bytes 884744 | tf_op jit(solution)/shard_map/ppermute | solution.py:724
  106.0 22.6 %collective-permute-start.11 = (f32[8,72,128]{2,1,0:T(8,128)S(1)}, f32[8,72,128]{2,1,0:T(8,128)S(1)}, u32[]{:S(2)}, u32[]{:S(2)}) collective-permute-start(f32[8,72,128]{2,1,0:T(8,128)S(1)} %bitcast.59), channel_id=1, source_target_pairs={{0,2},{1,15},{2,4},{3,1},{4,6},{5,3},{6,8},{7,5},{8,10},{9,7},{10,... | collective-permute-start | bytes 884744 | tf_op jit(solution)/shard_map/ppermute | solution.py:720
  130.8 1.5 %collective-permute-start.13 = (f32[4,72,128]{2,1,0:T(8,128)S(1)}, f32[4,72,128]{2,1,0:T(8,128)S(1)}, u32[]{:S(2)}, u32[]{:S(2)}) collective-permute-start(f32[4,72,128]{2,1,0:T(8,128)S(1)} %slice_bitcast_fusion), channel_id=1, source_target_pairs={{0,1},{1,0},{2,3},{3,2},{4,5},{5,4},{6,7},{7,6},{8,9},{9,8},{10,11... | collective-permute-start | bytes 442376 | tf_op jit(solution)/shard_map/ppermute | solution.py:564
